TPU v7x, 256 devices: a whole 4x4x8 slice. The times are simulated.
256 devices in a mesh: leaf: 32 (over z, x), scene: 8 (over y, core).
Axes of the slice: x: 4, y: 4, z: 8, core: 2. Of those that a mesh axis runs over, the one named last changes fastest.
Arguments:
- features: bfloat16 [8, 256, 8, 8, 8, 128], P('scene', 'leaf'), may hold values from -6 to 6
- weight_first: bfloat16 [27, 128, 128], replicated, may hold values from -0.109375 to 0.109375
- weight_second: bfloat16 [27, 128, 128], replicated, may hold values from -0.109375 to 0.109375
- cotangent: bfloat16 [8, 256, 4, 4, 4, 128], P('scene', 'leaf'), may hold values from -6 to 6
- neighbours: int32 [8, 256, 26], P('scene', 'leaf'), may hold values from -1 to 255, as said below
- voxel_mask: int32 [8, 256, 512], P('scene', 'leaf'), may hold values from 0 to 1, as said below
Outputs:
- coarse: bfloat16 [8, 256, 4, 4, 4, 128], P('scene', 'leaf')
- input_grad: bfloat16 [8, 256, 8, 8, 8, 128], P('scene', 'leaf')
- grad_first: float32 [27, 128, 128], replicated
- grad_second: float32 [27, 128, 128], replicated
Inputs may be any that keep to these rules, and one draw needn't show every extreme that they name: `neighbours`: leaf blocks are held 8 to an index of leaf in order. A neighbour found at an offset whose third component is c is held by the index of leaf c away from the leaf's own (the same for c = 0). The relation is symmetric: if n is the neighbour of m at an offset, m is that of n at the opposite offset. An inactive leaf block names no neighbour and is named by none. `voxel_mask`: all voxels of an inactive leaf block are 0; every leaf block of the last index of leaf is active.
All inputs are finite; a program needn't handle non-finite values.
Results may differ from a plain program's by a relative error of at most 0.005.
Values may be sent and summed in bfloat16 or wider, within the bound.
No kernel may reach another device: no remote copies, remote signals or barrier semaphores. Data moves between devices by JAX's collectives and lax.ppermute only.
A program may use at most 128 MiB of HBM per device.

v0:
```python
import math

import jax
import jax.numpy as jnp
from jax import lax
from jax.sharding import PartitionSpec as P

offsets = [
    (a, b, c) for a in (-1, 0, 1) for b in (-1, 0, 1) for c in (-1, 0, 1) if (a, b, c) != (0, 0, 0)
]


def with_halo(cells, sides, width):
    for axis, dim in sides:
        count = lax.axis_size(axis)
        ends = count - 1
        head = lax.slice_in_dim(cells, 0, width, axis=dim)
        tail = lax.slice_in_dim(cells, cells.shape[dim] - width, cells.shape[dim], axis=dim)
        cells = jnp.concatenate(
            [
                lax.ppermute(tail, axis, [(i, (i + 1) % count) for i in range(ends)]),
                cells,
                lax.ppermute(head, axis, [((i + 1) % count, i) for i in range(ends)]),
            ],
            axis=dim,
        )
    return cells


def passed_along(block, axis, distance):
    devices = range(lax.axis_size(axis))
    route = [(i - distance, i) for i in devices if i - distance in devices]
    return lax.ppermute(block, axis, route)


def pad_range(shift, edge_len):
    if shift < 0:
        return slice(0, 1)
    if shift > 0:
        return slice(edge_len + 1, edge_len + 2)
    return slice(1, edge_len + 1)


def leaf_range(shift, edge_len):
    if shift < 0:
        return slice(edge_len - 1, edge_len)
    if shift > 0:
        return slice(0, 1)
    return slice(0, edge_len)


def make_selector(lookup, usable, count):
    ids = jnp.arange(count, dtype=jnp.int32)
    return jnp.logical_and(lookup[:, :, None] == ids[None, None, :], usable[:, :, None])


def assemble(interior, source, chooser):
    edge_len = interior.shape[1]
    pieces = {(0, 0, 0): interior}
    for direction, (a, b, c) in enumerate(offsets):
        slab_part = source[
            :, leaf_range(a, edge_len), leaf_range(b, edge_len), leaf_range(c, edge_len), :
        ]
        pick = chooser[:, direction, :].astype(slab_part.dtype)
        picked = jnp.einsum("ls,sxyzc->lxyzc", pick, slab_part, preferred_element_type=jnp.float32)
        pieces[a, b, c] = picked.astype(interior.dtype)
    planes_x = []
    for a in (-1, 0, 1):
        planes_y = []
        for b in (-1, 0, 1):
            planes_y.append(jnp.concatenate([pieces[a, b, c] for c in (-1, 0, 1)], axis=3))
        planes_x.append(jnp.concatenate(planes_y, axis=2))
    return jnp.concatenate(planes_x, axis=1)


def conv_forward(padded, weight, stride):
    kernel = weight.reshape(3, 3, 3, weight.shape[1], weight.shape[2])
    return lax.conv_general_dilated(
        padded,
        kernel,
        (stride, stride, stride),
        "VALID",
        dimension_numbers=("NDHWC", "DHWIO", "NDHWC"),
        preferred_element_type=jnp.float32,
    )


def conv_adjoint(upstream, weight, stride, edge_len):
    kernel = weight.reshape(3, 3, 3, weight.shape[1], weight.shape[2])[::-1, ::-1, ::-1]
    dilated = stride * (upstream.shape[1] - 1) + 1
    upper = edge_len + 2 - dilated
    return lax.conv_general_dilated(
        upstream,
        kernel,
        (1, 1, 1),
        [(2, upper)] * 3,
        lhs_dilation=(stride, stride, stride),
        dimension_numbers=("NDHWC", "DHWOI", "NDHWC"),
        preferred_element_type=jnp.float32,
    )


def weight_grad(padded, upstream, stride):
    summed = lax.conv_general_dilated(
        padded,
        upstream,
        (1, 1, 1),
        "VALID",
        rhs_dilation=(stride, stride, stride),
        dimension_numbers=("CDHWN", "IDHWO", "DHWNC"),
        preferred_element_type=jnp.float32,
    )
    summed = summed[:3, :3, :3]
    return summed.reshape(27, summed.shape[3], summed.shape[4])


def route_back(back_pad, chooser, row_total):
    edge_len = back_pad.shape[1] - 2
    channels = back_pad.shape[-1]
    target = jnp.zeros((row_total, edge_len, edge_len, edge_len, channels), jnp.float32)
    for direction, (a, b, c) in enumerate(offsets):
        slab_part = back_pad[
            :, pad_range(a, edge_len), pad_range(b, edge_len), pad_range(c, edge_len), :
        ]
        pick = chooser[:, direction, :].astype(jnp.float32)
        sent = jnp.einsum("ls,lxyzc->sxyzc", pick, slab_part, precision=lax.Precision.HIGHEST)
        target = target.at[
            :, leaf_range(a, edge_len), leaf_range(b, edge_len), leaf_range(c, edge_len), :
        ].add(sent)
    return target


def shards(features, weight_first, weight_second, cotangent, neighbours, voxel_mask):
    scene_feat = features[0]
    leaf_count = scene_feat.shape[0]
    edge_len = scene_feat.shape[1]
    device = lax.axis_index("leaf")
    mask_f = voxel_mask[0].reshape(leaf_count, edge_len, edge_len, edge_len, 1).astype(jnp.float32)
    masked = scene_feat * mask_f.astype(jnp.bfloat16)
    scene_nbr = neighbours[0]
    usable = scene_nbr >= 0
    lookup = scene_nbr - (device - 1) * leaf_count
    chooser = make_selector(lookup, usable, 3 * leaf_count)
    inner = slice(1, edge_len + 1)
    extended = with_halo(masked, (("leaf", 0),), leaf_count)
    padded_in = assemble(masked, extended, chooser)
    pre_act = conv_forward(padded_in, weight_first, 1)
    sigma = jax.nn.sigmoid(pre_act)
    hidden = (mask_f * pre_act * sigma).astype(jnp.bfloat16)
    below = passed_along(hidden, "leaf", 1)
    extended_hidden = jnp.concatenate([below, hidden, jnp.zeros_like(hidden)], axis=0)
    padded_hidden = assemble(hidden, extended_hidden, chooser)
    coarse_mask = mask_f[:, ::2, ::2, ::2]
    coarse = (coarse_mask * conv_forward(padded_hidden, weight_second, 2)).astype(jnp.bfloat16)
    coarse_grad = cotangent[0] * coarse_mask.astype(jnp.bfloat16)
    grad_second = weight_grad(padded_hidden, coarse_grad, 2)
    back_second = conv_adjoint(coarse_grad, weight_second, 2, edge_len)
    routed = route_back(back_second, chooser, 3 * leaf_count)
    grad_hidden = back_second[:, inner, inner, inner, :] + routed[leaf_count : 2 * leaf_count]
    grad_hidden = grad_hidden + passed_along(routed[:leaf_count], "leaf", -1)
    slope = sigma * (1.0 + pre_act * (1.0 - sigma))
    delta = (grad_hidden * mask_f * slope).astype(jnp.bfloat16)
    grad_first = weight_grad(padded_in, delta, 1)
    back_first = conv_adjoint(delta, weight_first, 1, edge_len)
    routed = route_back(back_first, chooser, 3 * leaf_count)
    input_grad = back_first[:, inner, inner, inner, :] + routed[leaf_count : 2 * leaf_count]
    outgoing = jnp.concatenate([routed[:leaf_count], routed[2 * leaf_count :]], axis=0)
    arrived = with_halo(outgoing, (("leaf", 0),), leaf_count)
    input_grad = input_grad + arrived[:leaf_count] + arrived[3 * leaf_count :]
    input_grad = (input_grad * mask_f).astype(jnp.bfloat16)
    grad_first, grad_second = lax.psum((grad_first, grad_second), ("leaf", "scene"))
    factor = 1.0 / math.sqrt(
        lax.axis_size("leaf") * lax.axis_size("scene") * leaf_count * edge_len**3
    )
    return (coarse[None], input_grad[None], grad_first * factor, grad_second * factor)


def solution(mesh):
    placed = (
        P("scene", "leaf", None, None, None, None),
        P(),
        P(),
        P("scene", "leaf", None, None, None, None),
        P("scene", "leaf", None),
        P("scene", "leaf", None),
    )
    return jax.shard_map(
        shards,
        mesh=mesh,
        in_specs=placed,
        out_specs=(
            P("scene", "leaf", None, None, None, None),
            P("scene", "leaf", None, None, None, None),
            P(),
            P(),
        ),
        check_vma=False,
    )
```

profile of v0, /device:TPU:1, one launch (start us, length us, event | category | flops | bytes accessed | tf_op | source)
XLA Modules:
  0.0 500.3 jit_solution(5117071874292918326)
XLA Ops:
  8.2 2.0 bitcast_multiply_fusion
  11.5 5.6 %collective-permute-start = (bf16[8,8,8,8,128]{4,0,3,2,1:T(8,128)(2,1)S(1)}, bf16[8,8,8,8,128]{4,0,3,2,1:T(8,128)(2,1)}, u32[]{:S(2)}, u32[]{:S(2)}) collective-permute-start(bf16[8,8,8,8,128]{4,0,3,2,1:T(8,128)(2,1)S(1)} %bitcast_multiply_fusion), channel_id=1, source_target_pairs={{0,8},{8,16},{16,24},{24,32},{32,40},{40,48},{48,56},{56,64},{64,7... | collective-permute-start | bytes 3145736 | tf_op jit(solution)/shard_map/ppermute | solution.py:21
  22.3 4.9 fusion.157
  27.4 3.7 scatter-add.174
  32.8 1.8 fusion.40
  42.2 1.8 fusion.45
  47.6 2.6 fusion.11
  50.2 2.6 fusion.13
  55.0 4.1 fusion.50
  64.9 3.6 fusion.55
  70.1 3.7 fusion.58
  81.4 1.8 slice.2793
  101.9 1.9 pad_maximum_fusion
  105.0 8.5 %maximum_maximum_fusion.1 = bf16[8,10,10,10,128]{4,0,3,2,1:T(8,128)(2,1)S(1)} fusion(bf16[8,1,1,1,128]{4,0,3,2,1:T(8,128)(2,1)S(1)} %fusion.145, bf16[8,1,1,8,128]{4,0,3,2,1:T(8,128)(2,1)S(1)} %fusion.97, bf16[8,1,1,1,128]{4,0,3,2,1:T(8,128)(2,1)S(1)} %fusion.144, bf16[8,1,8,1,128]{4,0,3,2,1:T(8,128)(2,1)S(1)} %fusion.96, ...), kind=kLoop, calls=%fused_computation.16 | loop fusion | flops 26624000 | bytes 4096000 | tf_op jit(solution)/shard_map/concatenate | solution.py:73
  113.5 15.5 %collective-permute-done.3 = f32[8,8,8,8,128]{4,0,3,2,1:T(8,128)S(1)} collective-permute-done((f32[8,8,8,8,128]{4,0,3,2,1:T(8,128)S(1)}, f32[8,8,8,8,128]{4,0,3,2,1:T(8,128)S(1)}, u32[]{:S(2)}, u32[]{:S(2)}) %collective-permute-start.3) | collective-permute-done | bytes 2097184 | tf_op jit(solution)/shard_map/ppermute | solution.py:33
  129.0 10.1 %fusion.7 = (bf16[8,8,8,8,128]{4,0,3,2,1:T(8,128)(2,1)S(1)}, bf16[8,8,8,8,128]{4,0,3,2,1:T(8,128)(2,1)S(1)}) fusion(f32[8,8,8,8,128]{4,0,3,2,1:T(8,128)S(1)} %collective-permute-done.3, f32[24,8,8,8,128]{4,0,3,2,1:T(8,128)} %fusion.123, f32[8,10,10,10,128]{4,0,3,2,1:T(8,128)S(1)} %copy-done.6, f32[8,8,8,8]{0,3,2,1:T(8,128)S(1)} %bitcast.941, ...), kind=kOutput, calls=%fused_computation.13 | convolution fusion | flops 3631742976 | bytes 11337728 | tf_op jit(solution)/shard_map/conv_general_dilated | solution.py:78
  139.1 12.5 %fusion.265 = f32[3,3,3,128,128]{4,3,2,1,0:T(8,128)} fusion(bf16[8,10,10,10,128]{4,0,3,2,1:T(8,128)(2,1)S(1)} %maximum_maximum_fusion.1, bf16[8,8,8,8,128]{4,0,3,2,1:T(8,128)(2,1)S(1)} %get-tuple-element.638), kind=kOutput, calls=%fused_computation.540 | convolution fusion | flops 3623878656 | bytes 4866048 | tf_op jit(solution)/shard_map/conv_general_dilated | solution.py:104
  151.6 15.7 %fusion.264 = f32[8,10,10,10,128]{4,0,3,2,1:T(8,128)S(1)} fusion(bf16[8,8,8,8,128]{4,0,3,2,1:T(8,128)(2,1)S(1)} %get-tuple-element.638, bf16[3,3,3,128,128]{4,3,2,1,0:T(8,128)(2,1)S(1)} %bitcast.938), kind=kOutput, calls=%fused_computation.539 | convolution fusion | flops 3623878656 | bytes 6029312 | tf_op jit(solution)/shard_map/conv_general_dilated | solution.py:92
  167.4 4.2 collective-permute-start.2
  177.2 2.1 fusion.74
  180.4 2.1 fusion.79
  182.7 2.2 fusion.82
  186.4 3.0 fusion.262
  190.3 5.3 %collective-permute-start.4 = (f32[8,8,8,8,128]{4,0,3,2,1:T(8,128)}, f32[8,8,8,8,128]{4,0,3,2,1:T(8,128)S(1)}, u32[]{:S(2)}, u32[]{:S(2)}) collective-permute-start(f32[8,8,8,8,128]{4,0,3,2,1:T(8,128)} %get-tuple-element.636), channel_id=1, source_target_pairs={{0,8},{8,16},{16,24},{24,32},{32,40},{40,48},{48,56},{56,64},{64,7... | collective-permute-start | bytes 6291464 | tf_op jit(solution)/shard_map/ppermute | solution.py:21
  201.7 8.7 %maximum_maximum_fusion.2 = bf16[8,10,10,10,128]{4,0,3,2,1:T(8,128)(2,1)S(1)} fusion(bf16[8,1,1,1,128]{4,0,3,2,1:T(8,128)(2,1)S(1)} %fusion.153, bf16[8,1,1,8,128]{4,0,3,2,1:T(8,128)(2,1)S(1)} %fusion.109, bf16[8,1,1,1,128]{4,0,3,2,1:T(8,128)(2,1)S(1)} %fusion.152, bf16[8,1,8,1,128]{4,0,3,2,1:T(8,128)(2,1)S(1)} %fusion.108, ...), kind=kLoop, calls=%fused_computation.17 | loop fusion | flops 26624000 | bytes 4096000 | tf_op jit(solution)/shard_map/concatenate | solution.py:73
  210.5 2.7 fusion.155
  213.3 2.8 fusion.37
  216.7 23.0 %collective-permute-done.4 = f32[8,8,8,8,128]{4,0,3,2,1:T(8,128)S(1)} collective-permute-done((f32[8,8,8,8,128]{4,0,3,2,1:T(8,128)}, f32[8,8,8,8,128]{4,0,3,2,1:T(8,128)S(1)}, u32[]{:S(2)}, u32[]{:S(2)}) %collective-permute-start.4) | collective-permute-done | bytes 2097184 | tf_op jit(solution)/shard_map/ppermute | solution.py:21
  239.8 5.7 %collective-permute-done.5 = f32[8,8,8,8,128]{4,0,3,2,1:T(8,128)} collective-permute-done((f32[8,8,8,8,128]{4,0,3,2,1:T(8,128)}, f32[8,8,8,8,128]{4,0,3,2,1:T(8,128)}, u32[]{:S(2)}, u32[]{:S(2)}) %collective-permute-start.5) | collective-permute-done | bytes 2097184 | tf_op jit(solution)/shard_map/ppermute | solution.py:23
  245.4 3.4 fusion.154
  250.1 238.5 %all-reduce.5.cloned.1.call-done = (f32[27,128,128]{2,1,0:T(8,128)}, f32[27,128,128]{2,1,0:T(8,128)}) async-done(((f32[27,128,128]{2,1,0:T(8,128)}, f32[27,128,128]{2,1,0:T(8,128)}), (f32[27,128,128]{2,1,0:T(8,128)}, f32[27,128,128]{2,1,0:T(8,128)})) %all-reduce.5.cloned.1.call-update) | async-done | bytes 3538960 | tf_op jit(solution)/shard_map/psum | solution.py:171
  488.6 3.0 broadcast_multiply_fusion.1
  (171 shorter events, 76.0 us)
Async XLA Ops:
  7.2 121.9 %copy-start = (bf16[27,128,128]{2,1,0:T(8,128)(2,1)S(1)}, bf16[27,128,128]{2,1,0:T(8,128)(2,1)}, u32[]{:S(2)}) copy-start(bf16[27,128,128]{2,1,0:T(8,128)(2,1)} %param.111) | copy-start | bytes 2654212
  7.2 481.4 %all-reduce.5.cloned.1.call-start = ((), (), s32[]{:S(2)}) async-start(), calls=%async_computation | async-start | bytes 7077888 | tf_op jit(solution)/shard_map/psum | solution.py:171
  8.1 120.9 %copy-start.7 = (f32[1,8,512]{1,2,0:T(8,128)}, f32[1,8,512]{1,2,0:T(8,128)S(1)}, u32[]{:S(2)}) copy-start(f32[1,8,512]{1,2,0:T(8,128)S(1)} %copy.27) | copy-start | bytes 49156
  10.2 75.2 %collective-permute-start.1 = (bf16[8,8,8,8,128]{4,0,3,2,1:T(8,128)(2,1)S(1)}, bf16[8,8,8,8,128]{4,0,3,2,1:T(8,128)(2,1)S(1)}, u32[]{:S(2)}, u32[]{:S(2)}) collective-permute-start(bf16[8,8,8,8,128]{4,0,3,2,1:T(8,128)(2,1)S(1)} %bitcast_multiply_fusion), channel_id=1, source_target_pairs={{8,0},{16,8},{24,16},{32,24},{40,32},{48,40},{56,48},{64,56},{72,6... | collective-permute-start | bytes 3145736 | tf_op jit(solution)/shard_map/ppermute | solution.py:23
  11.5 73.9 %collective-permute-start = (bf16[8,8,8,8,128]{4,0,3,2,1:T(8,128)(2,1)S(1)}, bf16[8,8,8,8,128]{4,0,3,2,1:T(8,128)(2,1)}, u32[]{:S(2)}, u32[]{:S(2)}) collective-permute-start(bf16[8,8,8,8,128]{4,0,3,2,1:T(8,128)(2,1)S(1)} %bitcast_multiply_fusion), channel_id=1, source_target_pairs={{0,8},{8,16},{16,24},{24,32},{32,40},{40,48},{48,56},{56,64},{64,7... | collective-permute-start | bytes 3145736 | tf_op jit(solution)/shard_map/ppermute | solution.py:21
  19.6 0.6 copy-start.11
  21.7 0.7 copy-start.3
  27.2 23.0 %copy-start.5 = (f32[8,10,10,10,128]{4,0,3,2,1:T(8,128)}, f32[8,10,10,10,128]{4,0,3,2,1:T(8,128)S(1)}, u32[]{:S(2)}) copy-start(f32[8,10,10,10,128]{4,0,3,2,1:T(8,128)S(1)} %fusion.157) | copy-start | bytes 12288004
  37.2 17.0 %copy-start.13 = (s32[5]{0:T(128)S(1)}, s32[5]{0:T(128)}, u32[]{:S(2)}) copy-start(s32[5]{0:T(128)} %constant.1294.clone.1) | copy-start | bytes 64
  37.2 17.0 %copy-start.14 = (s32[5]{0:T(128)S(1)}, s32[5]{0:T(128)}, u32[]{:S(2)}) copy-start(s32[5]{0:T(128)} %constant.1293.clone.1) | copy-start | bytes 64
  37.2 17.0 %copy-start.15 = (s32[5]{0:T(128)S(1)}, s32[5]{0:T(128)}, u32[]{:S(2)}) copy-start(s32[5]{0:T(128)} %constant.1291.clone.1) | copy-start | bytes 64
  54.2 14.4 %copy-start.6 = (f32[8,10,10,10,128]{4,0,3,2,1:T(8,128)S(1)}, f32[8,10,10,10,128]{4,0,3,2,1:T(8,128)}, u32[]{:S(2)}) copy-start(f32[8,10,10,10,128]{4,0,3,2,1:T(8,128)} %copy-done.5) | copy-start | bytes 12288004
  83.2 45.8 %collective-permute-start.3 = (f32[8,8,8,8,128]{4,0,3,2,1:T(8,128)S(1)}, f32[8,8,8,8,128]{4,0,3,2,1:T(8,128)S(1)}, u32[]{:S(2)}, u32[]{:S(2)}) collective-permute-start(f32[8,8,8,8,128]{4,0,3,2,1:T(8,128)S(1)} %slice.2793), channel_id=1, source_target_pairs={{8,0},{16,8},{24,16},{32,24},{40,32},{48,40},{56,48},{64,56},{72,6... | collective-permute-start | bytes 6291464 | tf_op jit(solution)/shard_map/ppermute | solution.py:33
  167.4 18.8 %copy-start.2 = (f32[8,10,10,10,128]{4,0,3,2,1:T(8,128)}, f32[8,10,10,10,128]{4,0,3,2,1:T(8,128)S(1)}, u32[]{:S(2)}) copy-start(f32[8,10,10,10,128]{4,0,3,2,1:T(8,128)S(1)} %fusion.264) | copy-start | bytes 12288004
  167.4 29.5 %collective-permute-start.2 = (bf16[8,8,8,8,128]{4,0,3,2,1:T(8,128)(2,1)S(1)}, bf16[8,8,8,8,128]{4,0,3,2,1:T(8,128)(2,1)S(1)}, u32[]{:S(2)}, u32[]{:S(2)}) collective-permute-start(bf16[8,8,8,8,128]{4,0,3,2,1:T(8,128)(2,1)S(1)} %get-tuple-element.639), channel_id=1, source_target_pairs={{0,8},{8,16},{16,24},{24,32},{32,40},{40,48},{48,56},{56,64},{64,7... | collective-permute-start | bytes 3145736 | tf_op jit(solution)/shard_map/ppermute | solution.py:33
  186.4 3.9 copy-start.1
  186.4 10.5 %copy-start.16 = (bf16[24]{0:T(256)(128)(2,1)S(1)}, bf16[24]{0:T(256)(128)(2,1)}, u32[]{:S(2)}) copy-start(bf16[24]{0:T(256)(128)(2,1)} %pad.223.clone) | copy-start | bytes 148
  190.3 49.5 %collective-permute-start.4 = (f32[8,8,8,8,128]{4,0,3,2,1:T(8,128)}, f32[8,8,8,8,128]{4,0,3,2,1:T(8,128)S(1)}, u32[]{:S(2)}, u32[]{:S(2)}) collective-permute-start(f32[8,8,8,8,128]{4,0,3,2,1:T(8,128)} %get-tuple-element.636), channel_id=1, source_target_pairs={{0,8},{8,16},{16,24},{24,32},{32,40},{40,48},{48,56},{56,64},{64,7... | collective-permute-start | bytes 6291464 | tf_op jit(solution)/shard_map/ppermute | solution.py:21
  195.6 49.8 %collective-permute-start.5 = (f32[8,8,8,8,128]{4,0,3,2,1:T(8,128)}, f32[8,8,8,8,128]{4,0,3,2,1:T(8,128)}, u32[]{:S(2)}, u32[]{:S(2)}) collective-permute-start(f32[8,8,8,8,128]{4,0,3,2,1:T(8,128)} %get-tuple-element.637), channel_id=1, source_target_pairs={{8,0},{16,8},{24,16},{32,24},{40,32},{48,40},{56,48},{64,56},{72,6... | collective-permute-start | bytes 6291464 | tf_op jit(solution)/shard_map/ppermute | solution.py:23
  198.0 12.5 %copy-start.4 = (bf16[8,4,4,4,128]{4,3,2,1,0:T(4,128)(2,1)S(1)}, bf16[8,4,4,4,128]{4,3,2,1,0:T(4,128)(2,1)}, u32[]{:S(2)}) copy-start(bf16[8,4,4,4,128]{4,3,2,1,0:T(4,128)(2,1)} %copy-done.3) | copy-start | bytes 393220
  210.5 2.8 copy-start.9
  210.5 2.8 copy-start.12
  213.2 32.2 %copy-start.8 = (f32[1,8,512]{1,2,0:T(8,128)S(1)}, f32[1,8,512]{1,2,0:T(8,128)}, u32[]{:S(2)}) copy-start(f32[1,8,512]{1,2,0:T(8,128)} %copy-done.7) | copy-start | bytes 49156
  488.6 3.0 copy-start.10
Sparse Core Ops, SparseCore 0:
  213.4 275.1 all-reduce.4
where the time goes:
time: 510 us; the launch traced here: 500 us
  waiting for transfers between devices  283 us (55%)
  matrix products  127 us (25%)
  other arithmetic  34.2 us (7%)
  local copies, waits for them, and re-layouts  22.3 us (4%)
  starting transfers between devices  19.2 us (4%)
  between operations  15.1 us (3%)
    psum x1, waiting for transfers between devices, shards(): lax.psum((grad_first, grad_second), ('leaf', 'scene'))  239 us
    dot_general x52, matrix products, route_back(): jnp.einsum('ls,lxyzc->sxyzc', pick, slab_part, precision=lax.Precision.HI...  56.7 us
    ppermute x2, waiting for transfers between devices, with_halo(): lax.ppermute(tail, axis, [(i, (i + 1) % count) for i in range(ends)])  23 us
    dot_general x52, matrix products, assemble(): jnp.einsum('ls,sxyzc->lxyzc', pick, slab_part, preferred_element_type=jnp...  21.3 us
    conv_general_dilated x2, matrix products, conv_adjoint(): lax.conv_general_dilated(upstream, kernel, (1, 1, 1), [(2, upper)] * 3, l...  20.7 us
    concatenate x2, other arithmetic, assemble(): return jnp.concatenate(planes_x, axis=1)  17.2 us
    ppermute x2, waiting for transfers between devices, passed_along(): return lax.ppermute(block, axis, route)  15.5 us
    conv_general_dilated x2, matrix products, conv_forward(): lax.conv_general_dilated(padded, kernel, (stride, stride, stride), 'VALID...  12.9 us
  transfers between devices with their start and end apart: 7, of which 4 were waited for; matrix products, arithmetic and copies ran while one was open for 27% of the time, Pallas kernels for 0%

commit v1 on v0

v1 whole, which is shorter than its diff:
```python
import math

import jax
import jax.numpy as jnp
from jax import lax
from jax.experimental import pallas as pl
from jax.experimental.pallas import tpu as pltpu
from jax.sharding import PartitionSpec as P

bf16 = jnp.bfloat16
f32 = jnp.float32
C = 128
L = 8
E = 8
ROWS = 64
SPAN = 9 * C
PARAMS = pltpu.CompilerParams(vmem_limit_bytes=58 * 1024 * 1024)


def place(table, leaf, a, b, c):
    return table[leaf, 9 * (a + 1) + 3 * (b + 1) + (c + 1)]


def edge_row(face, block, i, j):
    return jnp.broadcast_to(face[block, i, pl.ds(j, 1), :], (E, C))


def columns(table, lines, low, high, leaf, x, top):
    first, last = x == 0, x == top + 1
    a = jnp.where(first, -1, jnp.where(last, 1, 0))
    i = jnp.where(first, top - 1, jnp.where(last, 0, x - 1))
    ids = lax.broadcasted_iota(jnp.int32, (E, C), 0)
    out = ([], [], [])
    for y in range(E + 2):
        b = -1 if y == 0 else 1 if y == E + 1 else 0
        j = E - 1 if y == 0 else 0 if y == E + 1 else y - 1
        line = lines[place(table, leaf, a, b, 0), i, j]
        below = pltpu.roll(line, 1, 0)
        above = pltpu.roll(line, E - 1, 0)
        if low is not None:
            below = jnp.where(ids == 0, edge_row(low, place(table, leaf, a, b, -1), i, j), below)
        else:
            below = jnp.where(ids == 0, 0.0, below)
        above = jnp.where(ids == E - 1, edge_row(high, place(table, leaf, a, b, 1), i, j), above)
        for r, part in enumerate((below, line, above)):
            out[r].append(part)
    return [jnp.concatenate(part, axis=0) for part in out]


def fill_columns(table, lines, low, high, leaf, x, top, store):
    cols = columns(table, lines, low, high, leaf, x, top)
    for q in range(3):
        for r in range(3):
            store((3 * q + r) * C, cols[r][E * q : E * q + ROWS].astype(bf16))


def banded(weight, first, second, shift):
    zero = jnp.zeros((SPAN, C), bf16)
    w = [weight[9 * s : 9 * s + 9].reshape(SPAN, C) for s in range(3)]
    first[:SPAN, :C] = w[0]
    first[:SPAN, C:] = zero
    first[SPAN:, :C] = w[1]
    first[SPAN:, C:] = w[0]
    second[:SPAN, :C] = w[2]
    second[:SPAN, C:] = w[1]
    second[SPAN:, :C] = zero
    second[SPAN:, C:] = w[2]


def pairs_dot(cols, leaf, first, second):
    lo = cols[leaf, 0:4].reshape(4 * ROWS, 2 * SPAN)
    hi = cols[leaf, 1:5].reshape(4 * ROWS, 2 * SPAN)
    return jnp.dot(lo, first[...], preferred_element_type=f32) + jnp.dot(hi, second[...], preferred_element_type=f32)


def first_kernel(
    table, feat, mask, low_in, high_in, cot, cot_high_in, w1, w2t,
    hidden, delta, grad,
    lines, low, high, clines, chigh, cols, ccols, wa, wb, turned, total,
):
    lines[L] = jnp.zeros((E, E, E, C), f32)
    low[L] = jnp.zeros((E, E, C), f32)
    high[L] = jnp.zeros((E, E, C), f32)
    clines[L] = jnp.zeros((4, E, E, C), f32)
    chigh[L] = jnp.zeros((4, E, C), f32)

    @pl.loop(0, L)
    def _(leaf):
        lines[leaf] = feat[leaf].astype(f32) * mask[leaf].astype(f32)
        low[leaf] = low_in[leaf].astype(f32)
        high[leaf] = high_in[leaf].astype(f32)
        clines[leaf] = cot[leaf].astype(f32)
        chigh[leaf] = cot_high_in[leaf].astype(f32)

    banded(w1, wa, wb, 0)

    @pl.loop(0, L)
    def _(leaf):
        @pl.loop(0, 5)
        def _(pair):
            for half in range(2):
                def store(at, value, half=half):
                    cols[leaf, pair, :, pl.ds(half * SPAN + at, C)] = value
                fill_columns(table, lines, low, high, leaf, 2 * pair + half, E, store)

            def store_c(at, value):
                ccols[pair, :, pl.ds(at, C)] = value
            fill_columns(table, clines, None, chigh, leaf, pair + 1, 4, store_c)

        pre = pairs_dot(cols, leaf, wa, wb)
        g = jnp.dot(ccols[0:4].reshape(4 * ROWS, SPAN), w2t[:, 0 : 2 * C], preferred_element_type=f32)
        g1 = jnp.dot(ccols[1:5].reshape(4 * ROWS, SPAN), w2t[:, 2 * C :], preferred_element_type=f32)
        sig = 1.0 / (1.0 + jnp.exp(-pre))
        slope = sig * (1.0 + pre * (1.0 - sig))
        for half in range(2):
            at = slice(half * C, half * C + C)
            m = mask[leaf].reshape(4, 2, ROWS, C)[:, half].reshape(4 * ROWS, C).astype(f32)
            h = (m * pre[:, at] * sig[:, at]).astype(bf16)
            gg = g[:, at] if half == 0 else g[:, at] + g1
            d = (gg * m * slope[:, at]).astype(bf16)
            hidden[leaf, :, half] = h.reshape(4, ROWS, C)
            delta[leaf, :, half] = d.reshape(4, ROWS, C)
            turned[half * C : half * C + C, pl.ds(pl.multiple_of(leaf * 256, 256), 256)] = d.T

    total[...] = jnp.zeros_like(total)
    for tile in range(9):
        at = slice(256 * tile, 256 * tile + 256)
        for step in range(2):
            rhs = cols[:, step : step + 4, :, at].reshape(L * 4 * ROWS, 256)
            for half in range(2):
                res = None
                for side in range(2):
                    p = 2 * step + side - half
                    lanes = [lane for lane in range(256 * tile, 256 * tile + 256, C) if lane // SPAN == side]
                    if not 0 <= p <= 2 or not lanes:
                        continue
                    if res is None:
                        res = jnp.dot(turned[half * C : half * C + C, :], rhs, preferred_element_type=f32)
                    for lane in lanes:
                        o = lane - SPAN * side
                        total[p, :, o : o + C] += res[:, lane - 256 * tile : lane - 256 * tile + C]
    for p in range(3):
        for t in range(9):
            grad[9 * p + t] = total[p, :, t * C : t * C + C].T.astype(grad.dtype)


def smem():
    return pl.BlockSpec(memory_space=pltpu.SMEM)


def vmem():
    return pl.BlockSpec(memory_space=pltpu.VMEM)


def first_call(table, feat, mask, low, high, cot, cot_high, w1, w2t, gdt=bf16):
    return pl.pallas_call(
        first_kernel,
        out_shape=(
            jax.ShapeDtypeStruct((L, 4, 2, ROWS, C), bf16),
            jax.ShapeDtypeStruct((L, 4, 2, ROWS, C), bf16),
            jax.ShapeDtypeStruct((27, C, C), gdt),
        ),
        in_specs=[smem()] + [vmem()] * 8,
        out_specs=(vmem(), vmem(), vmem()),
        scratch_shapes=[
            pltpu.VMEM((L + 1, E, E, E, C), f32),
            pltpu.VMEM((L + 1, E, E, C), f32),
            pltpu.VMEM((L + 1, E, E, C), f32),
            pltpu.VMEM((L + 1, 4, E, E, C), f32),
            pltpu.VMEM((L + 1, 4, E, C), f32),
            pltpu.VMEM((L, 5, ROWS, 2 * SPAN), bf16),
            pltpu.VMEM((5, ROWS, SPAN), bf16),
            pltpu.VMEM((2 * SPAN, 2 * C), bf16),
            pltpu.VMEM((2 * SPAN, 2 * C), bf16),
            pltpu.VMEM((2 * C, L * 256), bf16),
            pltpu.VMEM((3, C, SPAN), f32),
        ],
        compiler_params=PARAMS,
        cost_estimate=pl.CostEstimate(flops=8_000_000_000, bytes_accessed=8_000_000, transcendentals=0),
        name="first_conv",
    )(table, feat, mask, low, high, cot, cot_high, w1, w2t)


def adjoint_kernel(table, delta, mask, low_in, high_in, w, out, lines, low, high, cols, wa, wb):
    lines[L] = jnp.zeros((E, E, E, C), f32)
    low[L] = jnp.zeros((E, E, C), f32)
    high[L] = jnp.zeros((E, E, C), f32)

    @pl.loop(0, L)
    def _(leaf):
        lines[leaf] = delta[leaf].astype(f32)
        low[leaf] = low_in[leaf].astype(f32)
        high[leaf] = high_in[leaf].astype(f32)

    banded(w, wa, wb, 0)

    @pl.loop(0, L)
    def _(leaf):
        @pl.loop(0, 5)
        def _(pair):
            for half in range(2):
                def store(at, value, half=half):
                    cols[leaf % 2, pair, :, pl.ds(half * SPAN + at, C)] = value
                fill_columns(table, lines, low, high, leaf, 2 * pair + half, E, store)
        res = pairs_dot(cols, leaf % 2, wa, wb)
        for half in range(2):
            at = slice(half * C, half * C + C)
            m = mask[leaf].reshape(4, 2, ROWS, C)[:, half].reshape(4 * ROWS, C).astype(f32)
            out[leaf, :, half] = (res[:, at] * m).astype(bf16).reshape(4, ROWS, C)


def adjoint_call(table, delta, mask, low, high, w):
    return pl.pallas_call(
        adjoint_kernel,
        out_shape=jax.ShapeDtypeStruct((L, 4, 2, ROWS, C), bf16),
        in_specs=[smem()] + [vmem()] * 5,
        out_specs=vmem(),
        scratch_shapes=[
            pltpu.VMEM((L + 1, E, E, E, C), f32),
            pltpu.VMEM((L + 1, E, E, C), f32),
            pltpu.VMEM((L + 1, E, E, C), f32),
            pltpu.VMEM((2, 5, ROWS, 2 * SPAN), bf16),
            pltpu.VMEM((2 * SPAN, 2 * C), bf16),
            pltpu.VMEM((2 * SPAN, 2 * C), bf16),
        ],
        compiler_params=PARAMS,
        cost_estimate=pl.CostEstimate(flops=4_000_000_000, bytes_accessed=5_000_000, transcendentals=0),
        name="first_adjoint",
    )(table, delta, mask, low, high, w)


def second_kernel(table, hidden, low_in, cot, cmask, w2, coarse, grad, lines, low, cols, turned, total):
    lines[L] = jnp.zeros((E, E, E, C), f32)
    low[L] = jnp.zeros((E, E, C), f32)

    @pl.loop(0, L)
    def _(leaf):
        lines[leaf] = hidden[leaf].astype(f32)
        low[leaf] = low_in[leaf].astype(f32)

    ids = lax.broadcasted_iota(jnp.int32, (E, C), 0)
    w = w2[...].reshape(27 * C, C)

    @pl.loop(0, L)
    def _(leaf):
        @pl.loop(0, 5)
        def _(pair):
            for half in range(2):
                x = 2 * pair + half
                first = x == 0
                a = jnp.where(first, -1, 0)
                i = jnp.where(first, E - 1, jnp.minimum(x - 1, E - 1))
                out = ([], [], [])
                for y in range(E + 1):
                    b = -1 if y == 0 else 0
                    j = E - 1 if y == 0 else y - 1
                    line = lines[place(table, leaf, a, b, 0), i, j]
                    below = jnp.where(ids == 0, edge_row(low, place(table, leaf, a, b, -1), i, j), pltpu.roll(line, 1, 0))
                    above = pltpu.roll(line, E - 1, 0)
                    for r, part in enumerate((below, line, above)):
                        out[r].append(part)
                for q in range(3):
                    for r in range(3):
                        value = jnp.concatenate([out[r][q + 2 * m] for m in range(4)], axis=0).astype(bf16)
                        cols[leaf, pair, :, pl.ds(half * SPAN + (3 * q + r) * C, C)] = value
        lo = cols[leaf, 0:4].reshape(128, 2 * SPAN)
        hi = cols[leaf, 1:5, :, 0:SPAN].reshape(128, SPAN)
        res = jnp.dot(lo, w[: 2 * SPAN], preferred_element_type=f32) + jnp.dot(hi, w[2 * SPAN :], preferred_element_type=f32)
        coarse[leaf] = (res.reshape(4, 4, E, C) * cmask[leaf].astype(f32)).astype(bf16)
        d = cot[leaf].reshape(128, C)
        turned[:, pl.ds(pl.multiple_of(leaf * 128, 128), 128)] = d.T

    for tile in range(9):
        at = slice(256 * tile, 256 * tile + 256)
        rhs = cols[:, 0:4, :, at].reshape(L * 128, 256)
        total[:, at] = jnp.dot(turned[...], rhs, preferred_element_type=f32)
    for tile in range(5):
        hi = min(256 * tile + 256, SPAN)
        rhs = cols[:, 1:5, :, 256 * tile : hi].reshape(L * 128, hi - 256 * tile)
        total[:, 2 * SPAN + 256 * tile : 2 * SPAN + hi] = jnp.dot(turned[...], rhs, preferred_element_type=f32)
    for t in range(27):
        grad[t] = total[:, t * C : t * C + C].T.astype(grad.dtype)


def second_call(table, hidden, low, cot, cmask, w2, gdt=bf16):
    return pl.pallas_call(
        second_kernel,
        out_shape=(
            jax.ShapeDtypeStruct((L, 4, 4, E, C), bf16),
            jax.ShapeDtypeStruct((27, C, C), gdt),
        ),
        in_specs=[smem()] + [vmem()] * 5,
        out_specs=(vmem(), vmem()),
        scratch_shapes=[
            pltpu.VMEM((L + 1, E, E, E, C), f32),
            pltpu.VMEM((L + 1, E, E, C), f32),
            pltpu.VMEM((L, 5, 32, 2 * SPAN), bf16),
            pltpu.VMEM((C, L * 128), bf16),
            pltpu.VMEM((C, 3 * SPAN), f32),
        ],
        compiler_params=PARAMS,
        cost_estimate=pl.CostEstimate(flops=2_000_000_000, bytes_accessed=5_000_000, transcendentals=0),
        name="second_conv",
    )(table, hidden, low, cot, cmask, w2)


def passed(block, distance):
    count = lax.axis_size("leaf")
    return lax.ppermute(block, "leaf", [(i - distance, i) for i in range(count) if 0 <= i - distance < count])


def local_table(neighbours):
    found = jnp.where(neighbours >= 0, neighbours % L, L)
    own = jnp.arange(L, dtype=jnp.int32)[:, None]
    return jnp.concatenate([found[:, :13], own, found[:, 13:]], axis=1)


def spread(x, dims):
    cfg = [(0, 1, 1) if d in dims else (0, 0, 0) for d in range(x.ndim)]
    return lax.pad(x, jnp.zeros((), x.dtype), cfg)


def pieces_summed(pieces):
    return jnp.sum(pieces.astype(f32), axis=0)


def summed_everywhere(first, second):
    scene_count, leaf_count = lax.axis_size("scene"), lax.axis_size("leaf")
    core = lax.axis_index("scene") % 2
    swap = [(i, i ^ 1) for i in range(scene_count)]
    ring = [[c + 2 * y for y in range(scene_count // 2)] for c in range(2)]
    quarters = scene_count // 2
    rows = C // 2 // quarters
    taps = 2 * 27
    per = -(-taps // leaf_count)
    both = jnp.concatenate([first, second], axis=0).reshape(taps, 2, C // 2, C)
    kept = lax.dynamic_index_in_dim(both, core, axis=1, keepdims=False)
    sent = lax.dynamic_index_in_dim(both, 1 - core, axis=1, keepdims=False)
    with jax.named_scope("sum_core"):
        half = kept.astype(f32) + lax.ppermute(sent.astype(bf16), "scene", swap).astype(f32)
    with jax.named_scope("sum_y"):
        parts = half.reshape(taps, quarters, rows, C).swapaxes(0, 1).astype(bf16)
        quarter = pieces_summed(lax.all_to_all(parts, "scene", 0, 0, axis_index_groups=ring, tiled=True).reshape(quarters, taps, rows, C))
    with jax.named_scope("sum_leaf"):
        parts = jnp.pad(quarter.astype(bf16), ((0, per * leaf_count - taps), (0, 0), (0, 0))).reshape(leaf_count, per * rows, C)
        own = pieces_summed(lax.all_to_all(parts, "leaf", 0, 0, tiled=True))
    factor = 1.0 / math.sqrt(leaf_count * scene_count * L * E**3)
    own = (own * factor).astype(bf16)
    with jax.named_scope("gather_leaf"):
        parts = jnp.broadcast_to(own[None], (leaf_count, per * rows, C))
        quarter = lax.all_to_all(parts, "leaf", 0, 0, tiled=True).reshape(per * leaf_count, rows, C)[:taps]
    with jax.named_scope("gather_y"):
        parts = jnp.broadcast_to(quarter[None], (quarters, taps, rows, C))
        half = lax.all_to_all(parts, "scene", 0, 0, axis_index_groups=ring, tiled=True)
    with jax.named_scope("gather_core"):
        other = lax.ppermute(half, "scene", swap)
    low = jnp.where(core == 0, half, other)
    high = jnp.where(core == 0, other, half)
    whole = jnp.stack([low, high], axis=0).reshape(2, quarters, taps, rows, C)
    whole = whole.transpose(2, 0, 1, 3, 4).reshape(taps, C, C).astype(f32)
    return whole[:27], whole[27:]


def shards(features, weight_first, weight_second, cotangent, neighbours, voxel_mask):
    feat = features[0]
    cot = cotangent[0]
    voxels = voxel_mask[0].reshape(L, E, E, E, 1).astype(bf16)
    mask = jnp.broadcast_to(voxels, (L, E, E, E, C))
    table = local_table(neighbours[0])
    coarse_mask = voxels[:, ::2, ::2, ::2]
    coarse_grad = cot * coarse_mask
    up = feat[:, :, :, E - 1] * voxels[:, :, :, E - 1]
    down = feat[:, :, :, 0] * voxels[:, :, :, 0]
    with jax.named_scope("faces_in"):
        low = passed(up, 1)
        down = jnp.concatenate([down.reshape(L, ROWS, C), coarse_grad[:, :, :, 0].reshape(L, 16, C)], axis=1)
        high = passed(down, -1)
    cot_high = spread(high[:, ROWS:].reshape(L, 4, 4, C), (2,))
    high = high[:, :ROWS].reshape(L, E, E, C)
    turned_first = jnp.swapaxes(weight_first[::-1], 1, 2)
    turned_second = jnp.swapaxes(weight_second[::-1], 1, 2).reshape(3, SPAN, C)
    turned_second = jnp.concatenate([turned_second[1], turned_second[0], turned_second[2]], axis=1)
    hidden, delta, grad_first = first_call(
        table, feat, mask, low, high, spread(coarse_grad, (2, 3)), cot_high, weight_first, turned_second
    )
    hidden = hidden.reshape(L, E, E, E, C)
    delta = delta.reshape(L, E, E, E, C)
    with jax.named_scope("faces_mid"):
        tops = jnp.stack([hidden[:, :, :, E - 1], delta[:, :, :, E - 1]], axis=0)
        tops = passed(tops, 1)
        bottom = passed(delta[:, :, :, 0], -1)
    coarse, grad_second = second_call(
        table, hidden, tops[0], spread(coarse_grad, (3,)),
        spread(jnp.broadcast_to(coarse_mask, (L, 4, 4, 4, C)), (3,)), weight_second
    )
    coarse = coarse[:, :, :, ::2]
    grad_first, grad_second = summed_everywhere(grad_first, grad_second)
    input_grad = adjoint_call(table, delta, mask, tops[1], bottom, turned_first).reshape(L, E, E, E, C)
    return (coarse[None], input_grad[None], grad_first, grad_second)


def solution(mesh):
    placed = (
        P("scene", "leaf", None, None, None, None),
        P(),
        P(),
        P("scene", "leaf", None, None, None, None),
        P("scene", "leaf", None),
        P("scene", "leaf", None),
    )
    return jax.shard_map(
        shards,
        mesh=mesh,
        in_specs=placed,
        out_specs=(
            P("scene", "leaf", None, None, None, None),
            P("scene", "leaf", None, None, None, None),
            P(),
            P(),
        ),
        check_vma=False,
    )
```

time: 510 us -> 295 us (0.58); the launches traced: 500 us -> 294 us
  waiting for transfers between devices: 283 us -> 2.28 us
  local copies, waits for them, and re-layouts: 22.3 us -> 157 us
  matrix products: 127 us -> 0 us
  blocking collectives: 0 us -> 65.4 us
  Pallas kernels: 0 us -> 44 us
  other arithmetic: 34.2 us -> 6.43 us
  between operations: 15.1 us -> 0.96 us
    psum x1 -> x0, waiting for transfers between devices: 239 us -> none  [shards(): lax.psum((grad_first, grad_second), ('leaf', 'scene'))]
    pad x0 -> x5, local copies, waits for them, and re-layouts: none -> 127 us  [the longest x4 127 us: spread(): return lax.pad(x, jnp.zeros((), x.dtype), cfg)]
    dot_general x104 -> x0, matrix products: 78 us -> none  [the longest x52 56.7 us: route_back(): jnp.einsum('ls,lxyzc->sxyzc', pick, slab_part, precision=lax.Precision.HI...]
    all_to_all x0 -> x4, blocking collectives: none -> 65.4 us  [the longest x2 28 us: summed_everywhere(): lax.all_to_all(parts, 'scene', 0, 0, axis_index_groups=ring, tiled=True)]
    conv_general_dilated x5 -> x0, matrix products: 46 us -> none  [the longest x2 20.7 us: conv_adjoint(): lax.conv_general_dilated(upstream, kernel, (1, 1, 1), [(2, upper)] * 3, l...]
    pallas_call x0 -> x3, Pallas kernels: none -> 44 us  [the longest x1 22.3 us: first_call(): pl.pallas_call(first_kernel, out_shape=(jax.ShapeDtypeStruct((L, 4, 2, RO...]
    ppermute x6, waiting for transfers between devices: 44.2 us -> 2.28 us  [the longest x1 2.26 us: summed_everywhere(): lax.ppermute(sent.astype(bf16), 'scene', swap).astype(f32)]
    concatenate x4, other arithmetic: 20.2 us -> 3.08 us  [the longest x1 1.32 us: summed_everywhere(): both = jnp.concatenate([first, second], axis=0).reshape(taps, 2, C // 2, C)]
  transfers between devices with their start and end apart: 7 -> 6, of which waited for: 4 -> 1; matrix products, arithmetic and copies ran while one was open for 27% -> 50% of each run, Pallas kernels for 0% -> 4%
where the time goes in v1:
time: 295 us; the launch traced here: 294 us
  local copies, waits for them, and re-layouts  157 us (53%)
  blocking collectives  65.4 us (22%)
  Pallas kernels  44 us (15%)
  starting transfers between devices  17.7 us (6%)
  other arithmetic  6.43 us (2%)
    pad x4, local copies, waits for them, and re-layouts, spread(): return lax.pad(x, jnp.zeros((), x.dtype), cfg)  127 us
    all_to_all x2, blocking collectives, summed_everywhere(): lax.all_to_all(parts, 'scene', 0, 0, axis_index_groups=ring, tiled=True)  28 us
    all_to_all x1, blocking collectives, summed_everywhere(): own = pieces_summed(lax.all_to_all(parts, 'leaf', 0, 0, tiled=True))  23.3 us
    pallas_call x1, Pallas kernels, first_call(): pl.pallas_call(first_kernel, out_shape=(jax.ShapeDtypeStruct((L, 4, 2, RO...  22.3 us
    all_to_all x1, blocking collectives, summed_everywhere(): lax.all_to_all(parts, 'leaf', 0, 0, tiled=True)  14.2 us
    pallas_call x1, Pallas kernels, adjoint_call(): pl.pallas_call(adjoint_kernel, out_shape=jax.ShapeDtypeStruct((L, 4, 2, R...  12.6 us
    ppermute x4, starting transfers between devices, passed(): lax.ppermute(block, 'leaf', [(i - distance, i) for i in range(count) if 0...  10.5 us
    slice x1, local copies, waits for them, and re-layouts, shards(): coarse = coarse[:, :, :, ::2]  9.77 us
  transfers between devices with their start and end apart: 6, of which 1 were waited for; matrix products, arithmetic and copies ran while one was open for 50% of the time, Pallas kernels for 4%

profile of v1, /device:TPU:1, one launch (start us, length us, event | category | flops | bytes accessed | tf_op | source)
XLA Modules:
  0.0 294.3 jit_solution(2503672759004032297)
XLA Ops:
  1.9 1.6 copy.100
  3.6 4.0 %collective-permute-start = (bf16[8,8,8,128]{3,2,1,0:T(8,128)(2,1)S(1)}, bf16[8,8,8,128]{3,2,1,0:T(8,128)(2,1)S(1)}, u32[]{:S(2)}, u32[]{:S(2)}) collective-permute-start(bf16[8,8,8,128]{3,2,1,0:T(8,128)(2,1)S(1)} %fusion.2), channel_id=1, source_target_pairs={{0,8},{8,16},{16,24},{24,32},{32,40},{40,48},{48,56},{56,64},{64,7... | collective-permute-start | bytes 393224 | tf_op jit(solution)/shard_map/faces_in/ppermute | solution.py:309
  7.6 3.0 %slice.82 = bf16[8,4,4,4,1]{3,2,1,0,4:T(4,128)(2,1)S(1)} slice(bf16[8,8,8,8,1]{3,2,1,0,4:T(8,128)(2,1)S(1)} %convert_element_type.59), slice={[0:8:1], [0:8:2], [0:8:2], [0:8:2], [0:1:1]} | slice | bytes 2048 | tf_op jit(solution)/shard_map/slice | solution.py:370
  11.1 1.3 collective-permute-start.1
  13.3 1.1 pad_maximum_fusion.1.w2t
  14.7 39.0 %pad.16.cot = bf16[8,4,8,8,128]{4,3,2,1,0:T(8,128)(2,1)} pad(bf16[8,4,4,4,128]{4,3,2,1,0:T(4,128)(2,1)S(1)} %bitcast_multiply_fusion, bf16[]{:T(256)} %constant.43.clone.1), padding=0_0_0x0_0_0x0_1_1x0_1_1x0_0_0 | pad | bytes 655362 | tf_op jit(solution)/shard_map/pad | solution.py:320
  54.4 10.2 %pad.17.cot_high_in = bf16[8,4,8,128]{3,2,1,0:T(8,128)(2,1)} pad(bf16[8,4,4,128]{3,2,1,0:T(4,128)(2,1)S(1)} %bitcast.98, bf16[]{:T(256)} %constant.43.clone.1), padding=0_0_0x0_0_0x0_1_1x0_0_0 | pad | bytes 98306 | tf_op jit(solution)/shard_map/pad | solution.py:320
  65.3 1.6 broadcast_in_dim.12.mask
  66.8 22.3 %first_conv.1 = (bf16[8,4,2,64,128]{4,3,2,1,0:T(8,128)(2,1)}, bf16[8,4,2,64,128]{4,3,2,1,0:T(8,128)(2,1)}, bf16[27,128,128]{2,1,0:T(8,128)(2,1)}) custom-call(s32[8,27]{1,0:T(8,128)} %pad_add_fusion.table, bf16[8,8,8,8,128]{4,3,2,1,0:T(8,128)(2,1)} %bitcast.87, bf16[8,8,8,8,128]{4,3,2,1,0:T(8,128)(2,1)} %broadcast_in_dim.12.mask, ...), custom_call_target="tpu_custom_call" | custom-call | flops 8000000000 | bytes 8000000 | tf_op jit(solution)/shard_map/first_conv/pallas_call | solution.py:156
  89.2 1.5 slice.110
  90.7 2.2 fusion.7
  92.9 4.0 %collective-permute-start.2 = (bf16[2,8,8,8,128]{4,3,2,1,0:T(8,128)(2,1)S(1)}, bf16[2,8,8,8,128]{4,3,2,1,0:T(8,128)(2,1)S(1)}, u32[]{:S(2)}, u32[]{:S(2)}) collective-permute-start(bf16[2,8,8,8,128]{4,3,2,1,0:T(8,128)(2,1)S(1)} %pad_maximum_fusion.2), channel_id=1, source_target_pairs={{0,8},{8,16},{16,24},{24,32},{32,40},{40,48},{48,56},{56,64},{64,7... | collective-permute-start | bytes 786440 | tf_op jit(solution)/shard_map/faces_mid/ppermute | solution.py:309
  97.0 38.9 %pad.18.cot = bf16[8,4,4,8,128]{4,3,2,1,0:T(8,128)(2,1)} pad(bf16[8,4,4,4,128]{4,3,2,1,0:T(4,128)(2,1)S(1)} %bitcast_multiply_fusion, bf16[]{:T(256)} %constant.43.clone.1), padding=0_0_0x0_0_0x0_0_0x0_1_1x0_0_0 | pad | bytes 393218 | tf_op jit(solution)/shard_map/pad | solution.py:320
  136.1 38.8 %pad.19.cmask = bf16[8,4,4,8,128]{4,3,2,1,0:T(8,128)(2,1)} pad(bf16[8,4,4,4,128]{4,3,2,1,0:T(4,128)(2,1)S(1)} %mul.48, bf16[]{:T(256)} %constant.43.clone.1), padding=0_0_0x0_0_0x0_0_0x0_1_1x0_0_0 | pad | bytes 393218 | tf_op jit(solution)/shard_map/pad | solution.py:320
  175.6 9.1 %second_conv.1 = (bf16[8,4,4,8,128]{4,3,2,1,0:T(8,128)(2,1)}, bf16[27,128,128]{2,1,0:T(8,128)(2,1)}) custom-call(s32[8,27]{1,0:T(8,128)} %pad_add_fusion.table, bf16[8,8,8,8,128]{4,3,2,1,0:T(8,128)(2,1)} %bitcast.101, bf16[8,8,8,128]{3,2,1,0:T(8,128)(2,1)} %get-tuple-element.26.low_in, bf16[8,4,4,8,128]{4,3,2,1,0:T(8,128)(2,1)} %pad.18.cot, ...), custom_call_target="tpu_custom_call" | custom-call | flops 2000000000 | bytes 5000000 | tf_op jit(solution)/shard_map/second_conv/pallas_call | solution.py:286
  184.7 1.3 pad_maximum_fusion
  186.1 1.0 dynamic-slice_bitcast_fusion
  187.1 1.5 collective-permute-start.4
  188.6 2.3 collective-permute-done.4
  191.3 16.6 %all_to_all.20 = bf16[4,54,16,128]{3,2,1,0:T(8,128)(2,1)S(1)} all-to-all(bf16[4,54,16,128]{3,2,1,0:T(8,128)(2,1)S(1)} %copy.84), channel_id=1, replica_groups={{0,2,4,6},{1,3,5,7},{8,10,12,14},{9,11,13,15},{16,18,20,22},{17,19,21,2..., dimensions={0} | all-to-all | bytes 1769472 | tf_op jit(solution)/shard_map/sum_y/all_to_all | solution.py:343
  208.1 23.3 %all_to_all.21 = bf16[32,32,128]{2,1,0:T(8,128)(2,1)S(1)} all-to-all(bf16[32,32,128]{2,1,0:T(8,128)(2,1)S(1)} %bitcast.88), channel_id=1, replica_groups=mesh['leaf'=32,'scene'=8] {'leaf'}, dimensions={0} | all-to-all | bytes 524288 | tf_op jit(solution)/shard_map/sum_leaf/all_to_all | solution.py:346
  231.5 14.2 %all_to_all.22 = bf16[32,32,128]{2,1,0:T(8,128)(2,1)S(1)} all-to-all(bf16[32,32,128]{2,1,0:T(8,128)(2,1)S(1)} %broadcast_in_dim.14), channel_id=1, replica_groups=mesh['leaf'=32,'scene'=8] {'leaf'}, dimensions={0} | all-to-all | bytes 524288 | tf_op jit(solution)/shard_map/gather_leaf/all_to_all | solution.py:351
  245.8 11.4 %all_to_all.23 = bf16[4,54,16,128]{3,2,1,0:T(8,128)(2,1)S(1)} all-to-all(bf16[4,54,16,128]{3,2,1,0:T(8,128)(2,1)S(1)} %broadcast_in_dim.16), channel_id=1, replica_groups={{0,2,4,6},{1,3,5,7},{8,10,12,14},{9,11,13,15},{16,18,20,22},{17,19,21,2..., dimensions={0} | all-to-all | bytes 1769472 | tf_op jit(solution)/shard_map/gather_y/all_to_all | solution.py:354
  257.2 1.2 copy.86
  258.4 5.6 %collective-permute-start.5 = (bf16[4,54,16,128]{3,2,0,1:T(8,128)(2,1)}, bf16[4,54,16,128]{3,2,0,1:T(8,128)(2,1)}, u32[]{:S(2)}, u32[]{:S(2)}) collective-permute-start(bf16[4,54,16,128]{3,2,0,1:T(8,128)(2,1)} %copy.86), channel_id=1, source_target_pairs={{0,1},{1,0},{2,3},{3,2},{4,5},{5,4},{6,7},{7,6},{8,9},{9,8},{10,11... | collective-permute-start | bytes 2654216 | tf_op jit(solution)/shard_map/gather_core/ppermute | solution.py:356
  264.1 1.3 copy.82
  265.4 1.3 collective-permute-start.3
  266.7 1.0 reverse_bitcast_fusion.w
  267.7 9.8 %slice.92 = bf16[8,4,4,4,128]{4,3,2,1,0:T(4,128)(2,1)} slice(bf16[8,4,4,8,128]{4,3,2,1,0:T(8,128)(2,1)S(1)} %copy-done.4), slice={[0:8:1], [0:4:1], [0:4:1], [0:8:2], [0:128:1]} | slice | bytes 262144 | tf_op jit(solution)/shard_map/slice | solution.py:396
  278.1 12.6 %first_adjoint.1 = bf16[8,4,2,64,128]{4,3,2,1,0:T(8,128)(2,1)} custom-call(s32[8,27]{1,0:T(8,128)} %pad_add_fusion.table, bf16[8,8,8,8,128]{4,3,2,1,0:T(8,128)(2,1)} %bitcast.95, bf16[8,8,8,8,128]{4,3,2,1,0:T(8,128)(2,1)} %broadcast_in_dim.12.mask, bf16[8,8,8,128]{3,2,1,0:T(8,128)(2,1)} %get-tuple-element.25.low_in, bf16[8,8,8,128]{3,2,1,0:T(8,128)(2,1)} %copy-done.7, ...), custom_call_target="tpu_custom_call" | custom-call | flops 4000000000 | bytes 5000000 | tf_op jit(solution)/shard_map/first_adjoint/pallas_call | solution.py:213
  290.7 1.3 select_bitcast_fusion.1
  292.2 2.1 fusion.6
  (60 shorter events, 7.2 us)
Async XLA Ops:
  0.6 10.0 %copy-start.3 = (bf16[1,8,4,4,4,128]{5,4,3,2,1,0:T(4,128)(2,1)S(1)}, bf16[1,8,4,4,4,128]{5,4,3,2,1,0:T(4,128)(2,1)}, u32[]{:S(2)}) copy-start(bf16[1,8,4,4,4,128]{5,4,3,2,1,0:T(4,128)(2,1)} %param.9) | copy-start | bytes 393220
  1.9 10.6 %copy-start.5 = (s32[1,8,26]{2,1,0:T(8,128)S(1)}, s32[1,8,26]{2,1,0:T(8,128)}, u32[]{:S(2)}) copy-start(s32[1,8,26]{2,1,0:T(8,128)} %param.10) | copy-start | bytes 2500
  1.9 10.6 %copy-start.1 = (bf16[27,128,128]{2,1,0:T(8,128)(2,1)S(1)}, bf16[27,128,128]{2,1,0:T(8,128)(2,1)}, u32[]{:S(2)}) copy-start(bf16[27,128,128]{2,1,0:T(8,128)(2,1)} %w2.1) | copy-start | bytes 2654212
  3.6 61.6 %collective-permute-start = (bf16[8,8,8,128]{3,2,1,0:T(8,128)(2,1)S(1)}, bf16[8,8,8,128]{3,2,1,0:T(8,128)(2,1)S(1)}, u32[]{:S(2)}, u32[]{:S(2)}) collective-permute-start(bf16[8,8,8,128]{3,2,1,0:T(8,128)(2,1)S(1)} %fusion.2), channel_id=1, source_target_pairs={{0,8},{8,16},{16,24},{24,32},{32,40},{40,48},{48,56},{56,64},{64,7... | collective-permute-start | bytes 393224 | tf_op jit(solution)/shard_map/faces_in/ppermute | solution.py:309
  11.1 43.2 %collective-permute-start.1 = (bf16[8,80,128]{2,1,0:T(8,128)(2,1)S(1)}, bf16[8,80,128]{2,1,0:T(8,128)(2,1)S(1)}, u32[]{:S(2)}, u32[]{:S(2)}) collective-permute-start(bf16[8,80,128]{2,1,0:T(8,128)(2,1)S(1)} %pad_maximum_fusion.3), channel_id=1, source_target_pairs={{8,0},{16,8},{24,16},{32,24},{40,32},{48,40},{56,48},{64,56},{72,6... | collective-permute-start | bytes 491528 | tf_op jit(solution)/shard_map/faces_in/ppermute | solution.py:309
  65.3 1.6 copy-start.6
  92.9 82.0 %collective-permute-start.2 = (bf16[2,8,8,8,128]{4,3,2,1,0:T(8,128)(2,1)S(1)}, bf16[2,8,8,8,128]{4,3,2,1,0:T(8,128)(2,1)S(1)}, u32[]{:S(2)}, u32[]{:S(2)}) collective-permute-start(bf16[2,8,8,8,128]{4,3,2,1,0:T(8,128)(2,1)S(1)} %pad_maximum_fusion.2), channel_id=1, source_target_pairs={{0,8},{8,16},{16,24},{24,32},{32,40},{40,48},{48,56},{56,64},{64,7... | collective-permute-start | bytes 786440 | tf_op jit(solution)/shard_map/faces_mid/ppermute | solution.py:309
  175.6 9.1 %copy-start = (bf16[27,128,128]{2,1,0:T(8,128)(2,1)S(1)}, bf16[27,128,128]{2,1,0:T(8,128)(2,1)}, u32[]{:S(2)}) copy-start(bf16[27,128,128]{2,1,0:T(8,128)(2,1)} %get-tuple-element.12) | copy-start | bytes 2654212
  187.1 3.8 %collective-permute-start.4 = (bf16[54,64,128]{2,1,0:T(8,128)(2,1)}, bf16[54,64,128]{2,1,0:T(8,128)(2,1)S(1)}, u32[]{:S(2)}, u32[]{:S(2)}) collective-permute-start(bf16[54,64,128]{2,1,0:T(8,128)(2,1)} %dynamic-slice_bitcast_fusion), channel_id=1, source_target_pairs={{0,1},{1,0},{2,3},{3,2},{4,5},{5,4},{6,7},{7,6},{8,9},{9,8},{10,11... | collective-permute-start | bytes 2654216 | tf_op jit(solution)/shard_map/sum_core/ppermute | solution.py:340
  245.8 18.2 %copy-start.2 = (bf16[27,128,128]{2,1,0:T(8,128)(2,1)S(1)}, bf16[27,128,128]{2,1,0:T(8,128)(2,1)}, u32[]{:S(2)}) copy-start(bf16[27,128,128]{2,1,0:T(8,128)(2,1)} %w1.1) | copy-start | bytes 2654212
  258.4 32.3 %collective-permute-start.5 = (bf16[4,54,16,128]{3,2,0,1:T(8,128)(2,1)}, bf16[4,54,16,128]{3,2,0,1:T(8,128)(2,1)}, u32[]{:S(2)}, u32[]{:S(2)}) collective-permute-start(bf16[4,54,16,128]{3,2,0,1:T(8,128)(2,1)} %copy.86), channel_id=1, source_target_pairs={{0,1},{1,0},{2,3},{3,2},{4,5},{5,4},{6,7},{7,6},{8,9},{9,8},{10,11... | collective-permute-start | bytes 2654216 | tf_op jit(solution)/shard_map/gather_core/ppermute | solution.py:356
  264.1 3.6 %copy-start.4 = (bf16[8,4,4,8,128]{4,3,2,1,0:T(8,128)(2,1)S(1)}, bf16[8,4,4,8,128]{4,3,2,1,0:T(8,128)(2,1)}, u32[]{:S(2)}) copy-start(bf16[8,4,4,8,128]{4,3,2,1,0:T(8,128)(2,1)} %get-tuple-element.11) | copy-start | bytes 786436
  265.4 12.1 %collective-permute-start.3 = (bf16[8,8,8,128]{3,2,1,0:T(8,128)(2,1)S(1)}, bf16[8,8,8,128]{3,2,1,0:T(8,128)(2,1)S(1)}, u32[]{:S(2)}, u32[]{:S(2)}) collective-permute-start(bf16[8,8,8,128]{3,2,1,0:T(8,128)(2,1)S(1)} %bitcast.96), channel_id=1, source_target_pairs={{8,0},{16,8},{24,16},{32,24},{40,32},{48,40},{56,48},{64,56},{72,6... | collective-permute-start | bytes 393224 | tf_op jit(solution)/shard_map/faces_mid/ppermute | solution.py:309
  277.5 0.6 copy-start.7

commit v2 on v0

v2 whole, which is shorter than its diff:
```python
import math

import jax
import jax.numpy as jnp
from jax import lax
from jax.experimental import pallas as pl
from jax.experimental.pallas import tpu as pltpu
from jax.sharding import PartitionSpec as P

bf16 = jnp.bfloat16
f32 = jnp.float32
C = 128
L = 8
E = 8
FACE = E * E
SPAN = 9 * C
TAPS = 27
HALF = C // 2
PIECE = 16


def smem():
    return pl.BlockSpec(memory_space=pltpu.SMEM)


def vmem():
    return pl.BlockSpec(memory_space=pltpu.VMEM)


def params(mebibytes):
    return pltpu.CompilerParams(vmem_limit_bytes=mebibytes * 1024 * 1024)


def cost(flops, size):
    return pl.CostEstimate(flops=int(flops), bytes_accessed=int(size), transcendentals=0)


def edge_row(face, block, i, j):
    return jnp.broadcast_to(face[block, i, pl.ds(j, 1), :], (E, C))


def source_plane(x, top):
    if isinstance(x, int):
        a = 0 if x == 0 else 18 if x == top + 1 else 9
        return a, top - 1 if x == 0 else 0 if x == top + 1 else x - 1
    first, last = x == 0, x == top + 1
    return jnp.where(first, 0, jnp.where(last, 18, 9)), jnp.where(first, top - 1, jnp.where(last, 0, x - 1))


def shifted_lines(table, lines, low, high, leaf, x, top, rows):
    a, i = source_plane(x, top)
    at = [[table[leaf, a + 3 * b + c] for c in range(3)] for b in range(3)]
    ids = lax.broadcasted_iota(jnp.int32, (E, C), 0)
    out = ([], [], [])
    for y in rows:
        b = 0 if y == 0 else 2 if y == E + 1 else 1
        j = E - 1 if y == 0 else 0 if y == E + 1 else y - 1
        line = lines[at[b][1], i, E * j : E * j + E]
        below = jnp.where(ids == 0, 0.0 if low is None else edge_row(low, at[b][0], i, j), pltpu.roll(line, 1, 0))
        above = pltpu.roll(line, E - 1, 0)
        if high is not None:
            above = jnp.where(ids == E - 1, edge_row(high, at[b][2], i, j), above)
        for r, part in enumerate((below, line, above)):
            out[r].append(part)
    return out


def fill_plane(store, *where):
    parts = shifted_lines(*where, range(E + 2))
    whole = [jnp.concatenate(part, axis=0) for part in parts]
    for q in range(3):
        for r in range(3):
            store((3 * q + r) * C, whole[r][E * q : E * q + FACE].astype(bf16))


def banded(weight, first, second):
    zero = jnp.zeros((SPAN, C), bf16)
    w = [weight[9 * s : 9 * s + 9].reshape(SPAN, C) for s in range(3)]
    first[:SPAN, :C] = w[0]
    first[:SPAN, C:] = zero
    first[SPAN:, :C] = w[1]
    first[SPAN:, C:] = w[0]
    second[:SPAN, :C] = w[2]
    second[:SPAN, C:] = w[1]
    second[SPAN:, :C] = zero
    second[SPAN:, C:] = w[2]


def banded_turned(weight, first, second):
    zero = jnp.zeros((C, SPAN), bf16)
    w = [jnp.concatenate([weight[TAPS - 1 - t] for t in range(9 * s, 9 * s + 9)], axis=1) for s in range(3)]
    first[:C, :SPAN] = w[0]
    first[C:, :SPAN] = zero
    first[:C, SPAN:] = w[1]
    first[C:, SPAN:] = w[0]
    second[:C, :SPAN] = w[2]
    second[C:, :SPAN] = w[1]
    second[:C, SPAN:] = zero
    second[C:, SPAN:] = w[2]


def dot(x, w):
    return jnp.dot(x, w, preferred_element_type=f32)


def dot_turned(x, w):
    return lax.dot_general(x, w, (((1,), (1,)), ((), ())), preferred_element_type=f32)


def pairs_dot(multiply, cols, at, first, second):
    lo = cols[at, 0:4].reshape(4 * FACE, 2 * SPAN)
    hi = cols[at, 1:5].reshape(4 * FACE, 2 * SPAN)
    return multiply(lo, first[...]) + multiply(hi, second[...])


def half_planes(ref, leaf, half):
    return jnp.concatenate([ref[leaf, 2 * pair + half] for pair in range(4)], axis=0)


def prepare_kernel(voxels, feat, cot, mask, up, down, spread, held, coarse):
    @pl.loop(0, L)
    def _(leaf):
        row = jnp.broadcast_to(voxels[pl.ds(leaf, 1), :].astype(f32), (C, E**3))
        whole = row.T
        spread[...] = whole
        mask[leaf] = whole.reshape(E, FACE, C).astype(bf16)
        held[...] = feat[leaf].reshape(E**3, C).astype(f32) * whole
        up[leaf] = held[pl.ds(E - 1, FACE, stride=E), :].astype(bf16)
        down[leaf, 0:FACE] = held[pl.ds(0, FACE, stride=E), :].astype(bf16)
        coarse[...] = cot[leaf].astype(f32)
        edge = coarse[pl.ds(0, 16, stride=4), :]
        active = jnp.concatenate([spread[pl.ds(2 * FACE * i, 4, stride=16), :] for i in range(4)], axis=0)
        down[leaf, FACE : FACE + 16] = (edge * active).astype(bf16)


def prepare(voxels, feat, cot):
    return pl.pallas_call(
        prepare_kernel,
        out_shape=(
            jax.ShapeDtypeStruct((L, E, FACE, C), bf16),
            jax.ShapeDtypeStruct((L, FACE, C), bf16),
            jax.ShapeDtypeStruct((L, FACE + 16, C), bf16),
        ),
        in_specs=[vmem()] * 3,
        out_specs=(vmem(),) * 3,
        scratch_shapes=[pltpu.VMEM((E**3, C), f32), pltpu.VMEM((E**3, C), f32), pltpu.VMEM((64, C), f32)],
        compiler_params=params(16),
        name="prepare",
    )(voxels, feat, cot)


def first_kernel(
    table, feat, mask, low_in, high_in, cot, w1, w2,
    cols, hidden, delta, up, down,
    lines, low, high, clines, chigh, ccols, coarse, wa, wb, wc, faces,
):
    step = pl.program_id(0)

    @pl.when(step == 0)
    def _():
        lines[L] = jnp.zeros((E, FACE, C), f32)
        low[L] = jnp.zeros((E, E, C), f32)
        high[L] = jnp.zeros((E, E, C), f32)
        clines[L] = jnp.zeros((4, FACE, C), f32)
        chigh[...] = jnp.zeros((L + 1, 4, E, C), f32)

        @pl.loop(0, L)
        def _(leaf):
            lines[leaf] = feat[leaf].astype(f32) * mask[leaf].astype(f32)
            low[leaf] = low_in[leaf].astype(f32).reshape(E, E, C)
            high[leaf] = high_in[leaf, 0:FACE].astype(f32).reshape(E, E, C)
            coarse[0:16] = high_in[leaf, FACE : FACE + 16].astype(f32)
            for i in range(4):
                chigh[leaf, i, pl.ds(0, 4, stride=2), :] = coarse[4 * i : 4 * i + 4]
            coarse[...] = cot[leaf].astype(f32)
            clines[leaf] = jnp.zeros((4, FACE, C), f32)
            for i in range(4):
                for j in range(4):
                    clines[leaf, i, pl.ds(16 * j, 4, stride=2), :] = coarse[16 * i + 4 * j : 16 * i + 4 * j + 4]
                clines[leaf, i] = clines[leaf, i] * mask[leaf, 2 * i].astype(f32)

        banded(w1, wa, wb)
        for n, p in enumerate((1, 2, 0)):
            for t in range(9):
                wc[n * C : n * C + C, t * C : t * C + C] = w2[9 * p + 8 - t]

    for pair in range(5):
        for half in range(2):
            def store(at, value, pair=pair, half=half):
                cols[0, pair, :, half * SPAN + at : half * SPAN + at + C] = value
            fill_plane(store, table, lines, low, high, step, 2 * pair + half, E)

        def store_coarse(at, value, pair=pair):
            ccols[pair, :, at : at + C] = value
        fill_plane(store_coarse, table, clines, None, chigh, step, pair + 1, 4)

    pre = pairs_dot(dot, cols, 0, wa, wb)
    back = dot_turned(ccols[0:4].reshape(4 * FACE, SPAN), wc[: 2 * C])
    back_next = dot_turned(ccols[1:5].reshape(4 * FACE, SPAN), wc[2 * C :])
    sig = 1.0 / (1.0 + jnp.exp(-pre))
    slope = sig * (1.0 + pre * (1.0 - sig))
    for half in range(2):
        at = slice(half * C, half * C + C)
        m = half_planes(mask, step, half).astype(f32)
        h = m * pre[:, at] * sig[:, at]
        g = back[:, at] if half == 0 else back[:, at] + back_next
        d = g * m * slope[:, at]
        for pair in range(4):
            rows = slice(FACE * pair, FACE * pair + FACE)
            hidden[0, 2 * pair + half] = h[rows].astype(bf16)
            delta[0, 2 * pair + half] = d[rows].astype(bf16)
            faces[0, 2 * pair + half] = h[rows]
            faces[1, 2 * pair + half] = d[rows]
    for i in range(0, E, 2):
        def face(which, k, i=i):
            return jnp.concatenate([faces[which, i + n, pl.ds(k, E, stride=E), :] for n in range(2)], axis=0).astype(bf16)
        rows = slice(E * i, E * i + 2 * E)
        up[0, 0, rows] = face(0, E - 1)
        up[1, 0, rows] = face(1, E - 1)
        down[0, rows] = face(1, 0)


def first_conv(table, feat, mask, low, high, cot, w1, w2):
    def leafwise(*shape):
        return pl.BlockSpec((1, *shape), lambda s: (s,) + (0,) * len(shape))

    return pl.pallas_call(
        first_kernel,
        grid=(L,),
        out_shape=(
            jax.ShapeDtypeStruct((L, 5, FACE, 2 * SPAN), bf16),
            jax.ShapeDtypeStruct((L, E, FACE, C), bf16),
            jax.ShapeDtypeStruct((L, E, FACE, C), bf16),
            jax.ShapeDtypeStruct((2, L, FACE, C), bf16),
            jax.ShapeDtypeStruct((L, FACE, C), bf16),
        ),
        in_specs=[smem()] + [vmem()] * 7,
        out_specs=(
            leafwise(5, FACE, 2 * SPAN),
            leafwise(E, FACE, C),
            leafwise(E, FACE, C),
            pl.BlockSpec((2, 1, FACE, C), lambda s: (0, s, 0, 0)),
            leafwise(FACE, C),
        ),
        scratch_shapes=[
            pltpu.VMEM((L + 1, E, FACE, C), f32),
            pltpu.VMEM((L + 1, E, E, C), f32),
            pltpu.VMEM((L + 1, E, E, C), f32),
            pltpu.VMEM((L + 1, 4, FACE, C), f32),
            pltpu.VMEM((L + 1, 4, E, C), f32),
            pltpu.VMEM((5, FACE, SPAN), bf16),
            pltpu.VMEM((64, C), f32),
            pltpu.VMEM((2 * SPAN, 2 * C), bf16),
            pltpu.VMEM((2 * SPAN, 2 * C), bf16),
            pltpu.VMEM((3 * C, SPAN), bf16),
            pltpu.VMEM((2, E, FACE, C), f32),
        ],
        compiler_params=params(28),
        cost_estimate=cost(15e9, 18e6),
        name="first_conv",
    )(table, feat, mask, low, high, cot, w1, w2)


def split_halves(core, whole, kept, sent):
    mine = pl.multiple_of(core * HALF, HALF)
    theirs = pl.multiple_of(HALF - core * HALF, HALF)
    for t in range(TAPS):
        kept[t] = whole[t, pl.ds(mine, HALF), :]
        sent[t] = whole[t, pl.ds(theirs, HALF), :].astype(bf16)


def first_grad_kernel(core, cols, delta, kept, sent, turned, total, whole):
    @pl.loop(0, L)
    def _(leaf):
        for half in range(2):
            turned[half * C : half * C + C, pl.ds(pl.multiple_of(leaf * 256, 256), 256)] = half_planes(delta, leaf, half).T

    total[...] = jnp.zeros_like(total)
    for tile in range(9):
        lanes = range(256 * tile, 256 * tile + 256, C)
        for next_pair in range(2):
            rhs = cols[:, next_pair : next_pair + 4, :, 256 * tile : 256 * tile + 256].reshape(L * 4 * FACE, 256)
            for half in range(2):
                use = [lane for lane in lanes if 0 <= 2 * next_pair + lane // SPAN - half <= 2]
                if not use:
                    continue
                res = dot(turned[half * C : half * C + C, :], rhs)
                for lane in use:
                    p, o = 2 * next_pair + lane // SPAN - half, lane % SPAN
                    total[p, :, o : o + C] += res[:, lane - 256 * tile : lane - 256 * tile + C]

    for p in range(3):
        for t in range(9):
            whole[9 * p + t] = total[p, :, t * C : t * C + C].T
    split_halves(core[0], whole, kept, sent)


def halves_shape():
    return jax.ShapeDtypeStruct((TAPS, HALF, C), f32), jax.ShapeDtypeStruct((TAPS, HALF, C), bf16)


def first_grad(core, cols, delta):
    return pl.pallas_call(
        first_grad_kernel,
        out_shape=halves_shape(),
        in_specs=[smem(), vmem(), vmem()],
        out_specs=(vmem(), vmem()),
        scratch_shapes=[
            pltpu.VMEM((2 * C, L * 256), bf16),
            pltpu.VMEM((3, C, SPAN), f32),
            pltpu.VMEM((TAPS, C, C), f32),
        ],
        compiler_params=params(16),
        cost_estimate=cost(6e9, 14e6),
        name="first_grad",
    )(core, cols, delta)


def second_kernel(
    table, core, hidden, low_in, cot, mask, w2,
    coarse, kept, sent,
    lines, low, cols, turned, total, whole, thin,
):
    lines[L] = jnp.zeros((E, FACE, C), f32)
    low[L] = jnp.zeros((E, E, C), f32)
    thin[0] = jnp.zeros((2 * FACE, C), f32)

    @pl.loop(0, L)
    def _(leaf):
        lines[leaf] = hidden[leaf].astype(f32)
        low[leaf] = low_in[leaf].astype(f32).reshape(E, E, C)

    w = w2[...].reshape(TAPS * C, C)

    @pl.loop(0, L)
    def _(leaf):
        for x in range(E + 1):
            parts = shifted_lines(table, lines, low, None, leaf, x, E, range(E + 1))
            for q in range(3):
                for r in range(3):
                    value = jnp.concatenate([parts[r][q + 2 * m] for m in range(4)], axis=0).astype(bf16)
                    at = (x % 2) * SPAN + (3 * q + r) * C
                    cols[leaf, x // 2, :, at : at + C] = value
        lo = cols[leaf, 0:4].reshape(2 * FACE, 2 * SPAN)
        hi = cols[leaf, 1:5, :, 0:SPAN].reshape(2 * FACE, SPAN)
        res = jnp.dot(lo, w[: 2 * SPAN], preferred_element_type=f32) + jnp.dot(hi, w[2 * SPAN :], preferred_element_type=f32)
        active = []
        for i in range(4):
            plane = mask[leaf, 2 * i].astype(f32)
            active += [plane[16 * j : 16 * j + E] for j in range(4)]
        active = jnp.concatenate(active, axis=0)
        thin[1] = res * active
        coarse[leaf] = thin[1, pl.ds(0, FACE, stride=2), :].astype(bf16)
        thin[0, pl.ds(0, FACE, stride=2), :] = cot[leaf].astype(f32)
        upstream = (thin[0] * active).astype(bf16)
        turned[:, pl.ds(pl.multiple_of(leaf * 128, 128), 128)] = upstream.T

    for tile in range(9):
        at = slice(256 * tile, 256 * tile + 256)
        total[:, at] = jnp.dot(turned[...], cols[:, 0:4, :, at].reshape(L * 2 * FACE, 256), preferred_element_type=f32)
    for tile in range(5):
        end = min(256 * tile + 256, SPAN)
        rhs = cols[:, 1:5, :, 256 * tile : end].reshape(L * 2 * FACE, end - 256 * tile)
        total[:, 2 * SPAN + 256 * tile : 2 * SPAN + end] = jnp.dot(turned[...], rhs, preferred_element_type=f32)
    for t in range(TAPS):
        whole[t] = total[:, t * C : t * C + C].T
    split_halves(core[0], whole, kept, sent)


def second_conv(table, core, hidden, low, cot, mask, w2):
    return pl.pallas_call(
        second_kernel,
        out_shape=(jax.ShapeDtypeStruct((L, 64, C), bf16), *halves_shape()),
        in_specs=[smem()] * 2 + [vmem()] * 5,
        out_specs=(vmem(),) * 3,
        scratch_shapes=[
            pltpu.VMEM((L + 1, E, FACE, C), f32),
            pltpu.VMEM((L + 1, E, E, C), f32),
            pltpu.VMEM((L, 5, 32, 2 * SPAN), bf16),
            pltpu.VMEM((C, L * 128), bf16),
            pltpu.VMEM((C, 3 * SPAN), f32),
            pltpu.VMEM((TAPS, C, C), f32),
            pltpu.VMEM((2, 2 * FACE, C), f32),
        ],
        compiler_params=params(40),
        cost_estimate=cost(8e9, 6e6),
        name="second_conv",
    )(table, core, hidden, low, cot, mask, w2)


def adjoint_kernel(start, count, table, delta, mask, low_in, high_in, w, out, lines, low, high, cols, wa, wb):
    lines[L] = jnp.zeros((E, FACE, C), f32)
    low[L] = jnp.zeros((E, E, C), f32)
    high[L] = jnp.zeros((E, E, C), f32)

    @pl.loop(0, L)
    def _(leaf):
        lines[leaf] = delta[leaf].astype(f32)
        low[leaf] = low_in[leaf].astype(f32).reshape(E, E, C)
        high[leaf] = high_in[leaf].astype(f32).reshape(E, E, C)

    banded_turned(w, wa, wb)

    @pl.loop(0, count)
    def _(n):
        for pair in range(5):
            for half in range(2):
                def store(at, value, pair=pair, half=half):
                    cols[0, pair, :, half * SPAN + at : half * SPAN + at + C] = value
                fill_plane(store, table, lines, low, high, start + n, 2 * pair + half, E)
        res = pairs_dot(dot_turned, cols, 0, wa, wb)
        for half in range(2):
            m = half_planes(mask, start + n, half).astype(f32)
            value = (res[:, half * C : half * C + C] * m).astype(bf16)
            for pair in range(4):
                out[n, 2 * pair + half] = value[FACE * pair : FACE * pair + FACE]


def adjoint_conv(start, count, table, delta, mask, low, high, w):
    def kernel(*refs):
        adjoint_kernel(start, count, *refs)

    return pl.pallas_call(
        kernel,
        out_shape=jax.ShapeDtypeStruct((count, E, FACE, C), bf16),
        in_specs=[smem()] + [vmem()] * 5,
        out_specs=vmem(),
        scratch_shapes=[
            pltpu.VMEM((L + 1, E, FACE, C), f32),
            pltpu.VMEM((L + 1, E, E, C), f32),
            pltpu.VMEM((L + 1, E, E, C), f32),
            pltpu.VMEM((1, 5, FACE, 2 * SPAN), bf16),
            pltpu.VMEM((2 * C, 2 * SPAN), bf16),
            pltpu.VMEM((2 * C, 2 * SPAN), bf16),
        ],
        compiler_params=params(32),
        cost_estimate=cost(10e9 * count / L, 6e6),
        name="first_adjoint",
    )(table, delta, mask, low, high, w)


def start_sum_kernel(place, kept1, got1, kept2, got2, own, *sends):
    mine = place[0]
    for d in range(4):
        rows = pl.ds(pl.multiple_of(((mine + d) % 4) * PIECE, PIECE), PIECE)
        for t in range(2 * TAPS):
            kept, got, n = (kept1, got1, t) if t < TAPS else (kept2, got2, t - TAPS)
            value = kept[n, rows, :] + got[n, rows, :].astype(f32)
            if d == 0:
                own[t] = value
            else:
                sends[d - 1][t] = value.astype(bf16)


def start_sum(place, kept1, got1, kept2, got2):
    return pl.pallas_call(
        start_sum_kernel,
        out_shape=(jax.ShapeDtypeStruct((2 * TAPS, PIECE, C), f32),) + (jax.ShapeDtypeStruct((2 * TAPS, PIECE, C), bf16),) * 3,
        in_specs=[smem()] + [vmem()] * 4,
        out_specs=(vmem(),) * 4,
        compiler_params=params(12),
        cost_estimate=cost(1e6, 3e6),
        name="start_sum",
    )(place, kept1, got1, kept2, got2)


def next_sum_kernel(own, a, b, c, out):
    value = own[...] + a[...].astype(f32) + b[...].astype(f32) + c[...].astype(f32)
    out[0 : 2 * TAPS] = value.astype(bf16)
    out[2 * TAPS :] = jnp.zeros((out.shape[0] - 2 * TAPS, PIECE, C), bf16)


def next_sum(own, received, taps):
    return pl.pallas_call(
        next_sum_kernel,
        out_shape=jax.ShapeDtypeStruct((taps, PIECE, C), bf16),
        in_specs=[vmem()] * 4,
        out_specs=vmem(),
        compiler_params=params(8),
        cost_estimate=cost(1e6, 2e6),
        name="next_sum",
    )(own, *received)


def last_sum_kernel(factor, parts, out):
    total = parts[0].astype(f32)
    for n in range(1, parts.shape[0]):
        total = total + parts[n].astype(f32)
    total = (total * factor).astype(bf16)
    for n in range(parts.shape[0]):
        out[n] = total


def last_sum(parts, factor):
    def kernel(*refs):
        last_sum_kernel(factor, *refs)

    return pl.pallas_call(
        kernel,
        out_shape=jax.ShapeDtypeStruct(parts.shape, bf16),
        in_specs=[vmem()],
        out_specs=vmem(),
        compiler_params=params(8),
        cost_estimate=cost(1e6, 1e6),
        name="last_sum",
    )(parts)


def finish_kernel(place, *refs):
    mine, theirs, (first, second) = refs[0:4], refs[4:8], refs[8:10]

    for d in range(4):
        for parts, core, at in ((mine, place[2], place[0]), (theirs, 1 - place[2], place[1])):
            row = pl.multiple_of(core * HALF + ((at - d + 4) % 4) * PIECE, PIECE)
            for t in range(2 * TAPS):
                out, n = (first, t) if t < TAPS else (second, t - TAPS)
                out[n, pl.ds(row, PIECE), :] = parts[d][t].astype(f32)


def finish(place, pieces):
    return pl.pallas_call(
        finish_kernel,
        out_shape=(jax.ShapeDtypeStruct((TAPS, C, C), f32),) * 2,
        in_specs=[smem()] + [vmem()] * 8,
        out_specs=(vmem(),) * 2,
        compiler_params=params(12),
        cost_estimate=cost(1e6, 6e6),
        name="finish",
    )(place, *pieces)


def ring_orders(leaf_count):
    out = []
    for d in range(1, 4):
        pairs = []
        for leaf in range(leaf_count):
            for scene in range(8):
                z, x, y, core = leaf // 4, leaf % 4, scene // 2, scene % 2
                x, y = (x, (y + d) % 4) if core == 0 else ((x + d) % 4, y)
                pairs.append((leaf * 8 + scene, (z * 4 + x) * 8 + y * 2 + core))
        out.append(pairs)
    return out


def rest_groups(leaf_count):
    depth = leaf_count // 4
    first = [[(z * 4 + x) * 8 + 2 * y for z in range(depth) for x in range(4)] for y in range(4)]
    second = [[(z * 4 + x) * 8 + 2 * y + 1 for z in range(depth) for y in range(4)] for x in range(4)]
    return first + second


def passed(block, distance):
    count = lax.axis_size("leaf")
    return lax.ppermute(block, "leaf", [(i - distance, i) for i in range(count) if 0 <= i - distance < count])


def to_other_core(block):
    return lax.ppermute(block, "scene", [(i, i ^ 1) for i in range(lax.axis_size("scene"))])


def local_table(neighbours):
    found = jnp.where(neighbours >= 0, neighbours % L, L)
    own = jnp.arange(L, dtype=jnp.int32)[:, None]
    return jnp.concatenate([found[:, :13], own, found[:, 13:]], axis=1)


def shards(features, weight_first, weight_second, cotangent, neighbours, voxel_mask):
    both = ("leaf", "scene")
    leaf_count, scene_count = lax.axis_size("leaf"), lax.axis_size("scene")
    leaf_at, scene_at = lax.axis_index("leaf"), lax.axis_index("scene")
    core, x_at, y_at = scene_at % 2, leaf_at % 4, scene_at // 2
    place = jnp.stack([jnp.where(core == 0, y_at, x_at), jnp.where(core == 0, x_at, y_at), core]).astype(jnp.int32)
    core = place[2:3]
    feat = features[0].reshape(L, E, FACE, C)
    cot = cotangent[0].reshape(L, 64, C)
    table = local_table(neighbours[0])

    mask, up, down = prepare(voxel_mask[0], feat, cot)
    with jax.named_scope("faces_in"):
        low = passed(up, 1)
        high = passed(down, -1)
    cols, hidden, delta, up, down = first_conv(table, feat, mask, low, high, cot, weight_first, weight_second)
    with jax.named_scope("faces_mid"):
        tops = passed(up, 1)
        bottom = passed(down, -1)
    kept1, sent1 = first_grad(core, cols, delta)
    with jax.named_scope("sum_core"):
        got1 = to_other_core(sent1)
    coarse, kept2, sent2 = second_conv(table, core, hidden, tops[0], cot, mask, weight_second)
    with jax.named_scope("sum_core"):
        got2 = to_other_core(sent2)
    own, *sends = start_sum(place, kept1, got1, kept2, got2)
    orders, groups = ring_orders(leaf_count), rest_groups(leaf_count)
    per = -(-2 * TAPS // leaf_count)
    with jax.named_scope("sum_ring"):
        received = [lax.ppermute(s, both, o) for s, o in zip(sends, orders)]
    input_grad = adjoint_conv(0, L, table, delta, mask, tops[1], bottom, weight_first)
    own, input_grad = lax.optimization_barrier((own, input_grad))
    parts = next_sum(own, received, per * leaf_count).reshape(leaf_count, per * PIECE, C)
    with jax.named_scope("sum_rest"):
        parts = lax.all_to_all(parts, both, 0, 0, axis_index_groups=groups, tiled=True)
    parts = last_sum(parts, 1.0 / math.sqrt(leaf_count * scene_count * L * E**3))
    with jax.named_scope("gather_rest"):
        parts = lax.all_to_all(parts, both, 0, 0, axis_index_groups=groups, tiled=True)
    own = parts.reshape(per * leaf_count, PIECE, C)[: 2 * TAPS]
    with jax.named_scope("gather_ring"):
        mine = [own] + [lax.ppermute(own, both, o) for o in orders]
    with jax.named_scope("gather_core"):
        theirs = [to_other_core(piece) for piece in mine]
    grad_first, grad_second = finish(place, mine + theirs)
    return (
        coarse.reshape(1, L, 4, 4, 4, C),
        input_grad.reshape(1, L, E, E, E, C),
        grad_first,
        grad_second,
    )


def solution(mesh):
    placed = (
        P("scene", "leaf", None, None, None, None),
        P(),
        P(),
        P("scene", "leaf", None, None, None, None),
        P("scene", "leaf", None),
        P("scene", "leaf", None),
    )
    return jax.shard_map(
        shards,
        mesh=mesh,
        in_specs=placed,
        out_specs=(
            P("scene", "leaf", None, None, None, None),
            P("scene", "leaf", None, None, None, None),
            P(),
            P(),
        ),
        check_vma=False,
    )
```

time: 510 us -> 128 us (0.25); the launches traced: 500 us -> 127 us
  waiting for transfers between devices: 283 us -> 3.1 us
  matrix products: 127 us -> 0 us
  blocking collectives: 0 us -> 41.1 us
  Pallas kernels: 0 us -> 37.1 us
  other arithmetic: 34.2 us -> 0.85 us
  starting transfers between devices: 19.2 us -> 35.6 us
  between operations: 15.1 us -> 0.9 us
  local copies, waits for them, and re-layouts: 22.3 us -> 8.68 us
    psum x1 -> x0, waiting for transfers between devices: 239 us -> none  [shards(): lax.psum((grad_first, grad_second), ('leaf', 'scene'))]
    dot_general x104 -> x0, matrix products: 78 us -> none  [the longest x52 56.7 us: route_back(): jnp.einsum('ls,lxyzc->sxyzc', pick, slab_part, precision=lax.Precision.HI...]
    conv_general_dilated x5 -> x0, matrix products: 46 us -> none  [the longest x2 20.7 us: conv_adjoint(): lax.conv_general_dilated(upstream, kernel, (1, 1, 1), [(2, upper)] * 3, l...]
    all_to_all x0 -> x2, blocking collectives: none -> 41.1 us  [shards(): lax.all_to_all(parts, both, 0, 0, axis_index_groups=groups, tiled=True)]
    ppermute x6 -> x16, waiting for transfers between devices: 44.2 us -> 3.1 us  [the longest x6 2.01 us: to_other_core(): lax.ppermute(block, 'scene', [(i, i ^ 1) for i in range(lax.axis_size('sc...]
    pallas_call x0 -> x9, Pallas kernels: none -> 37.1 us  [the longest x1 12.5 us: first_conv(): pl.pallas_call(first_kernel, grid=(L,), out_shape=(jax.ShapeDtypeStruct((...]
    concatenate x4 -> x1, other arithmetic: 20.2 us -> 0.08 us  [local_table(): return jnp.concatenate([found[:, :13], own, found[:, 13:]], axis=1)]
    ppermute x6 -> x16, starting transfers between devices: 19.1 us -> 35.6 us  [the longest x6 15.2 us: to_other_core(): lax.ppermute(block, 'scene', [(i, i ^ 1) for i in range(lax.axis_size('sc...]
  transfers between devices with their start and end apart: 7 -> 16, of which waited for: 4 -> 4; matrix products, arithmetic and copies ran while one was open for 27% -> 1% of each run, Pallas kernels for 0% -> 16%
where the time goes in v2:
time: 128 us; the launch traced here: 127 us
  blocking collectives  41.1 us (32%)
  Pallas kernels  37.1 us (29%)
  starting transfers between devices  35.6 us (28%)
  local copies, waits for them, and re-layouts  8.68 us (7%)
  waiting for transfers between devices  3.1 us (2%)
    all_to_all x2, blocking collectives, shards(): lax.all_to_all(parts, both, 0, 0, axis_index_groups=groups, tiled=True)  41.1 us
    ppermute x6, starting transfers between devices, to_other_core(): lax.ppermute(block, 'scene', [(i, i ^ 1) for i in range(lax.axis_size('sc...  15.2 us
    pallas_call x1, Pallas kernels, first_conv(): pl.pallas_call(first_kernel, grid=(L,), out_shape=(jax.ShapeDtypeStruct((...  12.5 us
    ppermute x4, starting transfers between devices, passed(): lax.ppermute(block, 'leaf', [(i - distance, i) for i in range(count) if 0...  11.2 us
    unnamed x30, local copies, waits for them, and re-layouts  8.57 us
    pallas_call x1, Pallas kernels, adjoint_conv(): pl.pallas_call(kernel, out_shape=jax.ShapeDtypeStruct((count, E, FACE, C)...  8.49 us
    pallas_call x1, Pallas kernels, second_conv(): pl.pallas_call(second_kernel, out_shape=(jax.ShapeDtypeStruct((L, 64, C),...  6.32 us
    ppermute x3, starting transfers between devices, shards(): received = [lax.ppermute(s, both, o) for s, o in zip(sends, orders)]  6.29 us
  transfers between devices with their start and end apart: 16, of which 4 were waited for; matrix products, arithmetic and copies ran while one was open for 1% of the time, Pallas kernels for 16%

profile of v2, /device:TPU:1, one launch (start us, length us, event | category | flops | bytes accessed | tf_op | source)
XLA Modules:
  0.0 127.4 jit_solution(1970332558005480427)
XLA Ops:
  0.6 1.2 copy-done
  1.9 0.9 copy-done.2
  2.8 0.7 copy-done.5
  3.5 1.3 %prepare.1 = (bf16[8,8,64,128]{3,2,1,0:T(8,128)(2,1)S(1)}, bf16[8,64,128]{2,1,0:T(8,128)(2,1)S(1)}, bf16[8,80,128]{2,1,0:T(8,128)(2,1)S(1)}) custom-call(s32[8,512]{1,0:T(8,128)S(1)} %bitcast.36, bf16[8,8,64,128]{3,2,1,0:T(8,128)(2,1)S(1)} %bitcast.25, bf16[8,64,128]{2,1,0:T(8,128)(2,1)S(1)} %bitcast.33), custom_call_target="tpu_custom_call" | custom-call | tf_op jit(solution)/shard_map/prepare/pallas_call | solution.py:137
  4.8 1.3 %collective-permute-start.1 = (bf16[8,80,128]{2,1,0:T(8,128)(2,1)S(1)}, bf16[8,80,128]{2,1,0:T(8,128)(2,1)S(1)}, u32[]{:S(2)}, u32[]{:S(2)}) collective-permute-start(bf16[8,80,128]{2,1,0:T(8,128)(2,1)S(1)} %get-tuple-element.27), channel_id=1, source_target_pairs={{8,0},{16,8},{24,16},{32,24},{40,32},{48,40},{56,48},{64,56},{72,6... | collective-permute-start | bytes 491528 | tf_op jit(solution)/shard_map/faces_in/ppermute | solution.py:554
  6.1 4.6 %collective-permute-start = (bf16[8,64,128]{2,1,0:T(8,128)(2,1)S(1)}, bf16[8,64,128]{2,1,0:T(8,128)(2,1)S(1)}, u32[]{:S(2)}, u32[]{:S(2)}) collective-permute-start(bf16[8,64,128]{2,1,0:T(8,128)(2,1)S(1)} %get-tuple-element.26), channel_id=1, source_target_pairs={{0,8},{8,16},{16,24},{24,32},{32,40},{40,48},{48,56},{56,64},{64,7... | collective-permute-start | bytes 393224 | tf_op jit(solution)/shard_map/faces_in/ppermute | solution.py:554
  10.7 0.7 fusion.1
  11.5 1.1 collective-permute-done.low_in
  12.6 1.2 copy-done.1
  13.8 0.9 copy-done.3
  14.7 1.2 copy-done.9
  15.9 1.2 copy-done.11
  17.1 12.5 %first_conv.1 = (bf16[8,5,64,2304]{3,2,1,0:T(8,128)(2,1)S(1)}, bf16[8,8,64,128]{3,2,1,0:T(8,128)(2,1)S(1)}, bf16[8,8,64,128]{3,2,1,0:T(8,128)(2,1)S(1)}, bf16[2,...) custom-call(s32[8,27]{1,0:T(8,128)S(1)} %pad_add_fusion.table.refs_0_, bf16[8,8,64,128]{3,2,1,0:T(8,128)(2,1)S(1)} %bitcast.26, ...), custom_call_target="tpu_custom_call" | custom-call | flops 15000000512 | bytes 18000000 | tf_op jit(solution)/shard_map/first_conv/pallas_call | solution.py:227
  29.6 4.1 %collective-permute-start.2 = (bf16[2,8,64,128]{3,2,1,0:T(8,128)(2,1)S(1)}, bf16[2,8,64,128]{3,2,1,0:T(8,128)(2,1)S(1)}, u32[]{:S(2)}, u32[]{:S(2)}) collective-permute-start(bf16[2,8,64,128]{3,2,1,0:T(8,128)(2,1)S(1)} %get-tuple-element.29), channel_id=1, source_target_pairs={{0,8},{8,16},{16,24},{24,32},{32,40},{40,48},{48,56},{56,64},{64,7... | collective-permute-start | bytes 786440 | tf_op jit(solution)/shard_map/faces_mid/ppermute | solution.py:554
  33.7 5.0 %first_grad.1 = (f32[27,64,128]{2,1,0:T(8,128)S(1)}, bf16[27,64,128]{2,1,0:T(8,128)(2,1)S(1)}) custom-call(s32[1]{0:T(128)} %bitcast.1.core, bf16[8,5,64,2304]{3,2,1,0:T(8,128)(2,1)S(1)} %get-tuple-element.31.cols, bf16[8,8,64,128]{3,2,1,0:T(8,128)(2,1)S(1)} %get-tuple-element.32.delta.refs_1_), custom_call_target="tpu_custom_call" | custom-call | flops 6000000000 | bytes 14000000 | tf_op jit(solution)/shard_map/first_grad/pallas_call | solution.py:303
  38.7 4.2 %collective-permute-start.3 = (bf16[27,64,128]{2,1,0:T(8,128)(2,1)S(1)}, bf16[27,64,128]{2,1,0:T(8,128)(2,1)S(1)}, u32[]{:S(2)}, u32[]{:S(2)}) collective-permute-start(bf16[27,64,128]{2,1,0:T(8,128)(2,1)S(1)} %get-tuple-element.34), channel_id=1, source_target_pairs={{0,1},{1,0},{2,3},{3,2},{4,5},{5,4},{6,7},{7,6},{8,9},{9,8},{10,11... | collective-permute-start | bytes 1327112 | tf_op jit(solution)/shard_map/sum_core/ppermute | solution.py:558
  42.9 6.3 %second_conv.1 = (bf16[8,64,128]{2,1,0:T(8,128)(2,1)}, f32[27,64,128]{2,1,0:T(8,128)S(1)}, bf16[27,64,128]{2,1,0:T(8,128)(2,1)}) custom-call(s32[8,27]{1,0:T(8,128)S(1)} %pad_add_fusion.table.refs_0_, s32[1]{0:T(128)} %bitcast.1.core, bf16[8,8,64,128]{3,2,1,0:T(8,128)(2,1)S(1)} %get-tuple-element.28.hidden, ...), custom_call_target="tpu_custom_call" | custom-call | flops 8000000000 | bytes 6000000 | tf_op jit(solution)/shard_map/second_conv/pallas_call | solution.py:371
  49.3 1.3 %collective-permute-start.5 = (bf16[8,64,128]{2,1,0:T(8,128)(2,1)S(1)}, bf16[8,64,128]{2,1,0:T(8,128)(2,1)S(1)}, u32[]{:S(2)}, u32[]{:S(2)}) collective-permute-start(bf16[8,64,128]{2,1,0:T(8,128)(2,1)S(1)} %get-tuple-element.38), channel_id=1, source_target_pairs={{8,0},{16,8},{24,16},{32,24},{40,32},{48,40},{56,48},{64,56},{72,6... | collective-permute-start | bytes 393224 | tf_op jit(solution)/shard_map/faces_mid/ppermute | solution.py:554
  50.7 0.6 collective-permute-done.4.got2
  51.3 0.8 start_sum.1
  52.1 1.6 %collective-permute-start.6 = (bf16[54,16,128]{2,1,0:T(8,128)(2,1)S(1)}, bf16[54,16,128]{2,1,0:T(8,128)(2,1)S(1)}, u32[]{:S(2)}, u32[]{:S(2)}) collective-permute-start(bf16[54,16,128]{2,1,0:T(8,128)(2,1)S(1)} %get-tuple-element.41), channel_id=1, source_target_pairs={{0,2},{1,9},{2,4},{3,11},{4,6},{5,13},{6,0},{7,15},{8,10},{9,17},{... | collective-permute-start | bytes 663560 | tf_op jit(solution)/shard_map/sum_ring/ppermute | solution.py:596
  53.7 4.7 %collective-permute-start.7 = (bf16[54,16,128]{2,1,0:T(8,128)(2,1)S(1)}, bf16[54,16,128]{2,1,0:T(8,128)(2,1)S(1)}, u32[]{:S(2)}, u32[]{:S(2)}) collective-permute-start(bf16[54,16,128]{2,1,0:T(8,128)(2,1)S(1)} %get-tuple-element.42), channel_id=1, source_target_pairs={{0,4},{1,17},{2,6},{3,19},{4,0},{5,21},{6,2},{7,23},{8,12},{9,25},... | collective-permute-start | bytes 663560 | tf_op jit(solution)/shard_map/sum_ring/ppermute | solution.py:596
  58.4 1.2 copy-done.14
  59.6 8.5 %first_adjoint.1 = bf16[8,8,64,128]{3,2,1,0:T(8,128)(2,1)} custom-call(s32[8,27]{1,0:T(8,128)S(1)} %pad_add_fusion.table.refs_0_, bf16[8,8,64,128]{3,2,1,0:T(8,128)(2,1)S(1)} %copy-done.14, bf16[8,8,64,128]{3,2,1,0:T(8,128)(2,1)S(1)} %copy-done.8, bf16[8,64,128]{2,1,0:T(8,128)(2,1)S(1)} %get-tuple-element.46.refs_3_, ...), custom_call_target="tpu_custom_call" | custom-call | flops 10000000000 | bytes 6000000 | tf_op jit(solution)/shard_map/first_adjoint/pallas_call | solution.py:423
  68.2 25.9 %all_to_all.10.refs_0_ = bf16[32,32,128]{2,1,0:T(8,128)(2,1)S(1)} all-to-all(bf16[32,32,128]{2,1,0:T(8,128)(2,1)S(1)} %bitcast.27), channel_id=1, replica_groups={{0,8,16,24,32,40,48,56,64,72,80,88,96,104,112,120,128,136,144,152,160,1..., dimensions={0} | all-to-all | bytes 524288 | tf_op jit(solution)/shard_map/sum_rest/all_to_all | solution.py:601
  94.1 15.2 %all_to_all.11 = bf16[32,32,128]{2,1,0:T(8,128)(2,1)S(1)} all-to-all(bf16[32,32,128]{2,1,0:T(8,128)(2,1)S(1)} %last_sum.1), channel_id=1, replica_groups={{0,8,16,24,32,40,48,56,64,72,80,88,96,104,112,120,128,136,144,152,160,1..., dimensions={0} | all-to-all | bytes 524288 | tf_op jit(solution)/shard_map/gather_rest/all_to_all | solution.py:604
  109.5 2.8 %collective-permute-start.10 = (bf16[54,16,128]{2,1,0:T(8,128)(2,1)S(1)}, bf16[54,16,128]{2,1,0:T(8,128)(2,1)S(1)}, u32[]{:S(2)}, u32[]{:S(2)}) collective-permute-start(bf16[54,16,128]{2,1,0:T(8,128)(2,1)S(1)} %bitcast.29), channel_id=1, source_target_pairs={{0,4},{1,17},{2,6},{3,19},{4,0},{5,21},{6,2},{7,23},{8,12},{9,25},... | collective-permute-start | bytes 663560 | tf_op jit(solution)/shard_map/gather_ring/ppermute | solution.py:607
  112.3 6.2 %collective-permute-start.12 = (bf16[54,16,128]{2,1,0:T(8,128)(2,1)S(1)}, bf16[54,16,128]{2,1,0:T(8,128)(2,1)S(1)}, u32[]{:S(2)}, u32[]{:S(2)}) collective-permute-start(bf16[54,16,128]{2,1,0:T(8,128)(2,1)S(1)} %bitcast.31), channel_id=1, source_target_pairs={{0,1},{1,0},{2,3},{3,2},{4,5},{5,4},{6,7},{7,6},{8,9},{9,8},{10,11... | collective-permute-start | bytes 663560 | tf_op jit(solution)/shard_map/gather_core/ppermute | solution.py:558
  118.5 1.6 %collective-permute-start.13 = (bf16[54,16,128]{2,1,0:T(8,128)(2,1)S(1)}, bf16[54,16,128]{2,1,0:T(8,128)(2,1)S(1)}, u32[]{:S(2)}, u32[]{:S(2)}) collective-permute-start(bf16[54,16,128]{2,1,0:T(8,128)(2,1)S(1)} %collective-permute-done.9.refs_1_), channel_id=1, source_target_pairs={{0,1},{1,0},{2,3},{3,2},{4,5},{5,4},{6,7},{7,6},{8,9},{9,8},{10,11... | collective-permute-start | bytes 663560 | tf_op jit(solution)/shard_map/gather_core/ppermute | solution.py:558
  120.1 3.2 %collective-permute-start.14 = (bf16[54,16,128]{2,1,0:T(8,128)(2,1)S(1)}, bf16[54,16,128]{2,1,0:T(8,128)(2,1)S(1)}, u32[]{:S(2)}, u32[]{:S(2)}) collective-permute-start(bf16[54,16,128]{2,1,0:T(8,128)(2,1)S(1)} %collective-permute-done.10.refs_2_), channel_id=1, source_target_pairs={{0,1},{1,0},{2,3},{3,2},{4,5},{5,4},{6,7},{7,6},{8,9},{9,8},{10,11... | collective-permute-start | bytes 663560 | tf_op jit(solution)/shard_map/gather_core/ppermute | solution.py:558
  123.3 1.1 collective-permute-done.14.refs_6_
  124.8 2.6 %finish.1 = (f32[27,128,128]{2,1,0:T(8,128)}, f32[27,128,128]{2,1,0:T(8,128)}) custom-call(s32[3]{0:T(128)S(1)} %pad_add_fusion.1.place, bf16[54,16,128]{2,1,0:T(8,128)(2,1)S(1)} %bitcast.32, bf16[54,16,128]{2,1,0:T(8,128)(2,1)S(1)} %collective-permute-done.9.refs_1_, bf16[54,16,128]{2,1,0:T(8,128)(2,1)S(1)} %collective-permute-done.10.refs_2_, ...), custom_call_target="tpu_custom_call" | custom-call | flops 1000000 | bytes 6000000 | tf_op jit(solution)/shard_map/finish/pallas_call | solution.py:521
  (48 shorter events, 1.0 us)
Async XLA Ops:
  0.6 1.2 copy-start
  1.9 0.9 copy-start.2
  2.8 0.7 copy-start.5
  4.8 24.8 %copy-start.6 = (bf16[8,8,64,128]{3,2,1,0:T(8,128)(2,1)}, bf16[8,8,64,128]{3,2,1,0:T(8,128)(2,1)S(1)}, u32[]{:S(2)}) copy-start(bf16[8,8,64,128]{3,2,1,0:T(8,128)(2,1)S(1)} %get-tuple-element.25.mask.refs_2_) | copy-start | bytes 3145732
  4.8 7.8 %collective-permute-start.1 = (bf16[8,80,128]{2,1,0:T(8,128)(2,1)S(1)}, bf16[8,80,128]{2,1,0:T(8,128)(2,1)S(1)}, u32[]{:S(2)}, u32[]{:S(2)}) collective-permute-start(bf16[8,80,128]{2,1,0:T(8,128)(2,1)S(1)} %get-tuple-element.27), channel_id=1, source_target_pairs={{8,0},{16,8},{24,16},{32,24},{40,32},{48,40},{56,48},{64,56},{72,6... | collective-permute-start | bytes 491528 | tf_op jit(solution)/shard_map/faces_in/ppermute | solution.py:554
  6.1 6.5 %collective-permute-start = (bf16[8,64,128]{2,1,0:T(8,128)(2,1)S(1)}, bf16[8,64,128]{2,1,0:T(8,128)(2,1)S(1)}, u32[]{:S(2)}, u32[]{:S(2)}) collective-permute-start(bf16[8,64,128]{2,1,0:T(8,128)(2,1)S(1)} %get-tuple-element.26), channel_id=1, source_target_pairs={{0,8},{8,16},{16,24},{24,32},{32,40},{40,48},{48,56},{56,64},{64,7... | collective-permute-start | bytes 393224 | tf_op jit(solution)/shard_map/faces_in/ppermute | solution.py:554
  12.6 1.2 copy-start.1
  13.8 0.9 copy-start.3
  14.7 1.2 copy-start.9
  15.9 1.2 copy-start.11
  29.5 9.2 %copy-start.13 = (bf16[8,8,64,128]{3,2,1,0:T(8,128)(2,1)}, bf16[8,8,64,128]{3,2,1,0:T(8,128)(2,1)S(1)}, u32[]{:S(2)}) copy-start(bf16[8,8,64,128]{3,2,1,0:T(8,128)(2,1)S(1)} %get-tuple-element.32.delta.refs_1_) | copy-start | bytes 3145732
  29.6 13.3 %collective-permute-start.2 = (bf16[2,8,64,128]{3,2,1,0:T(8,128)(2,1)S(1)}, bf16[2,8,64,128]{3,2,1,0:T(8,128)(2,1)S(1)}, u32[]{:S(2)}, u32[]{:S(2)}) collective-permute-start(bf16[2,8,64,128]{3,2,1,0:T(8,128)(2,1)S(1)} %get-tuple-element.29), channel_id=1, source_target_pairs={{0,8},{8,16},{16,24},{24,32},{32,40},{40,48},{48,56},{56,64},{64,7... | collective-permute-start | bytes 786440 | tf_op jit(solution)/shard_map/faces_mid/ppermute | solution.py:554
  33.6 9.3 %copy-start.4 = (bf16[1,8,4,4,4,128]{5,4,3,2,1,0:T(4,128)(2,1)S(1)}, bf16[1,8,4,4,4,128]{5,4,3,2,1,0:T(4,128)(2,1)}, u32[]{:S(2)}) copy-start(bf16[1,8,4,4,4,128]{5,4,3,2,1,0:T(4,128)(2,1)} %param.9) | copy-start | bytes 393220
  33.7 9.3 %copy-start.7 = (bf16[8,8,64,128]{3,2,1,0:T(8,128)(2,1)S(1)}, bf16[8,8,64,128]{3,2,1,0:T(8,128)(2,1)}, u32[]{:S(2)}) copy-start(bf16[8,8,64,128]{3,2,1,0:T(8,128)(2,1)} %copy-done.6) | copy-start | bytes 3145732
  33.7 9.3 %copy-start.10 = (bf16[27,128,128]{2,1,0:T(8,128)(2,1)S(1)}, bf16[27,128,128]{2,1,0:T(8,128)(2,1)}, u32[]{:S(2)}) copy-start(bf16[27,128,128]{2,1,0:T(8,128)(2,1)} %w2.3) | copy-start | bytes 2654212
  38.7 12.0 %collective-permute-start.3 = (bf16[27,64,128]{2,1,0:T(8,128)(2,1)S(1)}, bf16[27,64,128]{2,1,0:T(8,128)(2,1)S(1)}, u32[]{:S(2)}, u32[]{:S(2)}) collective-permute-start(bf16[27,64,128]{2,1,0:T(8,128)(2,1)S(1)} %get-tuple-element.34), channel_id=1, source_target_pairs={{0,1},{1,0},{2,3},{3,2},{4,5},{5,4},{6,7},{7,6},{8,9},{9,8},{10,11... | collective-permute-start | bytes 1327112 | tf_op jit(solution)/shard_map/sum_core/ppermute | solution.py:558
  49.3 2.0 %collective-permute-start.4 = (bf16[27,64,128]{2,1,0:T(8,128)(2,1)}, bf16[27,64,128]{2,1,0:T(8,128)(2,1)S(1)}, u32[]{:S(2)}, u32[]{:S(2)}) collective-permute-start(bf16[27,64,128]{2,1,0:T(8,128)(2,1)} %get-tuple-element.36), channel_id=1, source_target_pairs={{0,1},{1,0},{2,3},{3,2},{4,5},{5,4},{6,7},{7,6},{8,9},{9,8},{10,11... | collective-permute-start | bytes 1327112 | tf_op jit(solution)/shard_map/sum_core/ppermute | solution.py:558
  49.3 9.1 %collective-permute-start.5 = (bf16[8,64,128]{2,1,0:T(8,128)(2,1)S(1)}, bf16[8,64,128]{2,1,0:T(8,128)(2,1)S(1)}, u32[]{:S(2)}, u32[]{:S(2)}) collective-permute-start(bf16[8,64,128]{2,1,0:T(8,128)(2,1)S(1)} %get-tuple-element.38), channel_id=1, source_target_pairs={{8,0},{16,8},{24,16},{32,24},{40,32},{48,40},{56,48},{64,56},{72,6... | collective-permute-start | bytes 393224 | tf_op jit(solution)/shard_map/faces_mid/ppermute | solution.py:554
  50.6 7.7 %copy-start.8 = (bf16[8,8,64,128]{3,2,1,0:T(8,128)(2,1)S(1)}, bf16[8,8,64,128]{3,2,1,0:T(8,128)(2,1)}, u32[]{:S(2)}) copy-start(bf16[8,8,64,128]{3,2,1,0:T(8,128)(2,1)} %copy-done.6) | copy-start | bytes 3145732
  50.6 7.7 %copy-start.12 = (bf16[27,128,128]{2,1,0:T(8,128)(2,1)S(1)}, bf16[27,128,128]{2,1,0:T(8,128)(2,1)}, u32[]{:S(2)}) copy-start(bf16[27,128,128]{2,1,0:T(8,128)(2,1)} %refs_5_.1) | copy-start | bytes 2654212
  52.1 16.0 %collective-permute-start.6 = (bf16[54,16,128]{2,1,0:T(8,128)(2,1)S(1)}, bf16[54,16,128]{2,1,0:T(8,128)(2,1)S(1)}, u32[]{:S(2)}, u32[]{:S(2)}) collective-permute-start(bf16[54,16,128]{2,1,0:T(8,128)(2,1)S(1)} %get-tuple-element.41), channel_id=1, source_target_pairs={{0,2},{1,9},{2,4},{3,11},{4,6},{5,13},{6,0},{7,15},{8,10},{9,17},{... | collective-permute-start | bytes 663560 | tf_op jit(solution)/shard_map/sum_ring/ppermute | solution.py:596
  53.7 14.4 %collective-permute-start.7 = (bf16[54,16,128]{2,1,0:T(8,128)(2,1)S(1)}, bf16[54,16,128]{2,1,0:T(8,128)(2,1)S(1)}, u32[]{:S(2)}, u32[]{:S(2)}) collective-permute-start(bf16[54,16,128]{2,1,0:T(8,128)(2,1)S(1)} %get-tuple-element.42), channel_id=1, source_target_pairs={{0,4},{1,17},{2,6},{3,19},{4,0},{5,21},{6,2},{7,23},{8,12},{9,25},... | collective-permute-start | bytes 663560 | tf_op jit(solution)/shard_map/sum_ring/ppermute | solution.py:596
  58.4 9.7 %collective-permute-start.8 = (bf16[54,16,128]{2,1,0:T(8,128)(2,1)S(1)}, bf16[54,16,128]{2,1,0:T(8,128)(2,1)S(1)}, u32[]{:S(2)}, u32[]{:S(2)}) collective-permute-start(bf16[54,16,128]{2,1,0:T(8,128)(2,1)S(1)} %get-tuple-element.43), channel_id=1, source_target_pairs={{0,6},{1,25},{2,0},{3,27},{4,2},{5,29},{6,4},{7,31},{8,14},{9,1},{... | collective-permute-start | bytes 663560 | tf_op jit(solution)/shard_map/sum_ring/ppermute | solution.py:596
  58.4 1.2 copy-start.14
  109.4 9.1 %collective-permute-start.9 = (bf16[54,16,128]{2,1,0:T(8,128)(2,1)S(1)}, bf16[54,16,128]{2,1,0:T(8,128)(2,1)S(1)}, u32[]{:S(2)}, u32[]{:S(2)}) collective-permute-start(bf16[54,16,128]{2,1,0:T(8,128)(2,1)S(1)} %bitcast.28), channel_id=1, source_target_pairs={{0,2},{1,9},{2,4},{3,11},{4,6},{5,13},{6,0},{7,15},{8,10},{9,17},{... | collective-permute-start | bytes 663560 | tf_op jit(solution)/shard_map/gather_ring/ppermute | solution.py:607
  109.5 10.6 %collective-permute-start.10 = (bf16[54,16,128]{2,1,0:T(8,128)(2,1)S(1)}, bf16[54,16,128]{2,1,0:T(8,128)(2,1)S(1)}, u32[]{:S(2)}, u32[]{:S(2)}) collective-permute-start(bf16[54,16,128]{2,1,0:T(8,128)(2,1)S(1)} %bitcast.29), channel_id=1, source_target_pairs={{0,4},{1,17},{2,6},{3,19},{4,0},{5,21},{6,2},{7,23},{8,12},{9,25},... | collective-permute-start | bytes 663560 | tf_op jit(solution)/shard_map/gather_ring/ppermute | solution.py:607
  112.3 11.1 %collective-permute-start.11 = (bf16[54,16,128]{2,1,0:T(8,128)(2,1)S(1)}, bf16[54,16,128]{2,1,0:T(8,128)(2,1)S(1)}, u32[]{:S(2)}, u32[]{:S(2)}) collective-permute-start(bf16[54,16,128]{2,1,0:T(8,128)(2,1)S(1)} %bitcast.30), channel_id=1, source_target_pairs={{0,6},{1,25},{2,0},{3,27},{4,2},{5,29},{6,4},{7,31},{8,14},{9,1},{... | collective-permute-start | bytes 663560 | tf_op jit(solution)/shard_map/gather_ring/ppermute | solution.py:607
  112.3 11.1 %collective-permute-start.12 = (bf16[54,16,128]{2,1,0:T(8,128)(2,1)S(1)}, bf16[54,16,128]{2,1,0:T(8,128)(2,1)S(1)}, u32[]{:S(2)}, u32[]{:S(2)}) collective-permute-start(bf16[54,16,128]{2,1,0:T(8,128)(2,1)S(1)} %bitcast.31), channel_id=1, source_target_pairs={{0,1},{1,0},{2,3},{3,2},{4,5},{5,4},{6,7},{7,6},{8,9},{9,8},{10,11... | collective-permute-start | bytes 663560 | tf_op jit(solution)/shard_map/gather_core/ppermute | solution.py:558
  118.5 4.8 %collective-permute-start.13 = (bf16[54,16,128]{2,1,0:T(8,128)(2,1)S(1)}, bf16[54,16,128]{2,1,0:T(8,128)(2,1)S(1)}, u32[]{:S(2)}, u32[]{:S(2)}) collective-permute-start(bf16[54,16,128]{2,1,0:T(8,128)(2,1)S(1)} %collective-permute-done.9.refs_1_), channel_id=1, source_target_pairs={{0,1},{1,0},{2,3},{3,2},{4,5},{5,4},{6,7},{7,6},{8,9},{9,8},{10,11... | collective-permute-start | bytes 663560 | tf_op jit(solution)/shard_map/gather_core/ppermute | solution.py:558
  120.1 4.3 %collective-permute-start.14 = (bf16[54,16,128]{2,1,0:T(8,128)(2,1)S(1)}, bf16[54,16,128]{2,1,0:T(8,128)(2,1)S(1)}, u32[]{:S(2)}, u32[]{:S(2)}) collective-permute-start(bf16[54,16,128]{2,1,0:T(8,128)(2,1)S(1)} %collective-permute-done.10.refs_2_), channel_id=1, source_target_pairs={{0,1},{1,0},{2,3},{3,2},{4,5},{5,4},{6,7},{7,6},{8,9},{9,8},{10,11... | collective-permute-start | bytes 663560 | tf_op jit(solution)/shard_map/gather_core/ppermute | solution.py:558
  123.3 1.5 %collective-permute-start.15 = (bf16[54,16,128]{2,1,0:T(8,128)(2,1)S(1)}, bf16[54,16,128]{2,1,0:T(8,128)(2,1)S(1)}, u32[]{:S(2)}, u32[]{:S(2)}) collective-permute-start(bf16[54,16,128]{2,1,0:T(8,128)(2,1)S(1)} %collective-permute-done.11.refs_3_), channel_id=1, source_target_pairs={{0,1},{1,0},{2,3},{3,2},{4,5},{5,4},{6,7},{7,6},{8,9},{9,8},{10,11... | collective-permute-start | bytes 663560 | tf_op jit(solution)/shard_map/gather_core/ppermute | solution.py:558

commit v3 on v2

--- a/solution.py
+++ b/solution.py
@@ -16,7 +16,16 @@
 SPAN = 9 * C
 TAPS = 27
 HALF = C // 2
+PER = 2
 PIECE = 16
+
+
+def core_at():
+    return lax.axis_index("scene") & 1
+
+
+def ring_at():
+    return jnp.where(core_at() == 0, lax.axis_index("scene") >> 1, lax.axis_index("leaf") & 3)
 
 
 def smem():
@@ -40,16 +49,21 @@
 
 
 def source_plane(x, top):
-    if isinstance(x, int):
-        a = 0 if x == 0 else 18 if x == top + 1 else 9
-        return a, top - 1 if x == 0 else 0 if x == top + 1 else x - 1
-    first, last = x == 0, x == top + 1
-    return jnp.where(first, 0, jnp.where(last, 18, 9)), jnp.where(first, top - 1, jnp.where(last, 0, x - 1))
+    return -1 if x == 0 else 1 if x == top + 1 else 0, top - 1 if x == 0 else 0 if x == top + 1 else x - 1
+
+
+def block_at(neighbours, leaf, a, b, c):
+    d = 9 * a + 3 * b + c
+    if d == 0:
+        return leaf
+    n = neighbours[leaf, 13 + d if d < 0 else 12 + d]
+    return jnp.where(n < 0, L, n & (L - 1))
 
 
 def shifted_lines(table, lines, low, high, leaf, x, top, rows):
     a, i = source_plane(x, top)
-    at = [[table[leaf, a + 3 * b + c] for c in range(3)] for b in range(3)]
+    ends = (-1, 0, 1)
+    at = [[block_at(table, leaf, a, b, c) if (c < 0 and low is not None) or c == 0 or (c > 0 and high is not None) else None for c in ends] for b in ends]
     ids = lax.broadcasted_iota(jnp.int32, (E, C), 0)
     out = ([], [], [])
     for y in rows:
@@ -117,116 +131,145 @@
     return jnp.concatenate([ref[leaf, 2 * pair + half] for pair in range(4)], axis=0)
 
 
-def prepare_kernel(voxels, feat, cot, mask, up, down, spread, held, coarse):
-    @pl.loop(0, L)
-    def _(leaf):
-        row = jnp.broadcast_to(voxels[pl.ds(leaf, 1), :].astype(f32), (C, E**3))
-        whole = row.T
+def spread_mask(voxels, leaf):
+    return jnp.broadcast_to(voxels[leaf : leaf + 1, :].astype(f32), (C, E**3)).T
+
+
+def faces_kernel(voxels, feat, cot, up, down, spread, held, coarse):
+    for leaf in range(L):
+        whole = spread_mask(voxels, leaf)
         spread[...] = whole
-        mask[leaf] = whole.reshape(E, FACE, C).astype(bf16)
-        held[...] = feat[leaf].reshape(E**3, C).astype(f32) * whole
-        up[leaf] = held[pl.ds(E - 1, FACE, stride=E), :].astype(bf16)
-        down[leaf, 0:FACE] = held[pl.ds(0, FACE, stride=E), :].astype(bf16)
         coarse[...] = cot[leaf].astype(f32)
         edge = coarse[pl.ds(0, 16, stride=4), :]
         active = jnp.concatenate([spread[pl.ds(2 * FACE * i, 4, stride=16), :] for i in range(4)], axis=0)
         down[leaf, FACE : FACE + 16] = (edge * active).astype(bf16)
-
-
-def prepare(voxels, feat, cot):
-    return pl.pallas_call(
-        prepare_kernel,
+        held[...] = feat[leaf].reshape(E**3, C).astype(f32) * whole
+        up[leaf] = held[pl.ds(E - 1, FACE, stride=E), :].astype(bf16)
+        down[leaf, 0:FACE] = held[pl.ds(0, FACE, stride=E), :].astype(bf16)
+
+
+def first_faces(voxels, feat, cot):
+    return pl.pallas_call(
+        faces_kernel,
         out_shape=(
-            jax.ShapeDtypeStruct((L, E, FACE, C), bf16),
             jax.ShapeDtypeStruct((L, FACE, C), bf16),
             jax.ShapeDtypeStruct((L, FACE + 16, C), bf16),
         ),
         in_specs=[vmem()] * 3,
-        out_specs=(vmem(),) * 3,
+        out_specs=(vmem(),) * 2,
         scratch_shapes=[pltpu.VMEM((E**3, C), f32), pltpu.VMEM((E**3, C), f32), pltpu.VMEM((64, C), f32)],
-        compiler_params=params(16),
-        name="prepare",
+        compiler_params=params(12),
+        cost_estimate=cost(6e9, 8e6),
+        name="first_faces",
     )(voxels, feat, cot)
 
 
+def setup_kernel(voxels, feat, cot, w1, w2, mask, lines, clines, wa, wb, wc, spread, coarse):
+    lines[L] = jnp.zeros((E, FACE, C), f32)
+    clines[...] = jnp.zeros((L + 1, 4, FACE, C), f32)
+    for leaf in range(L):
+        whole = spread_mask(voxels, leaf)
+        spread[...] = whole
+        mask[leaf] = whole.reshape(E, FACE, C).astype(bf16)
+        lines[leaf] = feat[leaf].astype(f32) * whole.reshape(E, FACE, C)
+        coarse[...] = cot[leaf].astype(f32)
+        for i in range(4):
+            for j in range(4):
+                clines[leaf, i, pl.ds(16 * j, 4, stride=2), :] = coarse[16 * i + 4 * j : 16 * i + 4 * j + 4]
+            clines[leaf, i] = clines[leaf, i] * spread[2 * FACE * i : 2 * FACE * i + FACE]
+    banded(w1, wa, wb)
+    for n, p in enumerate((1, 2, 0)):
+        for t in range(9):
+            wc[n * C : n * C + C, t * C : t * C + C] = w2[9 * p + 8 - t]
+
+
+def setup(voxels, feat, cot, w1, w2):
+    return pl.pallas_call(
+        setup_kernel,
+        out_shape=(
+            jax.ShapeDtypeStruct((L, E, FACE, C), bf16),
+            jax.ShapeDtypeStruct((L + 1, E, FACE, C), f32),
+            jax.ShapeDtypeStruct((L + 1, 4, FACE, C), f32),
+            jax.ShapeDtypeStruct((2 * SPAN, 2 * C), bf16),
+            jax.ShapeDtypeStruct((2 * SPAN, 2 * C), bf16),
+            jax.ShapeDtypeStruct((3 * C, SPAN), bf16),
+        ),
+        in_specs=[vmem()] * 5,
+        out_specs=(vmem(),) * 6,
+        scratch_shapes=[pltpu.VMEM((E**3, C), f32), pltpu.VMEM((64, C), f32)],
+        compiler_params=params(14),
+        cost_estimate=cost(1e9, 8e6),
+        name="setup",
+    )(voxels, feat, cot, w1, w2)
+
+
 def first_kernel(
-    table, feat, mask, low_in, high_in, cot, w1, w2,
+    table, lines, clines, mask, low_in, high_in, wa, wb, wc,
     cols, hidden, delta, up, down,
-    lines, low, high, clines, chigh, ccols, coarse, wa, wb, wc, faces,
+    low, high, chigh, ccols, coarse, faces,
 ):
     step = pl.program_id(0)
 
     @pl.when(step == 0)
     def _():
-        lines[L] = jnp.zeros((E, FACE, C), f32)
         low[L] = jnp.zeros((E, E, C), f32)
         high[L] = jnp.zeros((E, E, C), f32)
-        clines[L] = jnp.zeros((4, FACE, C), f32)
         chigh[...] = jnp.zeros((L + 1, 4, E, C), f32)
 
         @pl.loop(0, L)
         def _(leaf):
-            lines[leaf] = feat[leaf].astype(f32) * mask[leaf].astype(f32)
             low[leaf] = low_in[leaf].astype(f32).reshape(E, E, C)
             high[leaf] = high_in[leaf, 0:FACE].astype(f32).reshape(E, E, C)
-            coarse[0:16] = high_in[leaf, FACE : FACE + 16].astype(f32)
+            coarse[...] = high_in[leaf, FACE : FACE + 16].astype(f32)
             for i in range(4):
                 chigh[leaf, i, pl.ds(0, 4, stride=2), :] = coarse[4 * i : 4 * i + 4]
-            coarse[...] = cot[leaf].astype(f32)
-            clines[leaf] = jnp.zeros((4, FACE, C), f32)
-            for i in range(4):
-                for j in range(4):
-                    clines[leaf, i, pl.ds(16 * j, 4, stride=2), :] = coarse[16 * i + 4 * j : 16 * i + 4 * j + 4]
-                clines[leaf, i] = clines[leaf, i] * mask[leaf, 2 * i].astype(f32)
-
-        banded(w1, wa, wb)
-        for n, p in enumerate((1, 2, 0)):
-            for t in range(9):
-                wc[n * C : n * C + C, t * C : t * C + C] = w2[9 * p + 8 - t]
-
-    for pair in range(5):
+
+    for n in range(PER):
+        leaf = PER * step + n
+        for pair in range(5):
+            for half in range(2):
+                def store(at, value, n=n, pair=pair, half=half):
+                    cols[n, pair, :, half * SPAN + at : half * SPAN + at + C] = value
+                fill_plane(store, table, lines, low, high, leaf, 2 * pair + half, E)
+
+            def store_coarse(at, value, n=n, pair=pair):
+                ccols[n, pair, :, at : at + C] = value
+            fill_plane(store_coarse, table, clines, None, chigh, leaf, pair + 1, 4)
+
+        pre = pairs_dot(dot, cols, n, wa, wb)
+        back = dot_turned(ccols[n, 0:4].reshape(4 * FACE, SPAN), wc[: 2 * C])
+        back_next = dot_turned(ccols[n, 1:5].reshape(4 * FACE, SPAN), wc[2 * C :])
+        sig = 1.0 / (1.0 + jnp.exp(-pre))
+        slope = sig * (1.0 + pre * (1.0 - sig))
         for half in range(2):
-            def store(at, value, pair=pair, half=half):
-                cols[0, pair, :, half * SPAN + at : half * SPAN + at + C] = value
-            fill_plane(store, table, lines, low, high, step, 2 * pair + half, E)
-
-        def store_coarse(at, value, pair=pair):
-            ccols[pair, :, at : at + C] = value
-        fill_plane(store_coarse, table, clines, None, chigh, step, pair + 1, 4)
-
-    pre = pairs_dot(dot, cols, 0, wa, wb)
-    back = dot_turned(ccols[0:4].reshape(4 * FACE, SPAN), wc[: 2 * C])
-    back_next = dot_turned(ccols[1:5].reshape(4 * FACE, SPAN), wc[2 * C :])
-    sig = 1.0 / (1.0 + jnp.exp(-pre))
-    slope = sig * (1.0 + pre * (1.0 - sig))
-    for half in range(2):
-        at = slice(half * C, half * C + C)
-        m = half_planes(mask, step, half).astype(f32)
-        h = m * pre[:, at] * sig[:, at]
-        g = back[:, at] if half == 0 else back[:, at] + back_next
-        d = g * m * slope[:, at]
-        for pair in range(4):
-            rows = slice(FACE * pair, FACE * pair + FACE)
-            hidden[0, 2 * pair + half] = h[rows].astype(bf16)
-            delta[0, 2 * pair + half] = d[rows].astype(bf16)
-            faces[0, 2 * pair + half] = h[rows]
-            faces[1, 2 * pair + half] = d[rows]
-    for i in range(0, E, 2):
-        def face(which, k, i=i):
-            return jnp.concatenate([faces[which, i + n, pl.ds(k, E, stride=E), :] for n in range(2)], axis=0).astype(bf16)
-        rows = slice(E * i, E * i + 2 * E)
-        up[0, 0, rows] = face(0, E - 1)
-        up[1, 0, rows] = face(1, E - 1)
-        down[0, rows] = face(1, 0)
-
-
-def first_conv(table, feat, mask, low, high, cot, w1, w2):
+            at = slice(half * C, half * C + C)
+            m = half_planes(mask, leaf, half).astype(f32)
+            h = m * pre[:, at] * sig[:, at]
+            g = back[:, at] if half == 0 else back[:, at] + back_next
+            d = g * m * slope[:, at]
+            for pair in range(4):
+                rows = slice(FACE * pair, FACE * pair + FACE)
+                hidden[n, 2 * pair + half] = h[rows].astype(bf16)
+                delta[n, 2 * pair + half] = d[rows].astype(bf16)
+                faces[n, 0, 2 * pair + half] = h[rows]
+                faces[n, 1, 2 * pair + half] = d[rows]
+        for i in range(0, E, 2):
+            def face(which, k, i=i, n=n):
+                pair = [faces[n, which, i + m, pl.ds(k, E, stride=E), :] for m in range(2)]
+                return jnp.concatenate(pair, axis=0).astype(bf16)
+            rows = slice(E * i, E * i + 2 * E)
+            up[0, n, rows] = face(0, E - 1)
+            up[1, n, rows] = face(1, E - 1)
+            down[n, rows] = face(1, 0)
+
+
+def first_conv(table, lines, clines, mask, low, high, filters):
     def leafwise(*shape):
-        return pl.BlockSpec((1, *shape), lambda s: (s,) + (0,) * len(shape))
+        return pl.BlockSpec((PER, *shape), lambda s: (s,) + (0,) * len(shape))
 
     return pl.pallas_call(
         first_kernel,
-        grid=(L,),
+        grid=(L // PER,),
         out_shape=(
             jax.ShapeDtypeStruct((L, 5, FACE, 2 * SPAN), bf16),
             jax.ShapeDtypeStruct((L, E, FACE, C), bf16),
@@ -234,31 +277,26 @@
             jax.ShapeDtypeStruct((2, L, FACE, C), bf16),
             jax.ShapeDtypeStruct((L, FACE, C), bf16),
         ),
-        in_specs=[smem()] + [vmem()] * 7,
+        in_specs=[smem()] + [vmem()] * 8,
         out_specs=(
             leafwise(5, FACE, 2 * SPAN),
             leafwise(E, FACE, C),
             leafwise(E, FACE, C),
-            pl.BlockSpec((2, 1, FACE, C), lambda s: (0, s, 0, 0)),
+            pl.BlockSpec((2, PER, FACE, C), lambda s: (0, s, 0, 0)),
             leafwise(FACE, C),
         ),
         scratch_shapes=[
-            pltpu.VMEM((L + 1, E, FACE, C), f32),
             pltpu.VMEM((L + 1, E, E, C), f32),
             pltpu.VMEM((L + 1, E, E, C), f32),
-            pltpu.VMEM((L + 1, 4, FACE, C), f32),
             pltpu.VMEM((L + 1, 4, E, C), f32),
-            pltpu.VMEM((5, FACE, SPAN), bf16),
-            pltpu.VMEM((64, C), f32),
-            pltpu.VMEM((2 * SPAN, 2 * C), bf16),
-            pltpu.VMEM((2 * SPAN, 2 * C), bf16),
-            pltpu.VMEM((3 * C, SPAN), bf16),
-            pltpu.VMEM((2, E, FACE, C), f32),
+            pltpu.VMEM((PER, 5, FACE, SPAN), bf16),
+            pltpu.VMEM((16, C), f32),
+            pltpu.VMEM((PER, 2, E, FACE, C), f32),
         ],
-        compiler_params=params(28),
+        compiler_params=params(24),
         cost_estimate=cost(15e9, 18e6),
         name="first_conv",
-    )(table, feat, mask, low, high, cot, w1, w2)
+    )(table, lines, clines, mask, low, high, *filters)
 
 
 def split_halves(core, whole, kept, sent):
@@ -269,7 +307,7 @@
         sent[t] = whole[t, pl.ds(theirs, HALF), :].astype(bf16)
 
 
-def first_grad_kernel(core, cols, delta, kept, sent, turned, total, whole):
+def first_grad_kernel(cols, delta, kept, sent, turned, total, whole):
     @pl.loop(0, L)
     def _(leaf):
         for half in range(2):
@@ -292,18 +330,18 @@
     for p in range(3):
         for t in range(9):
             whole[9 * p + t] = total[p, :, t * C : t * C + C].T
-    split_halves(core[0], whole, kept, sent)
+    split_halves(core_at(), whole, kept, sent)
 
 
 def halves_shape():
     return jax.ShapeDtypeStruct((TAPS, HALF, C), f32), jax.ShapeDtypeStruct((TAPS, HALF, C), bf16)
 
 
-def first_grad(core, cols, delta):
+def first_grad(cols, delta):
     return pl.pallas_call(
         first_grad_kernel,
         out_shape=halves_shape(),
-        in_specs=[smem(), vmem(), vmem()],
+        in_specs=[vmem(), vmem()],
         out_specs=(vmem(), vmem()),
         scratch_shapes=[
             pltpu.VMEM((2 * C, L * 256), bf16),
@@ -313,11 +351,11 @@
         compiler_params=params(16),
         cost_estimate=cost(6e9, 14e6),
         name="first_grad",
-    )(core, cols, delta)
+    )(cols, delta)
 
 
 def second_kernel(
-    table, core, hidden, low_in, cot, mask, w2,
+    table, hidden, low_in, cot, mask, w2,
     coarse, kept, sent,
     lines, low, cols, turned, total, whole, thin,
 ):
@@ -364,14 +402,14 @@
         total[:, 2 * SPAN + 256 * tile : 2 * SPAN + end] = jnp.dot(turned[...], rhs, preferred_element_type=f32)
     for t in range(TAPS):
         whole[t] = total[:, t * C : t * C + C].T
-    split_halves(core[0], whole, kept, sent)
-
-
-def second_conv(table, core, hidden, low, cot, mask, w2):
+    split_halves(core_at(), whole, kept, sent)
+
+
+def second_conv(table, hidden, low, cot, mask, w2):
     return pl.pallas_call(
         second_kernel,
         out_shape=(jax.ShapeDtypeStruct((L, 64, C), bf16), *halves_shape()),
-        in_specs=[smem()] * 2 + [vmem()] * 5,
+        in_specs=[smem()] + [vmem()] * 5,
         out_specs=(vmem(),) * 3,
         scratch_shapes=[
             pltpu.VMEM((L + 1, E, FACE, C), f32),
@@ -382,10 +420,10 @@
             pltpu.VMEM((TAPS, C, C), f32),
             pltpu.VMEM((2, 2 * FACE, C), f32),
         ],
-        compiler_params=params(40),
+        compiler_params=params(20),
         cost_estimate=cost(8e9, 6e6),
         name="second_conv",
-    )(table, core, hidden, low, cot, mask, w2)
+    )(table, hidden, low, cot, mask, w2)
 
 
 def adjoint_kernel(start, count, table, delta, mask, low_in, high_in, w, out, lines, low, high, cols, wa, wb):
@@ -401,19 +439,21 @@
 
     banded_turned(w, wa, wb)
 
-    @pl.loop(0, count)
-    def _(n):
-        for pair in range(5):
+    @pl.loop(0, count // PER)
+    def _(step):
+        for n in range(PER):
+            leaf = start + PER * step + n
+            for pair in range(5):
+                for half in range(2):
+                    def store(at, value, n=n, pair=pair, half=half):
+                        cols[n, pair, :, half * SPAN + at : half * SPAN + at + C] = value
+                    fill_plane(store, table, lines, low, high, leaf, 2 * pair + half, E)
+            res = pairs_dot(dot_turned, cols, n, wa, wb)
             for half in range(2):
-                def store(at, value, pair=pair, half=half):
-                    cols[0, pair, :, half * SPAN + at : half * SPAN + at + C] = value
-                fill_plane(store, table, lines, low, high, start + n, 2 * pair + half, E)
-        res = pairs_dot(dot_turned, cols, 0, wa, wb)
-        for half in range(2):
-            m = half_planes(mask, start + n, half).astype(f32)
-            value = (res[:, half * C : half * C + C] * m).astype(bf16)
-            for pair in range(4):
-                out[n, 2 * pair + half] = value[FACE * pair : FACE * pair + FACE]
+                m = half_planes(mask, leaf, half).astype(f32)
+                value = (res[:, half * C : half * C + C] * m).astype(bf16)
+                for pair in range(4):
+                    out[PER * step + n, 2 * pair + half] = value[FACE * pair : FACE * pair + FACE]
 
 
 def adjoint_conv(start, count, table, delta, mask, low, high, w):
@@ -429,18 +469,18 @@
             pltpu.VMEM((L + 1, E, FACE, C), f32),
             pltpu.VMEM((L + 1, E, E, C), f32),
             pltpu.VMEM((L + 1, E, E, C), f32),
-            pltpu.VMEM((1, 5, FACE, 2 * SPAN), bf16),
+            pltpu.VMEM((PER, 5, FACE, 2 * SPAN), bf16),
             pltpu.VMEM((2 * C, 2 * SPAN), bf16),
             pltpu.VMEM((2 * C, 2 * SPAN), bf16),
         ],
-        compiler_params=params(32),
+        compiler_params=params(16),
         cost_estimate=cost(10e9 * count / L, 6e6),
         name="first_adjoint",
     )(table, delta, mask, low, high, w)
 
 
-def start_sum_kernel(place, kept1, got1, kept2, got2, own, *sends):
-    mine = place[0]
+def start_sum_kernel(kept1, got1, kept2, got2, own, *sends):
+    mine = ring_at()
     for d in range(4):
         rows = pl.ds(pl.multiple_of(((mine + d) % 4) * PIECE, PIECE), PIECE)
         for t in range(2 * TAPS):
@@ -452,16 +492,16 @@
                 sends[d - 1][t] = value.astype(bf16)
 
 
-def start_sum(place, kept1, got1, kept2, got2):
+def start_sum(kept1, got1, kept2, got2):
     return pl.pallas_call(
         start_sum_kernel,
         out_shape=(jax.ShapeDtypeStruct((2 * TAPS, PIECE, C), f32),) + (jax.ShapeDtypeStruct((2 * TAPS, PIECE, C), bf16),) * 3,
-        in_specs=[smem()] + [vmem()] * 4,
+        in_specs=[vmem()] * 4,
         out_specs=(vmem(),) * 4,
         compiler_params=params(12),
         cost_estimate=cost(1e6, 3e6),
         name="start_sum",
-    )(place, kept1, got1, kept2, got2)
+    )(kept1, got1, kept2, got2)
 
 
 def next_sum_kernel(own, a, b, c, out):
@@ -506,27 +546,29 @@
     )(parts)
 
 
-def finish_kernel(place, *refs):
+def finish_kernel(*refs):
     mine, theirs, (first, second) = refs[0:4], refs[4:8], refs[8:10]
-
-    for d in range(4):
-        for parts, core, at in ((mine, place[2], place[0]), (theirs, 1 - place[2], place[1])):
-            row = pl.multiple_of(core * HALF + ((at - d + 4) % 4) * PIECE, PIECE)
+    at_y, at_x = lax.axis_index("scene") >> 1, lax.axis_index("leaf") & 3
+    core = core_at()
+    for parts, which in ((mine, core), (theirs, 1 - core)):
+        at = jnp.where(which == 0, at_y, at_x)
+        for d in range(4):
+            row = pl.multiple_of(which * HALF + ((at - d) & 3) * PIECE, PIECE)
             for t in range(2 * TAPS):
                 out, n = (first, t) if t < TAPS else (second, t - TAPS)
                 out[n, pl.ds(row, PIECE), :] = parts[d][t].astype(f32)
 
 
-def finish(place, pieces):
+def finish(pieces):
     return pl.pallas_call(
         finish_kernel,
         out_shape=(jax.ShapeDtypeStruct((TAPS, C, C), f32),) * 2,
-        in_specs=[smem()] + [vmem()] * 8,
+        in_specs=[vmem()] * 8,
         out_specs=(vmem(),) * 2,
         compiler_params=params(12),
         cost_estimate=cost(1e6, 6e6),
         name="finish",
-    )(place, *pieces)
+    )(*pieces)
 
 
 def ring_orders(leaf_count):
@@ -558,44 +600,36 @@
     return lax.ppermute(block, "scene", [(i, i ^ 1) for i in range(lax.axis_size("scene"))])
 
 
-def local_table(neighbours):
-    found = jnp.where(neighbours >= 0, neighbours % L, L)
-    own = jnp.arange(L, dtype=jnp.int32)[:, None]
-    return jnp.concatenate([found[:, :13], own, found[:, 13:]], axis=1)
-
-
 def shards(features, weight_first, weight_second, cotangent, neighbours, voxel_mask):
     both = ("leaf", "scene")
     leaf_count, scene_count = lax.axis_size("leaf"), lax.axis_size("scene")
-    leaf_at, scene_at = lax.axis_index("leaf"), lax.axis_index("scene")
-    core, x_at, y_at = scene_at % 2, leaf_at % 4, scene_at // 2
-    place = jnp.stack([jnp.where(core == 0, y_at, x_at), jnp.where(core == 0, x_at, y_at), core]).astype(jnp.int32)
-    core = place[2:3]
     feat = features[0].reshape(L, E, FACE, C)
     cot = cotangent[0].reshape(L, 64, C)
-    table = local_table(neighbours[0])
-
-    mask, up, down = prepare(voxel_mask[0], feat, cot)
+    table = neighbours[0]
+    voxels = voxel_mask[0]
+
+    up, down = first_faces(voxels, feat, cot)
     with jax.named_scope("faces_in"):
         low = passed(up, 1)
         high = passed(down, -1)
-    cols, hidden, delta, up, down = first_conv(table, feat, mask, low, high, cot, weight_first, weight_second)
+    voxels, _ = lax.optimization_barrier((voxels, down))
+    mask, lines, clines, *filters = setup(voxels, feat, cot, weight_first, weight_second)
+    cols, hidden, delta, up, down = first_conv(table, lines, clines, mask, low, high, filters)
     with jax.named_scope("faces_mid"):
         tops = passed(up, 1)
         bottom = passed(down, -1)
-    kept1, sent1 = first_grad(core, cols, delta)
+        tops, bottom = lax.optimization_barrier((tops, bottom))
+    kept1, sent1 = first_grad(cols, delta)
     with jax.named_scope("sum_core"):
         got1 = to_other_core(sent1)
-    coarse, kept2, sent2 = second_conv(table, core, hidden, tops[0], cot, mask, weight_second)
+    coarse, kept2, sent2 = second_conv(table, hidden, tops[0], cot, mask, weight_second)
     with jax.named_scope("sum_core"):
         got2 = to_other_core(sent2)
-    own, *sends = start_sum(place, kept1, got1, kept2, got2)
+    own, *sends = start_sum(kept1, got1, kept2, got2)
     orders, groups = ring_orders(leaf_count), rest_groups(leaf_count)
     per = -(-2 * TAPS // leaf_count)
     with jax.named_scope("sum_ring"):
         received = [lax.ppermute(s, both, o) for s, o in zip(sends, orders)]
-    input_grad = adjoint_conv(0, L, table, delta, mask, tops[1], bottom, weight_first)
-    own, input_grad = lax.optimization_barrier((own, input_grad))
     parts = next_sum(own, received, per * leaf_count).reshape(leaf_count, per * PIECE, C)
     with jax.named_scope("sum_rest"):
         parts = lax.all_to_all(parts, both, 0, 0, axis_index_groups=groups, tiled=True)
@@ -604,10 +638,15 @@
         parts = lax.all_to_all(parts, both, 0, 0, axis_index_groups=groups, tiled=True)
     own = parts.reshape(per * leaf_count, PIECE, C)[: 2 * TAPS]
     with jax.named_scope("gather_ring"):
-        mine = [own] + [lax.ppermute(own, both, o) for o in orders]
+        received = [lax.ppermute(own, both, o) for o in orders]
     with jax.named_scope("gather_core"):
-        theirs = [to_other_core(piece) for piece in mine]
-    grad_first, grad_second = finish(place, mine + theirs)
+        theirs = [to_other_core(own)]
+    delta, own = lax.optimization_barrier((delta, own))
+    input_grad = adjoint_conv(0, L, table, delta, mask, tops[1], bottom, weight_first)
+    input_grad, received = lax.optimization_barrier((input_grad, received))
+    with jax.named_scope("gather_core"):
+        theirs += [to_other_core(piece) for piece in received]
+    grad_first, grad_second = finish([own, *received, *theirs])
     return (
         coarse.reshape(1, L, 4, 4, 4, C),
         input_grad.reshape(1, L, E, E, E, C),

time: 128 us -> 119 us (0.930)
  waiting for transfers between devices: 3.1 us -> 9.59 us
  starting transfers between devices: 35.6 us -> 29.4 us
  local copies, waits for them, and re-layouts: 8.68 us -> 2.9 us
  Pallas kernels: 37.1 us -> 33.7 us
  blocking collectives: 41.1 us -> 42.4 us
    ppermute x6, starting transfers between devices: 15.2 us -> 9.09 us  [to_other_core(): lax.ppermute(block, 'scene', [(i, i ^ 1) for i in range(lax.axis_size('sc...]
    unnamed x30 -> x18, local copies, waits for them, and re-layouts: 8.57 us -> 2.86 us
    ppermute x3, waiting for transfers between devices: 0.01 us -> 5.69 us  [shards(): received = [lax.ppermute(s, both, o) for s, o in zip(sends, orders)]]
    all_to_all x2, blocking collectives: 41.1 us -> 42.4 us  [shards(): lax.all_to_all(parts, both, 0, 0, axis_index_groups=groups, tiled=True)]
    pallas_call x3 -> x4, Pallas kernels: 18.8 us -> 17.5 us  [the longest x1 10.5 us: first_conv(): pl.pallas_call(first_kernel, grid=(L // PER,), out_shape=(jax.ShapeDtypeS...]
  transfers between devices with their start and end apart: 16 -> 16, of which waited for: 4 -> 7; matrix products, arithmetic and copies ran while one was open for 1% -> 0% of each run, Pallas kernels for 16% -> 17%
where the time goes in v3:
time: 119 us
  blocking collectives  42.4 us (36%)
  Pallas kernels  33.7 us (28%)
  starting transfers between devices  29.4 us (25%)
  waiting for transfers between devices  9.59 us (8%)
  local copies, waits for them, and re-layouts  2.9 us (2%)
    all_to_all x2, blocking collectives, shards(): lax.all_to_all(parts, both, 0, 0, axis_index_groups=groups, tiled=True)  42.4 us
    ppermute x4, starting transfers between devices, passed(): lax.ppermute(block, 'leaf', [(i - distance, i) for i in range(count) if 0...  12 us
    pallas_call x1, Pallas kernels, first_conv(): pl.pallas_call(first_kernel, grid=(L // PER,), out_shape=(jax.ShapeDtypeS...  10.5 us
    ppermute x6, starting transfers between devices, to_other_core(): lax.ppermute(block, 'scene', [(i, i ^ 1) for i in range(lax.axis_size('sc...  9.09 us
    pallas_call x1, Pallas kernels, adjoint_conv(): pl.pallas_call(kernel, out_shape=jax.ShapeDtypeStruct((count, E, FACE, C)...  7.95 us
    ppermute x3, starting transfers between devices, shards(): received = [lax.ppermute(s, both, o) for s, o in zip(sends, orders)]  6.38 us
    pallas_call x1, Pallas kernels, second_conv(): pl.pallas_call(second_kernel, out_shape=(jax.ShapeDtypeStruct((L, 64, C),...  5.76 us
    ppermute x3, waiting for transfers between devices, shards(): received = [lax.ppermute(s, both, o) for s, o in zip(sends, orders)]  5.69 us
  transfers between devices with their start and end apart: 16, of which 7 were waited for; matrix products, arithmetic and copies ran while one was open for 0% of the time, Pallas kernels for 17%

profile of v3, /device:TPU:1, one launch (start us, length us, event | category | flops | bytes accessed | tf_op | source)
XLA Modules:
  0.0 118.8 jit_solution(4114500596398150166)
XLA Ops:
  0.6 1.2 %copy-done = bf16[1,8,8,8,8,128]{5,4,3,2,1,0:T(8,128)(2,1)S(1)} copy-done((bf16[1,8,8,8,8,128]{5,4,3,2,1,0:T(8,128)(2,1)S(1)}, bf16[1,8,8,8,8,128]{5,4,3,2,1,0:T(8,128)(2,1)}, u32[]{:S(2)}) %copy-start) | copy-done | bytes 1048600
  1.9 0.9 copy-done.4
  2.8 0.7 copy-done.6
  3.5 0.7 first_faces.1
  4.2 1.4 %collective-permute-start.1 = (bf16[8,80,128]{2,1,0:T(8,128)(2,1)S(1)}, bf16[8,80,128]{2,1,0:T(8,128)(2,1)S(1)}, u32[]{:S(2)}, u32[]{:S(2)}) collective-permute-start(bf16[8,80,128]{2,1,0:T(8,128)(2,1)S(1)} %get-tuple-element.37), channel_id=1, source_target_pairs={{8,0},{16,8},{24,16},{32,24},{40,32},{48,40},{56,48},{64,56},{72,6... | collective-permute-start | bytes 491528 | tf_op jit(solution)/shard_map/faces_in/ppermute | solution.py:596
  5.6 4.6 %collective-permute-start = (bf16[8,64,128]{2,1,0:T(8,128)(2,1)S(1)}, bf16[8,64,128]{2,1,0:T(8,128)(2,1)S(1)}, u32[]{:S(2)}, u32[]{:S(2)}) collective-permute-start(bf16[8,64,128]{2,1,0:T(8,128)(2,1)S(1)} %get-tuple-element.42), channel_id=1, source_target_pairs={{0,8},{8,16},{16,24},{24,32},{32,40},{40,48},{48,56},{56,64},{64,7... | collective-permute-start | bytes 393224 | tf_op jit(solution)/shard_map/faces_in/ppermute | solution.py:596
  10.3 1.0 setup.1
  11.3 0.8 collective-permute-done.low_in
  12.2 10.5 %first_conv.1 = (bf16[8,5,64,2304]{3,2,1,0:T(8,128)(2,1)S(1)}, bf16[8,8,64,128]{3,2,1,0:T(8,128)(2,1)S(1)}, bf16[8,8,64,128]{3,2,1,0:T(8,128)(2,1)S(1)}, bf16[2,...) custom-call(s32[8,26]{1,0:T(8,128)S(1)} %bitcast.25, f32[9,8,64,128]{3,2,1,0:T(8,128)S(1)} %get-tuple-element.39.lines, ...), custom_call_target="tpu_custom_call" | custom-call | flops 15000000512 | bytes 18000000 | tf_op jit(solution)/shard_map/first_conv/pallas_call | solution.py:270
  22.7 1.3 %collective-permute-start.3 = (bf16[8,64,128]{2,1,0:T(8,128)(2,1)S(1)}, bf16[8,64,128]{2,1,0:T(8,128)(2,1)S(1)}, u32[]{:S(2)}, u32[]{:S(2)}) collective-permute-start(bf16[8,64,128]{2,1,0:T(8,128)(2,1)S(1)} %get-tuple-element.48), channel_id=1, source_target_pairs={{8,0},{16,8},{24,16},{32,24},{40,32},{48,40},{56,48},{64,56},{72,6... | collective-permute-start | bytes 393224 | tf_op jit(solution)/shard_map/faces_mid/ppermute | solution.py:596
  24.0 4.7 %collective-permute-start.2 = (bf16[2,8,64,128]{3,2,1,0:T(8,128)(2,1)S(1)}, bf16[2,8,64,128]{3,2,1,0:T(8,128)(2,1)S(1)}, u32[]{:S(2)}, u32[]{:S(2)}) collective-permute-start(bf16[2,8,64,128]{3,2,1,0:T(8,128)(2,1)S(1)} %get-tuple-element.47), channel_id=1, source_target_pairs={{0,8},{8,16},{16,24},{24,32},{32,40},{40,48},{48,56},{56,64},{64,7... | collective-permute-start | bytes 786440 | tf_op jit(solution)/shard_map/faces_mid/ppermute | solution.py:596
  28.7 5.3 %first_grad.1 = (f32[27,64,128]{2,1,0:T(8,128)S(1)}, bf16[27,64,128]{2,1,0:T(8,128)(2,1)S(1)}) custom-call(bf16[8,5,64,2304]{3,2,1,0:T(8,128)(2,1)S(1)} %get-tuple-element.52.cols, bf16[8,8,64,128]{3,2,1,0:T(8,128)(2,1)S(1)} %get-tuple-element.61.delta.refs_1_), custom_call_target="tpu_custom_call" | custom-call | flops 6000000000 | bytes 14000000 | tf_op jit(solution)/shard_map/first_grad/pallas_call | solution.py:341
  34.0 4.1 %collective-permute-start.4 = (bf16[27,64,128]{2,1,0:T(8,128)(2,1)S(1)}, bf16[27,64,128]{2,1,0:T(8,128)(2,1)S(1)}, u32[]{:S(2)}, u32[]{:S(2)}) collective-permute-start(bf16[27,64,128]{2,1,0:T(8,128)(2,1)S(1)} %get-tuple-element.54), channel_id=1, source_target_pairs={{0,1},{1,0},{2,3},{3,2},{4,5},{5,4},{6,7},{7,6},{8,9},{9,8},{10,11... | collective-permute-start | bytes 1327112 | tf_op jit(solution)/shard_map/sum_core/ppermute | solution.py:600
  38.2 5.8 %second_conv.1 = (bf16[8,64,128]{2,1,0:T(8,128)(2,1)}, f32[27,64,128]{2,1,0:T(8,128)S(1)}, bf16[27,64,128]{2,1,0:T(8,128)(2,1)S(1)}) custom-call(s32[8,26]{1,0:T(8,128)S(1)} %bitcast.26, bf16[8,8,64,128]{3,2,1,0:T(8,128)(2,1)S(1)} %get-tuple-element.46.hidden, bf16[8,64,128]{2,1,0:T(8,128)(2,1)S(1)} %get-tuple-element.71.low_in, ...), custom_call_target="tpu_custom_call" | custom-call | flops 8000000000 | bytes 6000000 | tf_op jit(solution)/shard_map/second_conv/pallas_call | solution.py:409
  44.0 1.8 %collective-permute-done.5.got2 = bf16[27,64,128]{2,1,0:T(8,128)(2,1)S(1)} collective-permute-done((bf16[27,64,128]{2,1,0:T(8,128)(2,1)S(1)}, bf16[27,64,128]{2,1,0:T(8,128)(2,1)S(1)}, u32[]{:S(2)}, u32[]{:S(2)}) %collective-permute-start.5) | collective-permute-done | bytes 442400 | tf_op jit(solution)/shard_map/sum_core/ppermute | solution.py:600
  45.8 0.2 start_sum.1
  46.1 2.0 %collective-permute-start.6 = (bf16[54,16,128]{2,1,0:T(8,128)(2,1)S(1)}, bf16[54,16,128]{2,1,0:T(8,128)(2,1)S(1)}, u32[]{:S(2)}, u32[]{:S(2)}) collective-permute-start(bf16[54,16,128]{2,1,0:T(8,128)(2,1)S(1)} %get-tuple-element.58), channel_id=1, source_target_pairs={{0,2},{1,9},{2,4},{3,11},{4,6},{5,13},{6,0},{7,15},{8,10},{9,17},{... | collective-permute-start | bytes 663560 | tf_op jit(solution)/shard_map/sum_ring/ppermute | solution.py:632
  48.0 4.4 %collective-permute-start.7 = (bf16[54,16,128]{2,1,0:T(8,128)(2,1)S(1)}, bf16[54,16,128]{2,1,0:T(8,128)(2,1)S(1)}, u32[]{:S(2)}, u32[]{:S(2)}) collective-permute-start(bf16[54,16,128]{2,1,0:T(8,128)(2,1)S(1)} %get-tuple-element.59), channel_id=1, source_target_pairs={{0,4},{1,17},{2,6},{3,19},{4,0},{5,21},{6,2},{7,23},{8,12},{9,25},... | collective-permute-start | bytes 663560 | tf_op jit(solution)/shard_map/sum_ring/ppermute | solution.py:632
  52.4 2.4 %collective-permute-done.6.a = bf16[54,16,128]{2,1,0:T(8,128)(2,1)S(1)} collective-permute-done((bf16[54,16,128]{2,1,0:T(8,128)(2,1)S(1)}, bf16[54,16,128]{2,1,0:T(8,128)(2,1)S(1)}, u32[]{:S(2)}, u32[]{:S(2)}) %collective-permute-start.6) | collective-permute-done | bytes 221216 | tf_op jit(solution)/shard_map/sum_ring/ppermute | solution.py:632
  54.9 3.3 %collective-permute-done.7.b = bf16[54,16,128]{2,1,0:T(8,128)(2,1)S(1)} collective-permute-done((bf16[54,16,128]{2,1,0:T(8,128)(2,1)S(1)}, bf16[54,16,128]{2,1,0:T(8,128)(2,1)S(1)}, u32[]{:S(2)}, u32[]{:S(2)}) %collective-permute-start.7) | collective-permute-done | bytes 221216 | tf_op jit(solution)/shard_map/sum_ring/ppermute | solution.py:632
  58.2 27.5 %all_to_all.10.refs_0_ = bf16[32,32,128]{2,1,0:T(8,128)(2,1)S(1)} all-to-all(bf16[32,32,128]{2,1,0:T(8,128)(2,1)S(1)} %bitcast.12), channel_id=1, replica_groups={{0,8,16,24,32,40,48,56,64,72,80,88,96,104,112,120,128,136,144,152,160,1..., dimensions={0} | all-to-all | bytes 524288 | tf_op jit(solution)/shard_map/sum_rest/all_to_all | solution.py:635
  85.8 14.9 %all_to_all.11 = bf16[32,32,128]{2,1,0:T(8,128)(2,1)S(1)} all-to-all(bf16[32,32,128]{2,1,0:T(8,128)(2,1)S(1)} %last_sum.1), channel_id=1, replica_groups={{0,8,16,24,32,40,48,56,64,72,80,88,96,104,112,120,128,136,144,152,160,1..., dimensions={0} | all-to-all | bytes 524288 | tf_op jit(solution)/shard_map/gather_rest/all_to_all | solution.py:638
  100.7 1.7 %collective-permute-start.12 = (bf16[54,16,128]{2,1,0:T(8,128)(2,1)S(1)}, bf16[54,16,128]{2,1,0:T(8,128)(2,1)S(1)}, u32[]{:S(2)}, u32[]{:S(2)}) collective-permute-start(bf16[54,16,128]{2,1,0:T(8,128)(2,1)S(1)} %bitcast.13), channel_id=1, source_target_pairs={{0,1},{1,0},{2,3},{3,2},{4,5},{5,4},{6,7},{7,6},{8,9},{9,8},{10,11... | collective-permute-start | bytes 663560 | tf_op jit(solution)/shard_map/gather_core/ppermute | solution.py:600
  102.4 1.0 collective-permute-start.11
  103.5 0.9 collective-permute-start.9
  104.3 7.9 %first_adjoint.1 = bf16[8,8,64,128]{3,2,1,0:T(8,128)(2,1)} custom-call(s32[8,26]{1,0:T(8,128)S(1)} %bitcast.27, bf16[8,8,64,128]{3,2,1,0:T(8,128)(2,1)S(1)} %get-tuple-element.61.delta.refs_1_, bf16[8,8,64,128]{3,2,1,0:T(8,128)(2,1)S(1)} %get-tuple-element.41.mask.refs_2_, bf16[8,64,128]{2,1,0:T(8,128)(2,1)S(1)} %get-tuple-element.70.refs_3_, ...), custom_call_target="tpu_custom_call" | custom-call | flops 10000000000 | bytes 6000000 | tf_op jit(solution)/shard_map/first_adjoint/pallas_call | solution.py:463
  112.3 2.7 %collective-permute-start.13 = (bf16[54,16,128]{2,1,0:T(8,128)(2,1)S(1)}, bf16[54,16,128]{2,1,0:T(8,128)(2,1)S(1)}, u32[]{:S(2)}, u32[]{:S(2)}) collective-permute-start(bf16[54,16,128]{2,1,0:T(8,128)(2,1)S(1)} %collective-permute-done.9.refs_1_), channel_id=1, source_target_pairs={{0,1},{1,0},{2,3},{3,2},{4,5},{5,4},{6,7},{7,6},{8,9},{9,8},{10,11... | collective-permute-start | bytes 663560 | tf_op jit(solution)/shard_map/gather_core/ppermute | solution.py:600
  115.0 0.5 collective-permute-start.15
  115.5 0.6 collective-permute-done.13.refs_5_
  116.1 0.4 collective-permute-done.14.refs_6_
  116.4 0.3 collective-permute-done.15.refs_7_
  116.8 2.0 %finish.1 = (f32[27,128,128]{2,1,0:T(8,128)}, f32[27,128,128]{2,1,0:T(8,128)}) custom-call(bf16[54,16,128]{2,1,0:T(8,128)(2,1)S(1)} %bitcast.17, bf16[54,16,128]{2,1,0:T(8,128)(2,1)S(1)} %collective-permute-done.9.refs_1_, bf16[54,16,128]{2,1,0:T(8,128)(2,1)S(1)} %collective-permute-done.10.refs_2_, ...), custom_call_target="tpu_custom_call" | custom-call | flops 1000000 | bytes 6000000 | tf_op jit(solution)/shard_map/finish/pallas_call | solution.py:563
  (32 shorter events, 0.5 us)
Async XLA Ops:
  0.6 1.2 %copy-start = (bf16[1,8,8,8,8,128]{5,4,3,2,1,0:T(8,128)(2,1)S(1)}, bf16[1,8,8,8,8,128]{5,4,3,2,1,0:T(8,128)(2,1)}, u32[]{:S(2)}) copy-start(bf16[1,8,8,8,8,128]{5,4,3,2,1,0:T(8,128)(2,1)} %param.6) | copy-start | bytes 3145732
  1.9 0.9 copy-start.4
  2.8 0.7 copy-start.6
  3.5 6.8 %copy-start.1 = (bf16[1,8,8,8,8,128]{5,4,3,2,1,0:T(8,128)(2,1)S(1)}, bf16[1,8,8,8,8,128]{5,4,3,2,1,0:T(8,128)(2,1)}, u32[]{:S(2)}) copy-start(bf16[1,8,8,8,8,128]{5,4,3,2,1,0:T(8,128)(2,1)} %param.6) | copy-start | bytes 3145732
  3.5 6.8 %copy-start.2 = (bf16[27,128,128]{2,1,0:T(8,128)(2,1)S(1)}, bf16[27,128,128]{2,1,0:T(8,128)(2,1)}, u32[]{:S(2)}) copy-start(bf16[27,128,128]{2,1,0:T(8,128)(2,1)} %w2.3) | copy-start | bytes 2654212
  3.5 6.8 %copy-start.3 = (bf16[27,128,128]{2,1,0:T(8,128)(2,1)S(1)}, bf16[27,128,128]{2,1,0:T(8,128)(2,1)}, u32[]{:S(2)}) copy-start(bf16[27,128,128]{2,1,0:T(8,128)(2,1)} %refs_5_.1) | copy-start | bytes 2654212
  3.5 6.8 %copy-start.5 = (bf16[1,8,4,4,4,128]{5,4,3,2,1,0:T(4,128)(2,1)S(1)}, bf16[1,8,4,4,4,128]{5,4,3,2,1,0:T(4,128)(2,1)}, u32[]{:S(2)}) copy-start(bf16[1,8,4,4,4,128]{5,4,3,2,1,0:T(4,128)(2,1)} %param.9) | copy-start | bytes 393220
  3.5 6.8 %copy-start.7 = (s32[1,8,512]{2,1,0:T(8,128)S(1)}, s32[1,8,512]{2,1,0:T(8,128)}, u32[]{:S(2)}) copy-start(s32[1,8,512]{2,1,0:T(8,128)} %param.11) | copy-start | bytes 49156
  4.2 8.0 %collective-permute-start.1 = (bf16[8,80,128]{2,1,0:T(8,128)(2,1)S(1)}, bf16[8,80,128]{2,1,0:T(8,128)(2,1)S(1)}, u32[]{:S(2)}, u32[]{:S(2)}) collective-permute-start(bf16[8,80,128]{2,1,0:T(8,128)(2,1)S(1)} %get-tuple-element.37), channel_id=1, source_target_pairs={{8,0},{16,8},{24,16},{32,24},{40,32},{48,40},{56,48},{64,56},{72,6... | collective-permute-start | bytes 491528 | tf_op jit(solution)/shard_map/faces_in/ppermute | solution.py:596
  5.6 6.5 %copy-start.8 = (s32[1,8,26]{2,1,0:T(8,128)S(1)}, s32[1,8,26]{2,1,0:T(8,128)}, u32[]{:S(2)}) copy-start(s32[1,8,26]{2,1,0:T(8,128)} %param.10) | copy-start | bytes 2500
  5.6 6.5 %collective-permute-start = (bf16[8,64,128]{2,1,0:T(8,128)(2,1)S(1)}, bf16[8,64,128]{2,1,0:T(8,128)(2,1)S(1)}, u32[]{:S(2)}, u32[]{:S(2)}) collective-permute-start(bf16[8,64,128]{2,1,0:T(8,128)(2,1)S(1)} %get-tuple-element.42), channel_id=1, source_target_pairs={{0,8},{8,16},{16,24},{24,32},{32,40},{40,48},{48,56},{56,64},{64,7... | collective-permute-start | bytes 393224 | tf_op jit(solution)/shard_map/faces_in/ppermute | solution.py:596
  22.7 15.4 %collective-permute-start.3 = (bf16[8,64,128]{2,1,0:T(8,128)(2,1)S(1)}, bf16[8,64,128]{2,1,0:T(8,128)(2,1)S(1)}, u32[]{:S(2)}, u32[]{:S(2)}) collective-permute-start(bf16[8,64,128]{2,1,0:T(8,128)(2,1)S(1)} %get-tuple-element.48), channel_id=1, source_target_pairs={{8,0},{16,8},{24,16},{32,24},{40,32},{48,40},{56,48},{64,56},{72,6... | collective-permute-start | bytes 393224 | tf_op jit(solution)/shard_map/faces_mid/ppermute | solution.py:596
  24.0 14.1 %collective-permute-start.2 = (bf16[2,8,64,128]{3,2,1,0:T(8,128)(2,1)S(1)}, bf16[2,8,64,128]{3,2,1,0:T(8,128)(2,1)S(1)}, u32[]{:S(2)}, u32[]{:S(2)}) collective-permute-start(bf16[2,8,64,128]{3,2,1,0:T(8,128)(2,1)S(1)} %get-tuple-element.47), channel_id=1, source_target_pairs={{0,8},{8,16},{16,24},{24,32},{32,40},{40,48},{48,56},{56,64},{64,7... | collective-permute-start | bytes 786440 | tf_op jit(solution)/shard_map/faces_mid/ppermute | solution.py:596
  34.0 10.1 %collective-permute-start.4 = (bf16[27,64,128]{2,1,0:T(8,128)(2,1)S(1)}, bf16[27,64,128]{2,1,0:T(8,128)(2,1)S(1)}, u32[]{:S(2)}, u32[]{:S(2)}) collective-permute-start(bf16[27,64,128]{2,1,0:T(8,128)(2,1)S(1)} %get-tuple-element.54), channel_id=1, source_target_pairs={{0,1},{1,0},{2,3},{3,2},{4,5},{5,4},{6,7},{7,6},{8,9},{9,8},{10,11... | collective-permute-start | bytes 1327112 | tf_op jit(solution)/shard_map/sum_core/ppermute | solution.py:600
  43.9 1.9 %collective-permute-start.5 = (bf16[27,64,128]{2,1,0:T(8,128)(2,1)S(1)}, bf16[27,64,128]{2,1,0:T(8,128)(2,1)S(1)}, u32[]{:S(2)}, u32[]{:S(2)}) collective-permute-start(bf16[27,64,128]{2,1,0:T(8,128)(2,1)S(1)} %get-tuple-element.56), channel_id=1, source_target_pairs={{0,1},{1,0},{2,3},{3,2},{4,5},{5,4},{6,7},{7,6},{8,9},{9,8},{10,11... | collective-permute-start | bytes 1327112 | tf_op jit(solution)/shard_map/sum_core/ppermute | solution.py:600
  46.1 8.8 %collective-permute-start.6 = (bf16[54,16,128]{2,1,0:T(8,128)(2,1)S(1)}, bf16[54,16,128]{2,1,0:T(8,128)(2,1)S(1)}, u32[]{:S(2)}, u32[]{:S(2)}) collective-permute-start(bf16[54,16,128]{2,1,0:T(8,128)(2,1)S(1)} %get-tuple-element.58), channel_id=1, source_target_pairs={{0,2},{1,9},{2,4},{3,11},{4,6},{5,13},{6,0},{7,15},{8,10},{9,17},{... | collective-permute-start | bytes 663560 | tf_op jit(solution)/shard_map/sum_ring/ppermute | solution.py:632
  48.0 10.1 %collective-permute-start.7 = (bf16[54,16,128]{2,1,0:T(8,128)(2,1)S(1)}, bf16[54,16,128]{2,1,0:T(8,128)(2,1)S(1)}, u32[]{:S(2)}, u32[]{:S(2)}) collective-permute-start(bf16[54,16,128]{2,1,0:T(8,128)(2,1)S(1)} %get-tuple-element.59), channel_id=1, source_target_pairs={{0,4},{1,17},{2,6},{3,19},{4,0},{5,21},{6,2},{7,23},{8,12},{9,25},... | collective-permute-start | bytes 663560 | tf_op jit(solution)/shard_map/sum_ring/ppermute | solution.py:632
  52.4 5.7 %collective-permute-start.8 = (bf16[54,16,128]{2,1,0:T(8,128)(2,1)S(1)}, bf16[54,16,128]{2,1,0:T(8,128)(2,1)S(1)}, u32[]{:S(2)}, u32[]{:S(2)}) collective-permute-start(bf16[54,16,128]{2,1,0:T(8,128)(2,1)S(1)} %get-tuple-element.60), channel_id=1, source_target_pairs={{0,6},{1,25},{2,0},{3,27},{4,2},{5,29},{6,4},{7,31},{8,14},{9,1},{... | collective-permute-start | bytes 663560 | tf_op jit(solution)/shard_map/sum_ring/ppermute | solution.py:632
  100.7 14.8 %collective-permute-start.12 = (bf16[54,16,128]{2,1,0:T(8,128)(2,1)S(1)}, bf16[54,16,128]{2,1,0:T(8,128)(2,1)S(1)}, u32[]{:S(2)}, u32[]{:S(2)}) collective-permute-start(bf16[54,16,128]{2,1,0:T(8,128)(2,1)S(1)} %bitcast.13), channel_id=1, source_target_pairs={{0,1},{1,0},{2,3},{3,2},{4,5},{5,4},{6,7},{7,6},{8,9},{9,8},{10,11... | collective-permute-start | bytes 663560 | tf_op jit(solution)/shard_map/gather_core/ppermute | solution.py:600
  102.4 9.9 %collective-permute-start.11 = (bf16[54,16,128]{2,1,0:T(8,128)(2,1)S(1)}, bf16[54,16,128]{2,1,0:T(8,128)(2,1)S(1)}, u32[]{:S(2)}, u32[]{:S(2)}) collective-permute-start(bf16[54,16,128]{2,1,0:T(8,128)(2,1)S(1)} %bitcast.14), channel_id=1, source_target_pairs={{0,6},{1,25},{2,0},{3,27},{4,2},{5,29},{6,4},{7,31},{8,14},{9,1},{... | collective-permute-start | bytes 663560 | tf_op jit(solution)/shard_map/gather_ring/ppermute | solution.py:641
  103.3 9.0 %collective-permute-start.10 = (bf16[54,16,128]{2,1,0:T(8,128)(2,1)S(1)}, bf16[54,16,128]{2,1,0:T(8,128)(2,1)S(1)}, u32[]{:S(2)}, u32[]{:S(2)}) collective-permute-start(bf16[54,16,128]{2,1,0:T(8,128)(2,1)S(1)} %bitcast.15), channel_id=1, source_target_pairs={{0,4},{1,17},{2,6},{3,19},{4,0},{5,21},{6,2},{7,23},{8,12},{9,25},... | collective-permute-start | bytes 663560 | tf_op jit(solution)/shard_map/gather_ring/ppermute | solution.py:641
  103.5 8.8 %collective-permute-start.9 = (bf16[54,16,128]{2,1,0:T(8,128)(2,1)S(1)}, bf16[54,16,128]{2,1,0:T(8,128)(2,1)S(1)}, u32[]{:S(2)}, u32[]{:S(2)}) collective-permute-start(bf16[54,16,128]{2,1,0:T(8,128)(2,1)S(1)} %bitcast.16), channel_id=1, source_target_pairs={{0,2},{1,9},{2,4},{3,11},{4,6},{5,13},{6,0},{7,15},{8,10},{9,17},{... | collective-permute-start | bytes 663560 | tf_op jit(solution)/shard_map/gather_ring/ppermute | solution.py:641
  112.3 3.8 %collective-permute-start.13 = (bf16[54,16,128]{2,1,0:T(8,128)(2,1)S(1)}, bf16[54,16,128]{2,1,0:T(8,128)(2,1)S(1)}, u32[]{:S(2)}, u32[]{:S(2)}) collective-permute-start(bf16[54,16,128]{2,1,0:T(8,128)(2,1)S(1)} %collective-permute-done.9.refs_1_), channel_id=1, source_target_pairs={{0,1},{1,0},{2,3},{3,2},{4,5},{5,4},{6,7},{7,6},{8,9},{9,8},{10,11... | collective-permute-start | bytes 663560 | tf_op jit(solution)/shard_map/gather_core/ppermute | solution.py:600
  115.0 1.5 %collective-permute-start.14 = (bf16[54,16,128]{2,1,0:T(8,128)(2,1)S(1)}, bf16[54,16,128]{2,1,0:T(8,128)(2,1)S(1)}, u32[]{:S(2)}, u32[]{:S(2)}) collective-permute-start(bf16[54,16,128]{2,1,0:T(8,128)(2,1)S(1)} %collective-permute-done.10.refs_2_), channel_id=1, source_target_pairs={{0,1},{1,0},{2,3},{3,2},{4,5},{5,4},{6,7},{7,6},{8,9},{9,8},{10,11... | collective-permute-start | bytes 663560 | tf_op jit(solution)/shard_map/gather_core/ppermute | solution.py:600
  115.0 1.8 %collective-permute-start.15 = (bf16[54,16,128]{2,1,0:T(8,128)(2,1)S(1)}, bf16[54,16,128]{2,1,0:T(8,128)(2,1)S(1)}, u32[]{:S(2)}, u32[]{:S(2)}) collective-permute-start(bf16[54,16,128]{2,1,0:T(8,128)(2,1)S(1)} %collective-permute-done.11.refs_3_), channel_id=1, source_target_pairs={{0,1},{1,0},{2,3},{3,2},{4,5},{5,4},{6,7},{7,6},{8,9},{9,8},{10,11... | collective-permute-start | bytes 663560 | tf_op jit(solution)/shard_map/gather_core/ppermute | solution.py:600

commit v4 on v3

--- a/solution.py
+++ b/solution.py
@@ -16,12 +16,19 @@
 SPAN = 9 * C
 TAPS = 27
 HALF = C // 2
-PER = 2
 PIECE = 16
 
 
 def core_at():
     return lax.axis_index("scene") & 1
+
+
+def by_parity(body):
+    odd = lax.axis_index("leaf") & 1
+    for parity in range(2):
+        @pl.when(odd == parity)
+        def _(parity=parity):
+            body(1 - parity, parity)
 
 
 def ring_at():
@@ -135,26 +142,31 @@
     return jnp.broadcast_to(voxels[leaf : leaf + 1, :].astype(f32), (C, E**3)).T
 
 
-def faces_kernel(voxels, feat, cot, up, down, spread, held, coarse):
+def faces_kernel(voxels, feat, cot, one, two, spread, held, coarse):
     for leaf in range(L):
         whole = spread_mask(voxels, leaf)
         spread[...] = whole
         coarse[...] = cot[leaf].astype(f32)
         edge = coarse[pl.ds(0, 16, stride=4), :]
         active = jnp.concatenate([spread[pl.ds(2 * FACE * i, 4, stride=16), :] for i in range(4)], axis=0)
-        down[leaf, FACE : FACE + 16] = (edge * active).astype(bf16)
         held[...] = feat[leaf].reshape(E**3, C).astype(f32) * whole
-        up[leaf] = held[pl.ds(E - 1, FACE, stride=E), :].astype(bf16)
-        down[leaf, 0:FACE] = held[pl.ds(0, FACE, stride=E), :].astype(bf16)
+        up = held[pl.ds(E - 1, FACE, stride=E), :].astype(bf16)
+        down = held[pl.ds(0, FACE, stride=E), :].astype(bf16)
+
+        def write(below, above, leaf=leaf, up=up, down=down, edge=edge, active=active):
+            out = (one, two)
+            out[above][leaf, 0:FACE] = up
+            out[above][leaf, FACE : FACE + 16] = jnp.zeros((16, C), bf16)
+            out[below][leaf, 0:FACE] = down
+            out[below][leaf, FACE : FACE + 16] = (edge * active).astype(bf16)
+
+        by_parity(write)
 
 
 def first_faces(voxels, feat, cot):
     return pl.pallas_call(
         faces_kernel,
-        out_shape=(
-            jax.ShapeDtypeStruct((L, FACE, C), bf16),
-            jax.ShapeDtypeStruct((L, FACE + 16, C), bf16),
-        ),
+        out_shape=(jax.ShapeDtypeStruct((L, FACE + 16, C), bf16),) * 2,
         in_specs=[vmem()] * 3,
         out_specs=(vmem(),) * 2,
         scratch_shapes=[pltpu.VMEM((E**3, C), f32), pltpu.VMEM((E**3, C), f32), pltpu.VMEM((64, C), f32)],
@@ -204,28 +216,27 @@
 
 
 def first_kernel(
-    table, lines, clines, mask, low_in, high_in, wa, wb, wc,
-    cols, hidden, delta, up, down,
+    table, lines, clines, mask, one_in, two_in, wa, wb, wc,
+    cols, hidden, delta, one, two,
     low, high, chigh, ccols, coarse, faces,
 ):
-    step = pl.program_id(0)
-
-    @pl.when(step == 0)
-    def _():
-        low[L] = jnp.zeros((E, E, C), f32)
-        high[L] = jnp.zeros((E, E, C), f32)
-        chigh[...] = jnp.zeros((L + 1, 4, E, C), f32)
-
-        @pl.loop(0, L)
-        def _(leaf):
-            low[leaf] = low_in[leaf].astype(f32).reshape(E, E, C)
+    low[L] = jnp.zeros((E, E, C), f32)
+    high[L] = jnp.zeros((E, E, C), f32)
+    chigh[...] = jnp.zeros((L + 1, 4, E, C), f32)
+
+    def receive(below, above):
+        low_in, high_in = (one_in, two_in)[below], (one_in, two_in)[above]
+        for leaf in range(L):
+            low[leaf] = low_in[leaf, 0:FACE].astype(f32).reshape(E, E, C)
             high[leaf] = high_in[leaf, 0:FACE].astype(f32).reshape(E, E, C)
             coarse[...] = high_in[leaf, FACE : FACE + 16].astype(f32)
             for i in range(4):
                 chigh[leaf, i, pl.ds(0, 4, stride=2), :] = coarse[4 * i : 4 * i + 4]
 
-    for n in range(PER):
-        leaf = PER * step + n
+    by_parity(receive)
+
+    for n in range(L):
+        leaf = n
         for pair in range(5):
             for half in range(2):
                 def store(at, value, n=n, pair=pair, half=half):
@@ -253,50 +264,47 @@
                 delta[n, 2 * pair + half] = d[rows].astype(bf16)
                 faces[n, 0, 2 * pair + half] = h[rows]
                 faces[n, 1, 2 * pair + half] = d[rows]
-        for i in range(0, E, 2):
-            def face(which, k, i=i, n=n):
-                pair = [faces[n, which, i + m, pl.ds(k, E, stride=E), :] for m in range(2)]
-                return jnp.concatenate(pair, axis=0).astype(bf16)
-            rows = slice(E * i, E * i + 2 * E)
-            up[0, n, rows] = face(0, E - 1)
-            up[1, n, rows] = face(1, E - 1)
-            down[n, rows] = face(1, 0)
-
-
-def first_conv(table, lines, clines, mask, low, high, filters):
-    def leafwise(*shape):
-        return pl.BlockSpec((PER, *shape), lambda s: (s,) + (0,) * len(shape))
-
+
+    def send(below, above):
+        up, down = (one, two)[above], (one, two)[below]
+        for n in range(L):
+            for i in range(0, E, 2):
+                def face(which, k):
+                    pair = [faces[n, which, i + m, pl.ds(k, E, stride=E), :] for m in range(2)]
+                    return jnp.concatenate(pair, axis=0).astype(bf16)
+                rows = slice(E * i, E * i + 2 * E)
+                up[0, n, rows] = face(0, E - 1)
+                up[1, n, rows] = face(1, E - 1)
+                down[0, n, rows] = face(1, 0)
+                down[1, n, rows] = jnp.zeros((2 * E, C), bf16)
+
+    by_parity(send)
+
+
+def first_conv(table, lines, clines, mask, faces, filters):
     return pl.pallas_call(
         first_kernel,
-        grid=(L // PER,),
         out_shape=(
             jax.ShapeDtypeStruct((L, 5, FACE, 2 * SPAN), bf16),
             jax.ShapeDtypeStruct((L, E, FACE, C), bf16),
             jax.ShapeDtypeStruct((L, E, FACE, C), bf16),
             jax.ShapeDtypeStruct((2, L, FACE, C), bf16),
-            jax.ShapeDtypeStruct((L, FACE, C), bf16),
+            jax.ShapeDtypeStruct((2, L, FACE, C), bf16),
         ),
         in_specs=[smem()] + [vmem()] * 8,
-        out_specs=(
-            leafwise(5, FACE, 2 * SPAN),
-            leafwise(E, FACE, C),
-            leafwise(E, FACE, C),
-            pl.BlockSpec((2, PER, FACE, C), lambda s: (0, s, 0, 0)),
-            leafwise(FACE, C),
-        ),
+        out_specs=(vmem(),) * 5,
         scratch_shapes=[
             pltpu.VMEM((L + 1, E, E, C), f32),
             pltpu.VMEM((L + 1, E, E, C), f32),
             pltpu.VMEM((L + 1, 4, E, C), f32),
-            pltpu.VMEM((PER, 5, FACE, SPAN), bf16),
+            pltpu.VMEM((L, 5, FACE, SPAN), bf16),
             pltpu.VMEM((16, C), f32),
-            pltpu.VMEM((PER, 2, E, FACE, C), f32),
+            pltpu.VMEM((L, 2, E, FACE, C), f32),
         ],
         compiler_params=params(24),
         cost_estimate=cost(15e9, 18e6),
         name="first_conv",
-    )(table, lines, clines, mask, low, high, *filters)
+    )(table, lines, clines, mask, *faces, *filters)
 
 
 def split_halves(core, whole, kept, sent):
@@ -355,23 +363,25 @@
 
 
 def second_kernel(
-    table, hidden, low_in, cot, mask, w2,
-    coarse, kept, sent,
-    lines, low, cols, turned, total, whole, thin,
+    table, hidden, one_in, two_in, cot, mask, sent_first,
+    cols, active_out, kept, sent,
+    lines, low, turned, total, whole, thin,
 ):
     lines[L] = jnp.zeros((E, FACE, C), f32)
     low[L] = jnp.zeros((E, E, C), f32)
-    thin[0] = jnp.zeros((2 * FACE, C), f32)
+    thin[...] = jnp.zeros_like(thin)
 
     @pl.loop(0, L)
     def _(leaf):
         lines[leaf] = hidden[leaf].astype(f32)
-        low[leaf] = low_in[leaf].astype(f32).reshape(E, E, C)
-
-    w = w2[...].reshape(TAPS * C, C)
-
-    @pl.loop(0, L)
-    def _(leaf):
+
+    def receive(below, above):
+        for leaf in range(L):
+            low[leaf] = (one_in, two_in)[below][0, leaf].astype(f32).reshape(E, E, C)
+
+    by_parity(receive)
+
+    for leaf in range(L):
         for x in range(E + 1):
             parts = shifted_lines(table, lines, low, None, leaf, x, E, range(E + 1))
             for q in range(3):
@@ -379,19 +389,15 @@
                     value = jnp.concatenate([parts[r][q + 2 * m] for m in range(4)], axis=0).astype(bf16)
                     at = (x % 2) * SPAN + (3 * q + r) * C
                     cols[leaf, x // 2, :, at : at + C] = value
-        lo = cols[leaf, 0:4].reshape(2 * FACE, 2 * SPAN)
-        hi = cols[leaf, 1:5, :, 0:SPAN].reshape(2 * FACE, SPAN)
-        res = jnp.dot(lo, w[: 2 * SPAN], preferred_element_type=f32) + jnp.dot(hi, w[2 * SPAN :], preferred_element_type=f32)
         active = []
         for i in range(4):
             plane = mask[leaf, 2 * i].astype(f32)
             active += [plane[16 * j : 16 * j + E] for j in range(4)]
         active = jnp.concatenate(active, axis=0)
-        thin[1] = res * active
-        coarse[leaf] = thin[1, pl.ds(0, FACE, stride=2), :].astype(bf16)
-        thin[0, pl.ds(0, FACE, stride=2), :] = cot[leaf].astype(f32)
-        upstream = (thin[0] * active).astype(bf16)
-        turned[:, pl.ds(pl.multiple_of(leaf * 128, 128), 128)] = upstream.T
+        active_out[leaf] = active.astype(bf16)
+        thin[leaf, pl.ds(0, FACE, stride=2), :] = cot[leaf].astype(f32)
+        upstream = (thin[leaf] * active).astype(bf16)
+        turned[:, 128 * leaf : 128 * leaf + 128] = upstream.T
 
     for tile in range(9):
         at = slice(256 * tile, 256 * tile + 256)
@@ -402,31 +408,58 @@
         total[:, 2 * SPAN + 256 * tile : 2 * SPAN + end] = jnp.dot(turned[...], rhs, preferred_element_type=f32)
     for t in range(TAPS):
         whole[t] = total[:, t * C : t * C + C].T
-    split_halves(core_at(), whole, kept, sent)
-
-
-def second_conv(table, hidden, low, cot, mask, w2):
+    sent[0:TAPS] = sent_first[...]
+    split_halves(core_at(), whole, kept, sent.at[TAPS:])
+
+
+def second_grad(table, hidden, faces, cot, mask, sent_first):
     return pl.pallas_call(
         second_kernel,
-        out_shape=(jax.ShapeDtypeStruct((L, 64, C), bf16), *halves_shape()),
-        in_specs=[smem()] + [vmem()] * 5,
-        out_specs=(vmem(),) * 3,
+        out_shape=(
+            jax.ShapeDtypeStruct((L, 5, 32, 2 * SPAN), bf16),
+            jax.ShapeDtypeStruct((L, 2 * FACE, C), bf16),
+            jax.ShapeDtypeStruct((TAPS, HALF, C), f32),
+            jax.ShapeDtypeStruct((2 * TAPS, HALF, C), bf16),
+        ),
+        in_specs=[smem()] + [vmem()] * 6,
+        out_specs=(vmem(),) * 4,
         scratch_shapes=[
             pltpu.VMEM((L + 1, E, FACE, C), f32),
             pltpu.VMEM((L + 1, E, E, C), f32),
-            pltpu.VMEM((L, 5, 32, 2 * SPAN), bf16),
             pltpu.VMEM((C, L * 128), bf16),
             pltpu.VMEM((C, 3 * SPAN), f32),
             pltpu.VMEM((TAPS, C, C), f32),
-            pltpu.VMEM((2, 2 * FACE, C), f32),
+            pltpu.VMEM((L, 2 * FACE, C), f32),
         ],
         compiler_params=params(20),
         cost_estimate=cost(8e9, 6e6),
-        name="second_conv",
-    )(table, hidden, low, cot, mask, w2)
-
-
-def adjoint_kernel(start, count, table, delta, mask, low_in, high_in, w, out, lines, low, high, cols, wa, wb):
+        name="second_grad",
+    )(table, hidden, *faces, cot, mask, sent_first)
+
+
+def coarse_kernel(cols, active, w2, coarse, thin):
+    w = w2[...].reshape(TAPS * C, C)
+    for leaf in range(L):
+        lo = cols[leaf, 0:4].reshape(2 * FACE, 2 * SPAN)
+        hi = cols[leaf, 1:5, :, 0:SPAN].reshape(2 * FACE, SPAN)
+        thin[leaf] = (dot(lo, w[: 2 * SPAN]) + dot(hi, w[2 * SPAN :])) * active[leaf].astype(f32)
+        coarse[leaf] = thin[leaf, pl.ds(0, FACE, stride=2), :].astype(bf16)
+
+
+def coarse_conv(cols, active, w2):
+    return pl.pallas_call(
+        coarse_kernel,
+        out_shape=jax.ShapeDtypeStruct((L, 64, C), bf16),
+        in_specs=[vmem()] * 3,
+        out_specs=vmem(),
+        scratch_shapes=[pltpu.VMEM((L, 2 * FACE, C), f32)],
+        compiler_params=params(12),
+        cost_estimate=cost(1e9, 2e6),
+        name="coarse_conv",
+    )(cols, active, w2)
+
+
+def adjoint_kernel(start, count, table, delta, mask, one_in, two_in, w, out, lines, low, high, cols, wa, wb):
     lines[L] = jnp.zeros((E, FACE, C), f32)
     low[L] = jnp.zeros((E, E, C), f32)
     high[L] = jnp.zeros((E, E, C), f32)
@@ -434,29 +467,32 @@
     @pl.loop(0, L)
     def _(leaf):
         lines[leaf] = delta[leaf].astype(f32)
-        low[leaf] = low_in[leaf].astype(f32).reshape(E, E, C)
-        high[leaf] = high_in[leaf].astype(f32).reshape(E, E, C)
+
+    def receive(below, above):
+        for leaf in range(L):
+            low[leaf] = (one_in, two_in)[below][1, leaf].astype(f32).reshape(E, E, C)
+            high[leaf] = (one_in, two_in)[above][0, leaf].astype(f32).reshape(E, E, C)
+
+    by_parity(receive)
 
     banded_turned(w, wa, wb)
 
-    @pl.loop(0, count // PER)
-    def _(step):
-        for n in range(PER):
-            leaf = start + PER * step + n
-            for pair in range(5):
-                for half in range(2):
-                    def store(at, value, n=n, pair=pair, half=half):
-                        cols[n, pair, :, half * SPAN + at : half * SPAN + at + C] = value
-                    fill_plane(store, table, lines, low, high, leaf, 2 * pair + half, E)
-            res = pairs_dot(dot_turned, cols, n, wa, wb)
+    for n in range(count):
+        leaf = start + n
+        for pair in range(5):
             for half in range(2):
-                m = half_planes(mask, leaf, half).astype(f32)
-                value = (res[:, half * C : half * C + C] * m).astype(bf16)
-                for pair in range(4):
-                    out[PER * step + n, 2 * pair + half] = value[FACE * pair : FACE * pair + FACE]
-
-
-def adjoint_conv(start, count, table, delta, mask, low, high, w):
+                def store(at, value, n=n, pair=pair, half=half):
+                    cols[n, pair, :, half * SPAN + at : half * SPAN + at + C] = value
+                fill_plane(store, table, lines, low, high, leaf, 2 * pair + half, E)
+        res = pairs_dot(dot_turned, cols, n, wa, wb)
+        for half in range(2):
+            m = half_planes(mask, leaf, half).astype(f32)
+            value = (res[:, half * C : half * C + C] * m).astype(bf16)
+            for pair in range(4):
+                out[n, 2 * pair + half] = value[FACE * pair : FACE * pair + FACE]
+
+
+def adjoint_conv(start, count, table, delta, mask, faces, w):
     def kernel(*refs):
         adjoint_kernel(start, count, *refs)
 
@@ -469,39 +505,39 @@
             pltpu.VMEM((L + 1, E, FACE, C), f32),
             pltpu.VMEM((L + 1, E, E, C), f32),
             pltpu.VMEM((L + 1, E, E, C), f32),
-            pltpu.VMEM((PER, 5, FACE, 2 * SPAN), bf16),
+            pltpu.VMEM((count, 5, FACE, 2 * SPAN), bf16),
             pltpu.VMEM((2 * C, 2 * SPAN), bf16),
             pltpu.VMEM((2 * C, 2 * SPAN), bf16),
         ],
-        compiler_params=params(16),
+        compiler_params=params(26),
         cost_estimate=cost(10e9 * count / L, 6e6),
         name="first_adjoint",
-    )(table, delta, mask, low, high, w)
-
-
-def start_sum_kernel(kept1, got1, kept2, got2, own, *sends):
+    )(table, delta, mask, *faces, w)
+
+
+def start_sum_kernel(kept1, kept2, got, own, *sends):
     mine = ring_at()
     for d in range(4):
-        rows = pl.ds(pl.multiple_of(((mine + d) % 4) * PIECE, PIECE), PIECE)
+        rows = pl.ds(pl.multiple_of((mine ^ d) * PIECE, PIECE), PIECE)
         for t in range(2 * TAPS):
-            kept, got, n = (kept1, got1, t) if t < TAPS else (kept2, got2, t - TAPS)
-            value = kept[n, rows, :] + got[n, rows, :].astype(f32)
+            kept, n = (kept1, t) if t < TAPS else (kept2, t - TAPS)
+            value = kept[n, rows, :] + got[t, rows, :].astype(f32)
             if d == 0:
                 own[t] = value
             else:
                 sends[d - 1][t] = value.astype(bf16)
 
 
-def start_sum(kept1, got1, kept2, got2):
+def start_sum(kept1, kept2, got):
     return pl.pallas_call(
         start_sum_kernel,
         out_shape=(jax.ShapeDtypeStruct((2 * TAPS, PIECE, C), f32),) + (jax.ShapeDtypeStruct((2 * TAPS, PIECE, C), bf16),) * 3,
-        in_specs=[vmem()] * 4,
+        in_specs=[vmem()] * 3,
         out_specs=(vmem(),) * 4,
         compiler_params=params(12),
         cost_estimate=cost(1e6, 3e6),
         name="start_sum",
-    )(kept1, got1, kept2, got2)
+    )(kept1, kept2, got)
 
 
 def next_sum_kernel(own, a, b, c, out):
@@ -553,7 +589,7 @@
     for parts, which in ((mine, core), (theirs, 1 - core)):
         at = jnp.where(which == 0, at_y, at_x)
         for d in range(4):
-            row = pl.multiple_of(which * HALF + ((at - d) & 3) * PIECE, PIECE)
+            row = pl.multiple_of(which * HALF + (at ^ d) * PIECE, PIECE)
             for t in range(2 * TAPS):
                 out, n = (first, t) if t < TAPS else (second, t - TAPS)
                 out[n, pl.ds(row, PIECE), :] = parts[d][t].astype(f32)
@@ -578,7 +614,7 @@
         for leaf in range(leaf_count):
             for scene in range(8):
                 z, x, y, core = leaf // 4, leaf % 4, scene // 2, scene % 2
-                x, y = (x, (y + d) % 4) if core == 0 else ((x + d) % 4, y)
+                x, y = (x, y ^ d) if core == 0 else (x ^ d, y)
                 pairs.append((leaf * 8 + scene, (z * 4 + x) * 8 + y * 2 + core))
         out.append(pairs)
     return out
@@ -591,9 +627,11 @@
     return first + second
 
 
-def passed(block, distance):
+def exchanged(first, second):
     count = lax.axis_size("leaf")
-    return lax.ppermute(block, "leaf", [(i - distance, i) for i in range(count) if 0 <= i - distance < count])
+    pairs = [(i, i ^ 1) for i in range(count)]
+    shifted = [(i, i + 1 if i % 2 else i - 1) for i in range(1, count - 1)]
+    return lax.ppermute(first, "leaf", pairs), lax.ppermute(second, "leaf", shifted)
 
 
 def to_other_core(block):
@@ -608,28 +646,25 @@
     table = neighbours[0]
     voxels = voxel_mask[0]
 
-    up, down = first_faces(voxels, feat, cot)
+    one, two = first_faces(voxels, feat, cot)
     with jax.named_scope("faces_in"):
-        low = passed(up, 1)
-        high = passed(down, -1)
-    voxels, _ = lax.optimization_barrier((voxels, down))
+        faces = exchanged(one, two)
+    voxels, _ = lax.optimization_barrier((voxels, one))
     mask, lines, clines, *filters = setup(voxels, feat, cot, weight_first, weight_second)
-    cols, hidden, delta, up, down = first_conv(table, lines, clines, mask, low, high, filters)
+    cols, hidden, delta, one, two = first_conv(table, lines, clines, mask, faces, filters)
     with jax.named_scope("faces_mid"):
-        tops = passed(up, 1)
-        bottom = passed(down, -1)
-        tops, bottom = lax.optimization_barrier((tops, bottom))
+        faces = exchanged(one, two)
     kept1, sent1 = first_grad(cols, delta)
+    cols2, active, kept2, sent = second_grad(table, hidden, faces, cot, mask, sent1)
     with jax.named_scope("sum_core"):
-        got1 = to_other_core(sent1)
-    coarse, kept2, sent2 = second_conv(table, hidden, tops[0], cot, mask, weight_second)
-    with jax.named_scope("sum_core"):
-        got2 = to_other_core(sent2)
-    own, *sends = start_sum(kept1, got1, kept2, got2)
+        got = to_other_core(sent)
+    own, *sends = start_sum(kept1, kept2, got)
     orders, groups = ring_orders(leaf_count), rest_groups(leaf_count)
     per = -(-2 * TAPS // leaf_count)
     with jax.named_scope("sum_ring"):
         received = [lax.ppermute(s, both, o) for s, o in zip(sends, orders)]
+    input_grad = adjoint_conv(0, L, table, delta, mask, faces, weight_first)
+    own, input_grad = lax.optimization_barrier((own, input_grad))
     parts = next_sum(own, received, per * leaf_count).reshape(leaf_count, per * PIECE, C)
     with jax.named_scope("sum_rest"):
         parts = lax.all_to_all(parts, both, 0, 0, axis_index_groups=groups, tiled=True)
@@ -639,14 +674,12 @@
     own = parts.reshape(per * leaf_count, PIECE, C)[: 2 * TAPS]
     with jax.named_scope("gather_ring"):
         received = [lax.ppermute(own, both, o) for o in orders]
+    cols2, own = lax.optimization_barrier((cols2, own))
+    coarse = coarse_conv(cols2, active, weight_second)
+    coarse, mine = lax.optimization_barrier((coarse, [own, *received]))
     with jax.named_scope("gather_core"):
-        theirs = [to_other_core(own)]
-    delta, own = lax.optimization_barrier((delta, own))
-    input_grad = adjoint_conv(0, L, table, delta, mask, tops[1], bottom, weight_first)
-    input_grad, received = lax.optimization_barrier((input_grad, received))
-    with jax.named_scope("gather_core"):
-        theirs += [to_other_core(piece) for piece in received]
-    grad_first, grad_second = finish([own, *received, *theirs])
+        theirs = [to_other_core(piece) for piece in mine]
+    grad_first, grad_second = finish([*mine, *theirs])
     return (
         coarse.reshape(1, L, 4, 4, 4, C),
         input_grad.reshape(1, L, E, E, E, C),

time: 119 us -> 112 us (0.941)
  starting transfers between devices: 29.4 us -> 22.4 us
    ppermute x6 -> x5, starting transfers between devices: 9.09 us -> 3.68 us  [to_other_core(): lax.ppermute(block, 'scene', [(i, i ^ 1) for i in range(lax.axis_size('sc...]
    ppermute x3, waiting for transfers between devices: 5.69 us -> 0.64 us  [shards(): received = [lax.ppermute(s, both, o) for s, o in zip(sends, orders)]]
    ppermute x4, starting transfers between devices: 12 us -> 7.33 us  [the longest x2 5.82 us: exchanged(): lax.ppermute(first, 'leaf', pairs)]
    ppermute x3, waiting for transfers between devices: 0.01 us -> 3.21 us  [shards(): received = [lax.ppermute(own, both, o) for o in orders]]
    ppermute x3, starting transfers between devices: 6.38 us -> 8.1 us  [shards(): received = [lax.ppermute(s, both, o) for s, o in zip(sends, orders)]]
    ppermute x4, waiting for transfers between devices: 0.85 us -> 2.56 us  [the longest x2 2.56 us: exchanged(): lax.ppermute(first, 'leaf', pairs)]
    ppermute x3, starting transfers between devices: 1.97 us -> 3.33 us  [shards(): received = [lax.ppermute(own, both, o) for o in orders]]
    ppermute x6 -> x5, waiting for transfers between devices: 3.04 us -> 3.65 us  [to_other_core(): lax.ppermute(block, 'scene', [(i, i ^ 1) for i in range(lax.axis_size('sc...]
  transfers between devices with their start and end apart: 16 -> 15, of which waited for: 7 -> 9; matrix products, arithmetic and copies ran while one was open for 0% -> 0% of each run, Pallas kernels for 17% -> 15%
where the time goes in v4:
time: 112 us; the launch traced here: 111 us
  blocking collectives  42 us (38%)
  Pallas kernels  33.1 us (30%)
  starting transfers between devices  22.4 us (20%)
  waiting for transfers between devices  10.1 us (9%)
  local copies, waits for them, and re-layouts  2.88 us (3%)
    all_to_all x2, blocking collectives, shards(): lax.all_to_all(parts, both, 0, 0, axis_index_groups=groups, tiled=True)  42 us
    pallas_call x1, Pallas kernels, first_conv(): pl.pallas_call(first_kernel, out_shape=(jax.ShapeDtypeStruct((L, 5, FACE,...  9.89 us
    ppermute x3, starting transfers between devices, shards(): received = [lax.ppermute(s, both, o) for s, o in zip(sends, orders)]  8.1 us
    pallas_call x1, Pallas kernels, adjoint_conv(): pl.pallas_call(kernel, out_shape=jax.ShapeDtypeStruct((count, E, FACE, C)...  7.41 us
    ppermute x2, starting transfers between devices, exchanged(): lax.ppermute(first, 'leaf', pairs)  5.82 us
    pallas_call x1, Pallas kernels, first_grad(): pl.pallas_call(first_grad_kernel, out_shape=halves_shape(), in_specs=[vme...  5.27 us
    ppermute x5, starting transfers between devices, to_other_core(): lax.ppermute(block, 'scene', [(i, i ^ 1) for i in range(lax.axis_size('sc...  3.68 us
    ppermute x5, waiting for transfers between devices, to_other_core(): lax.ppermute(block, 'scene', [(i, i ^ 1) for i in range(lax.axis_size('sc...  3.65 us
  transfers between devices with their start and end apart: 15, of which 9 were waited for; matrix products, arithmetic and copies ran while one was open for 0% of the time, Pallas kernels for 15%

profile of v4, /device:TPU:1, one launch (start us, length us, event | category | flops | bytes accessed | tf_op | source)
XLA Modules:
  0.0 111.2 jit_solution(15734847398910253078)
XLA Ops:
  0.6 1.2 %copy-done.1 = bf16[1,8,8,8,8,128]{5,4,3,2,1,0:T(8,128)(2,1)S(1)} copy-done((bf16[1,8,8,8,8,128]{5,4,3,2,1,0:T(8,128)(2,1)S(1)}, bf16[1,8,8,8,8,128]{5,4,3,2,1,0:T(8,128)(2,1)}, u32[]{:S(2)}) %copy-start.1) | copy-done | bytes 1048600
  1.9 0.9 copy-done.4
  2.8 0.7 copy-done.6
  3.5 1.3 %first_faces.1 = (bf16[8,80,128]{2,1,0:T(8,128)(2,1)S(1)}, bf16[8,80,128]{2,1,0:T(8,128)(2,1)S(1)}) custom-call(s32[8,512]{1,0:T(8,128)S(1)} %bitcast.19, bf16[8,8,64,128]{3,2,1,0:T(8,128)(2,1)S(1)} %bitcast.14, bf16[8,64,128]{2,1,0:T(8,128)(2,1)S(1)} %bitcast.16), custom_call_target="tpu_custom_call" | custom-call | flops 6000000000 | bytes 8000000 | tf_op jit(solution)/shard_map/first_faces/pallas_call | solution.py:167
  4.8 0.7 collective-permute-start.1
  5.4 4.6 %collective-permute-start = (bf16[8,80,128]{2,1,0:T(8,128)(2,1)S(1)}, bf16[8,80,128]{2,1,0:T(8,128)(2,1)S(1)}, u32[]{:S(2)}, u32[]{:S(2)}) collective-permute-start(bf16[8,80,128]{2,1,0:T(8,128)(2,1)S(1)} %get-tuple-element.39), channel_id=1, source_target_pairs={{0,8},{8,0},{16,24},{24,16},{32,40},{40,32},{48,56},{56,48},{64,72... | collective-permute-start | bytes 491528 | tf_op jit(solution)/shard_map/faces_in/ppermute | solution.py:634
  10.0 1.0 setup.1
  11.1 2.6 %collective-permute-done.one_in = bf16[8,80,128]{2,1,0:T(8,128)(2,1)S(1)} collective-permute-done((bf16[8,80,128]{2,1,0:T(8,128)(2,1)S(1)}, bf16[8,80,128]{2,1,0:T(8,128)(2,1)S(1)}, u32[]{:S(2)}, u32[]{:S(2)}) %collective-permute-start) | collective-permute-done | bytes 163872 | tf_op jit(solution)/shard_map/faces_in/ppermute | solution.py:634
  13.6 9.9 %first_conv.1 = (bf16[8,5,64,2304]{3,2,1,0:T(8,128)(2,1)S(1)}, bf16[8,8,64,128]{3,2,1,0:T(8,128)(2,1)S(1)}, bf16[8,8,64,128]{3,2,1,0:T(8,128)(2,1)S(1)}, bf16[2,...) custom-call(s32[8,26]{1,0:T(8,128)S(1)} %bitcast.21, f32[9,8,64,128]{3,2,1,0:T(8,128)S(1)} %get-tuple-element.41.lines, ...), custom_call_target="tpu_custom_call" | custom-call | flops 15000000512 | bytes 18000000 | tf_op jit(solution)/shard_map/first_conv/pallas_call | solution.py:285
  23.5 1.2 %collective-permute-start.2 = (bf16[2,8,64,128]{3,2,1,0:T(8,128)(2,1)S(1)}, bf16[2,8,64,128]{3,2,1,0:T(8,128)(2,1)S(1)}, u32[]{:S(2)}, u32[]{:S(2)}) collective-permute-start(bf16[2,8,64,128]{3,2,1,0:T(8,128)(2,1)S(1)} %get-tuple-element.49), channel_id=1, source_target_pairs={{0,8},{8,0},{16,24},{24,16},{32,40},{40,32},{48,56},{56,48},{64,72... | collective-permute-start | bytes 786440 | tf_op jit(solution)/shard_map/faces_mid/ppermute | solution.py:634
  24.8 0.8 collective-permute-start.3
  25.6 5.3 %first_grad.1 = (f32[27,64,128]{2,1,0:T(8,128)S(1)}, bf16[27,64,128]{2,1,0:T(8,128)(2,1)S(1)}) custom-call(bf16[8,5,64,2304]{3,2,1,0:T(8,128)(2,1)S(1)} %get-tuple-element.51.cols, bf16[8,8,64,128]{3,2,1,0:T(8,128)(2,1)S(1)} %get-tuple-element.52.delta.refs_1_), custom_call_target="tpu_custom_call" | custom-call | flops 6000000000 | bytes 14000000 | tf_op jit(solution)/shard_map/first_grad/pallas_call | solution.py:349
  30.9 3.0 %second_grad.1 = (bf16[8,5,32,2304]{3,2,1,0:T(8,128)(2,1)S(1)}, bf16[8,128,128]{2,1,0:T(8,128)(2,1)S(1)}, f32[27,64,128]{2,1,0:T(8,128)S(1)}, bf16[54,64,128]{2,1,0:T(8,128)(2,1)S(1)}) custom-call(s32[8,26]{1,0:T(8,128)S(1)} %bitcast.22, bf16[8,8,64,128]{3,2,1,0:T(8,128)(2,1)S(1)} %get-tuple-element.48.hidden, ...), custom_call_target="tpu_custom_call" | custom-call | flops 8000000000 | bytes 6000000 | tf_op jit(solution)/shard_map/second_grad/pallas_call | solution.py:416
  34.0 2.2 %collective-permute-start.4 = (bf16[54,64,128]{2,1,0:T(8,128)(2,1)S(1)}, bf16[54,64,128]{2,1,0:T(8,128)(2,1)S(1)}, u32[]{:S(2)}, u32[]{:S(2)}) collective-permute-start(bf16[54,64,128]{2,1,0:T(8,128)(2,1)S(1)} %get-tuple-element.57), channel_id=1, source_target_pairs={{0,1},{1,0},{2,3},{3,2},{4,5},{5,4},{6,7},{7,6},{8,9},{9,8},{10,11... | collective-permute-start | bytes 2654216 | tf_op jit(solution)/shard_map/sum_core/ppermute | solution.py:638
  36.2 2.1 %collective-permute-done.4.got = bf16[54,64,128]{2,1,0:T(8,128)(2,1)S(1)} collective-permute-done((bf16[54,64,128]{2,1,0:T(8,128)(2,1)S(1)}, bf16[54,64,128]{2,1,0:T(8,128)(2,1)S(1)}, u32[]{:S(2)}, u32[]{:S(2)}) %collective-permute-start.4) | collective-permute-done | bytes 884768 | tf_op jit(solution)/shard_map/sum_core/ppermute | solution.py:638
  38.5 4.5 %collective-permute-start.5 = (bf16[54,16,128]{2,1,0:T(8,128)(2,1)S(1)}, bf16[54,16,128]{2,1,0:T(8,128)(2,1)S(1)}, u32[]{:S(2)}, u32[]{:S(2)}) collective-permute-start(bf16[54,16,128]{2,1,0:T(8,128)(2,1)S(1)} %get-tuple-element.60), channel_id=1, source_target_pairs={{0,2},{1,9},{2,0},{3,11},{4,6},{5,13},{6,4},{7,15},{8,10},{9,1},{1... | collective-permute-start | bytes 663560 | tf_op jit(solution)/shard_map/sum_ring/ppermute | solution.py:665
  43.0 3.6 %collective-permute-start.6 = (bf16[54,16,128]{2,1,0:T(8,128)(2,1)S(1)}, bf16[54,16,128]{2,1,0:T(8,128)(2,1)S(1)}, u32[]{:S(2)}, u32[]{:S(2)}) collective-permute-start(bf16[54,16,128]{2,1,0:T(8,128)(2,1)S(1)} %get-tuple-element.61), channel_id=1, source_target_pairs={{0,4},{1,17},{2,6},{3,19},{4,0},{5,21},{6,2},{7,23},{8,12},{9,25},... | collective-permute-start | bytes 663560 | tf_op jit(solution)/shard_map/sum_ring/ppermute | solution.py:665
  46.6 7.4 %first_adjoint.1 = bf16[8,8,64,128]{3,2,1,0:T(8,128)(2,1)} custom-call(s32[8,26]{1,0:T(8,128)S(1)} %bitcast.23, bf16[8,8,64,128]{3,2,1,0:T(8,128)(2,1)S(1)} %get-tuple-element.52.delta.refs_1_, bf16[8,8,64,128]{3,2,1,0:T(8,128)(2,1)S(1)} %get-tuple-element.43.mask.refs_2_, bf16[2,8,64,128]{3,2,1,0:T(8,128)(2,1)S(1)} %collective-permute-done.2.one_in.refs_3_, ...), custom_call_target="tpu_custom_call" | custom-call | flops 10000000000 | bytes 6000000 | tf_op jit(solution)/shard_map/first_adjoint/pallas_call | solution.py:499
  54.0 0.6 collective-permute-done.7.c
  54.7 26.0 %all_to_all.10.refs_0_ = bf16[32,32,128]{2,1,0:T(8,128)(2,1)S(1)} all-to-all(bf16[32,32,128]{2,1,0:T(8,128)(2,1)S(1)} %bitcast.8), channel_id=1, replica_groups={{0,8,16,24,32,40,48,56,64,72,80,88,96,104,112,120,128,136,144,152,160,1..., dimensions={0} | all-to-all | bytes 524288 | tf_op jit(solution)/shard_map/sum_rest/all_to_all | solution.py:670
  80.8 16.0 %all_to_all.11 = bf16[32,32,128]{2,1,0:T(8,128)(2,1)S(1)} all-to-all(bf16[32,32,128]{2,1,0:T(8,128)(2,1)S(1)} %last_sum.1), channel_id=1, replica_groups={{0,8,16,24,32,40,48,56,64,72,80,88,96,104,112,120,128,136,144,152,160,1..., dimensions={0} | all-to-all | bytes 524288 | tf_op jit(solution)/shard_map/gather_rest/all_to_all | solution.py:673
  97.0 3.1 %collective-permute-start.8 = (bf16[54,16,128]{2,1,0:T(8,128)(2,1)S(1)}, bf16[54,16,128]{2,1,0:T(8,128)(2,1)S(1)}, u32[]{:S(2)}, u32[]{:S(2)}) collective-permute-start(bf16[54,16,128]{2,1,0:T(8,128)(2,1)S(1)} %bitcast.11), channel_id=1, source_target_pairs={{0,2},{1,9},{2,0},{3,11},{4,6},{5,13},{6,4},{7,15},{8,10},{9,1},{1... | collective-permute-start | bytes 663560 | tf_op jit(solution)/shard_map/gather_ring/ppermute | solution.py:676
  100.1 2.8 %coarse_conv.1 = bf16[8,64,128]{2,1,0:T(8,128)(2,1)} custom-call(bf16[8,5,32,2304]{3,2,1,0:T(8,128)(2,1)S(1)} %get-tuple-element.63.cols, bf16[8,128,128]{2,1,0:T(8,128)(2,1)S(1)} %get-tuple-element.64.active, bf16[27,128,128]{2,1,0:T(8,128)(2,1)S(1)} %copy-done), custom_call_target="tpu_custom_call" | custom-call | flops 1000000000 | bytes 2000000 | tf_op jit(solution)/shard_map/coarse_conv/pallas_call | solution.py:450
  102.9 2.6 %collective-permute-done.10.refs_3_ = bf16[54,16,128]{2,1,0:T(8,128)(2,1)S(1)} collective-permute-done((bf16[54,16,128]{2,1,0:T(8,128)(2,1)S(1)}, bf16[54,16,128]{2,1,0:T(8,128)(2,1)S(1)}, u32[]{:S(2)}, u32[]{:S(2)}) %collective-permute-start.10) | collective-permute-done | bytes 221216 | tf_op jit(solution)/shard_map/gather_ring/ppermute | solution.py:676
  105.5 0.6 collective-permute-done.8.refs_1_
  106.1 1.0 collective-permute-start.11
  107.1 0.5 collective-permute-start.13
  107.6 0.6 collective-permute-done.11.refs_4_
  108.2 0.4 collective-permute-done.12.refs_5_
  108.6 0.3 collective-permute-done.13.refs_6_
  108.9 0.3 collective-permute-done.14.refs_7_
  109.2 2.0 %finish.1 = (f32[27,128,128]{2,1,0:T(8,128)}, f32[27,128,128]{2,1,0:T(8,128)}) custom-call(bf16[54,16,128]{2,1,0:T(8,128)(2,1)S(1)} %bitcast.13, bf16[54,16,128]{2,1,0:T(8,128)(2,1)S(1)} %collective-permute-done.8.refs_1_, bf16[54,16,128]{2,1,0:T(8,128)(2,1)S(1)} %collective-permute-done.9.refs_2_, bf16[54,16,128]{2,1,0:T(8,128)(2,1)S(1)} %collective-permute-done.10.refs_3_, ...), custom_call_target="tpu_custom_call" | custom-call | flops 1000000 | bytes 6000000 | tf_op jit(solution)/shard_map/finish/pallas_call | solution.py:599
  (30 shorter events, 0.7 us)
Async XLA Ops:
  0.6 1.2 %copy-start.1 = (bf16[1,8,8,8,8,128]{5,4,3,2,1,0:T(8,128)(2,1)S(1)}, bf16[1,8,8,8,8,128]{5,4,3,2,1,0:T(8,128)(2,1)}, u32[]{:S(2)}) copy-start(bf16[1,8,8,8,8,128]{5,4,3,2,1,0:T(8,128)(2,1)} %param.6) | copy-start | bytes 3145732
  1.9 0.9 copy-start.4
  2.8 0.7 copy-start.6
  3.5 6.5 %copy-start = (bf16[27,128,128]{2,1,0:T(8,128)(2,1)S(1)}, bf16[27,128,128]{2,1,0:T(8,128)(2,1)}, u32[]{:S(2)}) copy-start(bf16[27,128,128]{2,1,0:T(8,128)(2,1)} %w2.3) | copy-start | bytes 2654212
  3.5 6.5 %copy-start.2 = (bf16[1,8,8,8,8,128]{5,4,3,2,1,0:T(8,128)(2,1)S(1)}, bf16[1,8,8,8,8,128]{5,4,3,2,1,0:T(8,128)(2,1)}, u32[]{:S(2)}) copy-start(bf16[1,8,8,8,8,128]{5,4,3,2,1,0:T(8,128)(2,1)} %param.6) | copy-start | bytes 3145732
  3.5 6.5 %copy-start.3 = (bf16[27,128,128]{2,1,0:T(8,128)(2,1)S(1)}, bf16[27,128,128]{2,1,0:T(8,128)(2,1)}, u32[]{:S(2)}) copy-start(bf16[27,128,128]{2,1,0:T(8,128)(2,1)} %refs_5_.1) | copy-start | bytes 2654212
  3.5 6.5 %copy-start.7 = (s32[1,8,512]{2,1,0:T(8,128)S(1)}, s32[1,8,512]{2,1,0:T(8,128)}, u32[]{:S(2)}) copy-start(s32[1,8,512]{2,1,0:T(8,128)} %param.11) | copy-start | bytes 49156
  4.8 6.3 %collective-permute-start.1 = (bf16[8,80,128]{2,1,0:T(8,128)(2,1)S(1)}, bf16[8,80,128]{2,1,0:T(8,128)(2,1)S(1)}, u32[]{:S(2)}, u32[]{:S(2)}) collective-permute-start(bf16[8,80,128]{2,1,0:T(8,128)(2,1)S(1)} %get-tuple-element.44), channel_id=1, source_target_pairs={{8,16},{16,8},{24,32},{32,24},{40,48},{48,40},{56,64},{64,56},{72,... | collective-permute-start | bytes 491528 | tf_op jit(solution)/shard_map/faces_in/ppermute | solution.py:634
  5.4 8.2 %copy-start.8 = (s32[1,8,26]{2,1,0:T(8,128)S(1)}, s32[1,8,26]{2,1,0:T(8,128)}, u32[]{:S(2)}) copy-start(s32[1,8,26]{2,1,0:T(8,128)} %param.10) | copy-start | bytes 2500
  5.4 8.2 %collective-permute-start = (bf16[8,80,128]{2,1,0:T(8,128)(2,1)S(1)}, bf16[8,80,128]{2,1,0:T(8,128)(2,1)S(1)}, u32[]{:S(2)}, u32[]{:S(2)}) collective-permute-start(bf16[8,80,128]{2,1,0:T(8,128)(2,1)S(1)} %get-tuple-element.39), channel_id=1, source_target_pairs={{0,8},{8,0},{16,24},{24,16},{32,40},{40,32},{48,56},{56,48},{64,72... | collective-permute-start | bytes 491528 | tf_op jit(solution)/shard_map/faces_in/ppermute | solution.py:634
  23.5 7.4 %collective-permute-start.2 = (bf16[2,8,64,128]{3,2,1,0:T(8,128)(2,1)S(1)}, bf16[2,8,64,128]{3,2,1,0:T(8,128)(2,1)S(1)}, u32[]{:S(2)}, u32[]{:S(2)}) collective-permute-start(bf16[2,8,64,128]{3,2,1,0:T(8,128)(2,1)S(1)} %get-tuple-element.49), channel_id=1, source_target_pairs={{0,8},{8,0},{16,24},{24,16},{32,40},{40,32},{48,56},{56,48},{64,72... | collective-permute-start | bytes 786440 | tf_op jit(solution)/shard_map/faces_mid/ppermute | solution.py:634
  24.8 6.2 %collective-permute-start.3 = (bf16[2,8,64,128]{3,2,1,0:T(8,128)(2,1)S(1)}, bf16[2,8,64,128]{3,2,1,0:T(8,128)(2,1)S(1)}, u32[]{:S(2)}, u32[]{:S(2)}) collective-permute-start(bf16[2,8,64,128]{3,2,1,0:T(8,128)(2,1)S(1)} %get-tuple-element.50), channel_id=1, source_target_pairs={{8,16},{16,8},{24,32},{32,24},{40,48},{48,40},{56,64},{64,56},{72,... | collective-permute-start | bytes 786440 | tf_op jit(solution)/shard_map/faces_mid/ppermute | solution.py:634
  25.6 5.3 %copy-start.5 = (bf16[1,8,4,4,4,128]{5,4,3,2,1,0:T(4,128)(2,1)S(1)}, bf16[1,8,4,4,4,128]{5,4,3,2,1,0:T(4,128)(2,1)}, u32[]{:S(2)}) copy-start(bf16[1,8,4,4,4,128]{5,4,3,2,1,0:T(4,128)(2,1)} %param.9) | copy-start | bytes 393220
  34.0 4.3 %collective-permute-start.4 = (bf16[54,64,128]{2,1,0:T(8,128)(2,1)S(1)}, bf16[54,64,128]{2,1,0:T(8,128)(2,1)S(1)}, u32[]{:S(2)}, u32[]{:S(2)}) collective-permute-start(bf16[54,64,128]{2,1,0:T(8,128)(2,1)S(1)} %get-tuple-element.57), channel_id=1, source_target_pairs={{0,1},{1,0},{2,3},{3,2},{4,5},{5,4},{6,7},{7,6},{8,9},{9,8},{10,11... | collective-permute-start | bytes 2654216 | tf_op jit(solution)/shard_map/sum_core/ppermute | solution.py:638
  38.5 15.5 %collective-permute-start.5 = (bf16[54,16,128]{2,1,0:T(8,128)(2,1)S(1)}, bf16[54,16,128]{2,1,0:T(8,128)(2,1)S(1)}, u32[]{:S(2)}, u32[]{:S(2)}) collective-permute-start(bf16[54,16,128]{2,1,0:T(8,128)(2,1)S(1)} %get-tuple-element.60), channel_id=1, source_target_pairs={{0,2},{1,9},{2,0},{3,11},{4,6},{5,13},{6,4},{7,15},{8,10},{9,1},{1... | collective-permute-start | bytes 663560 | tf_op jit(solution)/shard_map/sum_ring/ppermute | solution.py:665
  43.0 11.0 %collective-permute-start.6 = (bf16[54,16,128]{2,1,0:T(8,128)(2,1)S(1)}, bf16[54,16,128]{2,1,0:T(8,128)(2,1)S(1)}, u32[]{:S(2)}, u32[]{:S(2)}) collective-permute-start(bf16[54,16,128]{2,1,0:T(8,128)(2,1)S(1)} %get-tuple-element.61), channel_id=1, source_target_pairs={{0,4},{1,17},{2,6},{3,19},{4,0},{5,21},{6,2},{7,23},{8,12},{9,25},... | collective-permute-start | bytes 663560 | tf_op jit(solution)/shard_map/sum_ring/ppermute | solution.py:665
  46.6 8.1 %collective-permute-start.7 = (bf16[54,16,128]{2,1,0:T(8,128)(2,1)S(1)}, bf16[54,16,128]{2,1,0:T(8,128)(2,1)S(1)}, u32[]{:S(2)}, u32[]{:S(2)}) collective-permute-start(bf16[54,16,128]{2,1,0:T(8,128)(2,1)S(1)} %get-tuple-element.62), channel_id=1, source_target_pairs={{0,6},{1,25},{2,4},{3,27},{4,2},{5,29},{6,0},{7,31},{8,14},{9,17},... | collective-permute-start | bytes 663560 | tf_op jit(solution)/shard_map/sum_ring/ppermute | solution.py:665
  96.8 8.7 %collective-permute-start.10 = (bf16[54,16,128]{2,1,0:T(8,128)(2,1)S(1)}, bf16[54,16,128]{2,1,0:T(8,128)(2,1)S(1)}, u32[]{:S(2)}, u32[]{:S(2)}) collective-permute-start(bf16[54,16,128]{2,1,0:T(8,128)(2,1)S(1)} %bitcast.9), channel_id=1, source_target_pairs={{0,6},{1,25},{2,4},{3,27},{4,2},{5,29},{6,0},{7,31},{8,14},{9,17},... | collective-permute-start | bytes 663560 | tf_op jit(solution)/shard_map/gather_ring/ppermute | solution.py:676
  96.9 8.6 %collective-permute-start.9 = (bf16[54,16,128]{2,1,0:T(8,128)(2,1)S(1)}, bf16[54,16,128]{2,1,0:T(8,128)(2,1)S(1)}, u32[]{:S(2)}, u32[]{:S(2)}) collective-permute-start(bf16[54,16,128]{2,1,0:T(8,128)(2,1)S(1)} %bitcast.10), channel_id=1, source_target_pairs={{0,4},{1,17},{2,6},{3,19},{4,0},{5,21},{6,2},{7,23},{8,12},{9,25},... | collective-permute-start | bytes 663560 | tf_op jit(solution)/shard_map/gather_ring/ppermute | solution.py:676
  97.0 9.1 %collective-permute-start.8 = (bf16[54,16,128]{2,1,0:T(8,128)(2,1)S(1)}, bf16[54,16,128]{2,1,0:T(8,128)(2,1)S(1)}, u32[]{:S(2)}, u32[]{:S(2)}) collective-permute-start(bf16[54,16,128]{2,1,0:T(8,128)(2,1)S(1)} %bitcast.11), channel_id=1, source_target_pairs={{0,2},{1,9},{2,0},{3,11},{4,6},{5,13},{6,4},{7,15},{8,10},{9,1},{1... | collective-permute-start | bytes 663560 | tf_op jit(solution)/shard_map/gather_ring/ppermute | solution.py:676
  106.1 2.1 %collective-permute-start.11 = (bf16[54,16,128]{2,1,0:T(8,128)(2,1)S(1)}, bf16[54,16,128]{2,1,0:T(8,128)(2,1)S(1)}, u32[]{:S(2)}, u32[]{:S(2)}) collective-permute-start(bf16[54,16,128]{2,1,0:T(8,128)(2,1)S(1)} %bitcast.12), channel_id=1, source_target_pairs={{0,1},{1,0},{2,3},{3,2},{4,5},{5,4},{6,7},{7,6},{8,9},{9,8},{10,11... | collective-permute-start | bytes 663560 | tf_op jit(solution)/shard_map/gather_core/ppermute | solution.py:638
  107.1 1.5 %collective-permute-start.12 = (bf16[54,16,128]{2,1,0:T(8,128)(2,1)S(1)}, bf16[54,16,128]{2,1,0:T(8,128)(2,1)S(1)}, u32[]{:S(2)}, u32[]{:S(2)}) collective-permute-start(bf16[54,16,128]{2,1,0:T(8,128)(2,1)S(1)} %collective-permute-done.8.refs_1_), channel_id=1, source_target_pairs={{0,1},{1,0},{2,3},{3,2},{4,5},{5,4},{6,7},{7,6},{8,9},{9,8},{10,11... | collective-permute-start | bytes 663560 | tf_op jit(solution)/shard_map/gather_core/ppermute | solution.py:638
  107.1 1.8 %collective-permute-start.13 = (bf16[54,16,128]{2,1,0:T(8,128)(2,1)S(1)}, bf16[54,16,128]{2,1,0:T(8,128)(2,1)S(1)}, u32[]{:S(2)}, u32[]{:S(2)}) collective-permute-start(bf16[54,16,128]{2,1,0:T(8,128)(2,1)S(1)} %collective-permute-done.9.refs_2_), channel_id=1, source_target_pairs={{0,1},{1,0},{2,3},{3,2},{4,5},{5,4},{6,7},{7,6},{8,9},{9,8},{10,11... | collective-permute-start | bytes 663560 | tf_op jit(solution)/shard_map/gather_core/ppermute | solution.py:638
  107.6 1.6 %collective-permute-start.14 = (bf16[54,16,128]{2,1,0:T(8,128)(2,1)S(1)}, bf16[54,16,128]{2,1,0:T(8,128)(2,1)S(1)}, u32[]{:S(2)}, u32[]{:S(2)}) collective-permute-start(bf16[54,16,128]{2,1,0:T(8,128)(2,1)S(1)} %collective-permute-done.10.refs_3_), channel_id=1, source_target_pairs={{0,1},{1,0},{2,3},{3,2},{4,5},{5,4},{6,7},{7,6},{8,9},{9,8},{10,11... | collective-permute-start | bytes 663560 | tf_op jit(solution)/shard_map/gather_core/ppermute | solution.py:638

commit v5 on v4

--- a/solution.py
+++ b/solution.py
@@ -16,6 +16,7 @@
 SPAN = 9 * C
 TAPS = 27
 HALF = C // 2
+TOGETHER = 2
 PIECE = 16
 
 
@@ -129,8 +130,8 @@
 
 
 def pairs_dot(multiply, cols, at, first, second):
-    lo = cols[at, 0:4].reshape(4 * FACE, 2 * SPAN)
-    hi = cols[at, 1:5].reshape(4 * FACE, 2 * SPAN)
+    lo = cols[at : at + TOGETHER, 0:4].reshape(TOGETHER * 4 * FACE, 2 * SPAN)
+    hi = cols[at : at + TOGETHER, 1:5].reshape(TOGETHER * 4 * FACE, 2 * SPAN)
     return multiply(lo, first[...]) + multiply(hi, second[...])
 
 
@@ -176,23 +177,27 @@
     )(voxels, feat, cot)
 
 
-def setup_kernel(voxels, feat, cot, w1, w2, mask, lines, clines, wa, wb, wc, spread, coarse):
+def setup_kernel(voxels, feat, cot, w1, w2, mask, lines, clines, active, upturned, wa, wb, wc, thin):
     lines[L] = jnp.zeros((E, FACE, C), f32)
-    clines[...] = jnp.zeros((L + 1, 4, FACE, C), f32)
+    clines[L] = jnp.zeros((4, 4 * E, C), f32)
+    thin[...] = jnp.zeros_like(thin)
     for leaf in range(L):
         whole = spread_mask(voxels, leaf)
-        spread[...] = whole
         mask[leaf] = whole.reshape(E, FACE, C).astype(bf16)
         lines[leaf] = feat[leaf].astype(f32) * whole.reshape(E, FACE, C)
-        coarse[...] = cot[leaf].astype(f32)
-        for i in range(4):
-            for j in range(4):
-                clines[leaf, i, pl.ds(16 * j, 4, stride=2), :] = coarse[16 * i + 4 * j : 16 * i + 4 * j + 4]
-            clines[leaf, i] = clines[leaf, i] * spread[2 * FACE * i : 2 * FACE * i + FACE]
+        starts = [2 * FACE * i + 2 * E * j for i in range(4) for j in range(4)]
+        kept = jnp.concatenate([whole[at : at + E] for at in starts], axis=0)
+        active[leaf] = kept.astype(bf16)
+        thin[leaf, pl.ds(0, FACE, stride=2), :] = cot[leaf].astype(f32)
+        upstream = thin[leaf] * kept
+        clines[leaf] = upstream.reshape(4, 4 * E, C)
+        upturned[:, 2 * FACE * leaf : 2 * FACE * leaf + 2 * FACE] = upstream.astype(bf16).T
     banded(w1, wa, wb)
     for n, p in enumerate((1, 2, 0)):
-        for t in range(9):
-            wc[n * C : n * C + C, t * C : t * C + C] = w2[9 * p + 8 - t]
+        for m, q in enumerate((1, 2, 0)):
+            for r in range(3):
+                at = (3 * m + r) * C
+                wc[n * C : n * C + C, at : at + C] = w2[9 * p + 3 * q + 2 - r]
 
 
 def setup(voxels, feat, cot, w1, w2):
@@ -201,81 +206,109 @@
         out_shape=(
             jax.ShapeDtypeStruct((L, E, FACE, C), bf16),
             jax.ShapeDtypeStruct((L + 1, E, FACE, C), f32),
-            jax.ShapeDtypeStruct((L + 1, 4, FACE, C), f32),
+            jax.ShapeDtypeStruct((L + 1, 4, 4 * E, C), f32),
+            jax.ShapeDtypeStruct((L, 2 * FACE, C), bf16),
+            jax.ShapeDtypeStruct((C, L * 2 * FACE), bf16),
             jax.ShapeDtypeStruct((2 * SPAN, 2 * C), bf16),
             jax.ShapeDtypeStruct((2 * SPAN, 2 * C), bf16),
             jax.ShapeDtypeStruct((3 * C, SPAN), bf16),
         ),
         in_specs=[vmem()] * 5,
-        out_specs=(vmem(),) * 6,
-        scratch_shapes=[pltpu.VMEM((E**3, C), f32), pltpu.VMEM((64, C), f32)],
+        out_specs=(vmem(),) * 8,
+        scratch_shapes=[pltpu.VMEM((L, 2 * FACE, C), f32)],
         compiler_params=params(14),
         cost_estimate=cost(1e9, 8e6),
         name="setup",
     )(voxels, feat, cot, w1, w2)
 
 
+def fill_coarse(store, table, clines, chigh, leaf, x):
+    a, i = (1, 0) if x == 4 else (0, x)
+    ids = lax.broadcasted_iota(jnp.int32, (E, C), 0)
+    out = ([], [], [])
+    for y in range(5):
+        b, j = (1, 0) if y == 4 else (0, y)
+        line = clines[block_at(table, leaf, a, b, 0), i, E * j : E * j + E]
+        beyond = chigh[block_at(table, leaf, a, b, 1), 4 * i + j : 4 * i + j + 1, :]
+        above = jnp.where(ids == E - 1, jnp.broadcast_to(beyond, (E, C)), pltpu.roll(line, E - 1, 0))
+        for r, part in enumerate((pltpu.roll(line, 1, 0), line, above)):
+            out[r].append(part)
+    for r in range(3):
+        whole = jnp.concatenate(out[r], axis=0)
+        store(r * C, whole[: 4 * E].astype(bf16))
+        store((3 + r) * C, whole[E:].astype(bf16))
+
+
 def first_kernel(
     table, lines, clines, mask, one_in, two_in, wa, wb, wc,
-    cols, hidden, delta, one, two,
-    low, high, chigh, ccols, coarse, faces,
+    cols, hidden, delta, turned, one, two,
+    low, high, chigh, ccols,
 ):
     low[L] = jnp.zeros((E, E, C), f32)
     high[L] = jnp.zeros((E, E, C), f32)
-    chigh[...] = jnp.zeros((L + 1, 4, E, C), f32)
+    chigh[L] = jnp.zeros((16, C), f32)
+    hidden[L] = jnp.zeros((E, FACE, C), f32)
+    delta[L] = jnp.zeros((E, FACE, C), f32)
 
     def receive(below, above):
         low_in, high_in = (one_in, two_in)[below], (one_in, two_in)[above]
         for leaf in range(L):
             low[leaf] = low_in[leaf, 0:FACE].astype(f32).reshape(E, E, C)
             high[leaf] = high_in[leaf, 0:FACE].astype(f32).reshape(E, E, C)
-            coarse[...] = high_in[leaf, FACE : FACE + 16].astype(f32)
-            for i in range(4):
-                chigh[leaf, i, pl.ds(0, 4, stride=2), :] = coarse[4 * i : 4 * i + 4]
+            chigh[leaf] = high_in[leaf, FACE : FACE + 16].astype(f32)
 
     by_parity(receive)
 
-    for n in range(L):
-        leaf = n
+    def fill(n):
         for pair in range(5):
             for half in range(2):
-                def store(at, value, n=n, pair=pair, half=half):
+                def store(at, value, pair=pair, half=half):
                     cols[n, pair, :, half * SPAN + at : half * SPAN + at + C] = value
-                fill_plane(store, table, lines, low, high, leaf, 2 * pair + half, E)
-
-            def store_coarse(at, value, n=n, pair=pair):
+                fill_plane(store, table, lines, low, high, n, 2 * pair + half, E)
+
+            def store_coarse(at, value, pair=pair):
                 ccols[n, pair, :, at : at + C] = value
-            fill_plane(store_coarse, table, clines, None, chigh, leaf, pair + 1, 4)
-
-        pre = pairs_dot(dot, cols, n, wa, wb)
-        back = dot_turned(ccols[n, 0:4].reshape(4 * FACE, SPAN), wc[: 2 * C])
-        back_next = dot_turned(ccols[n, 1:5].reshape(4 * FACE, SPAN), wc[2 * C :])
-        sig = 1.0 / (1.0 + jnp.exp(-pre))
-        slope = sig * (1.0 + pre * (1.0 - sig))
-        for half in range(2):
-            at = slice(half * C, half * C + C)
-            m = half_planes(mask, leaf, half).astype(f32)
-            h = m * pre[:, at] * sig[:, at]
-            g = back[:, at] if half == 0 else back[:, at] + back_next
-            d = g * m * slope[:, at]
-            for pair in range(4):
-                rows = slice(FACE * pair, FACE * pair + FACE)
-                hidden[n, 2 * pair + half] = h[rows].astype(bf16)
-                delta[n, 2 * pair + half] = d[rows].astype(bf16)
-                faces[n, 0, 2 * pair + half] = h[rows]
-                faces[n, 1, 2 * pair + half] = d[rows]
+            fill_coarse(store_coarse, table, clines, chigh, n, pair)
+
+    for base in range(0, L, TOGETHER):
+        for n in range(base, base + TOGETHER):
+            fill(n)
+        pre_all = pairs_dot(dot, cols, base, wa, wb)
+        here = ccols[base : base + TOGETHER, 0:4].reshape(TOGETHER * 128, 6 * C)
+        there = ccols[base : base + TOGETHER, 1:5].reshape(TOGETHER * 128, 6 * C)
+        even, odd = slice(0, 3 * C), slice(3 * C, 9 * C)
+        back = [dot_turned(here[:, : 3 * C], wc[: 2 * C, even]), dot_turned(here, wc[: 2 * C, odd])]
+        back_next = [dot_turned(there[:, : 3 * C], wc[2 * C :, even]), dot_turned(there, wc[2 * C :, odd])]
+        for n in range(base, base + TOGETHER):
+            pre = pre_all[4 * FACE * (n - base) : 4 * FACE * (n - base) + 4 * FACE]
+            sig = 1.0 / (1.0 + jnp.exp(-pre))
+            slope = sig * (1.0 + pre * (1.0 - sig))
+            for half in range(2):
+                at = slice(half * C, half * C + C)
+                m = half_planes(mask, n, half).astype(f32)
+                h = m * pre[:, at] * sig[:, at]
+                parts = [back[o][:, at] if half == 0 else back[o][:, at] + back_next[o] for o in range(2)]
+                first_row = 128 * (n - base)
+                rows = range(first_row, first_row + 128, E)
+                g = jnp.concatenate([parts[o][i : i + E] for i in rows for o in range(2)], axis=0)
+                d = g * m * slope[:, at]
+                for pair in range(4):
+                    rows = slice(FACE * pair, FACE * pair + FACE)
+                    hidden[n, 2 * pair + half] = h[rows]
+                    delta[n, 2 * pair + half] = d[rows]
+                turned[half * C : half * C + C, 256 * n : 256 * n + 256] = d.astype(bf16).T
 
     def send(below, above):
         up, down = (one, two)[above], (one, two)[below]
         for n in range(L):
             for i in range(0, E, 2):
-                def face(which, k):
-                    pair = [faces[n, which, i + m, pl.ds(k, E, stride=E), :] for m in range(2)]
+                def face(ref, k):
+                    pair = [ref[n, i + m, pl.ds(k, E, stride=E), :] for m in range(2)]
                     return jnp.concatenate(pair, axis=0).astype(bf16)
                 rows = slice(E * i, E * i + 2 * E)
-                up[0, n, rows] = face(0, E - 1)
-                up[1, n, rows] = face(1, E - 1)
-                down[0, n, rows] = face(1, 0)
+                up[0, n, rows] = face(hidden, E - 1)
+                up[1, n, rows] = face(delta, E - 1)
+                down[0, n, rows] = face(delta, 0)
                 down[1, n, rows] = jnp.zeros((2 * E, C), bf16)
 
     by_parity(send)
@@ -286,22 +319,21 @@
         first_kernel,
         out_shape=(
             jax.ShapeDtypeStruct((L, 5, FACE, 2 * SPAN), bf16),
-            jax.ShapeDtypeStruct((L, E, FACE, C), bf16),
-            jax.ShapeDtypeStruct((L, E, FACE, C), bf16),
+            jax.ShapeDtypeStruct((L + 1, E, FACE, C), f32),
+            jax.ShapeDtypeStruct((L + 1, E, FACE, C), f32),
+            jax.ShapeDtypeStruct((2 * C, L * 256), bf16),
             jax.ShapeDtypeStruct((2, L, FACE, C), bf16),
             jax.ShapeDtypeStruct((2, L, FACE, C), bf16),
         ),
         in_specs=[smem()] + [vmem()] * 8,
-        out_specs=(vmem(),) * 5,
+        out_specs=(vmem(),) * 6,
         scratch_shapes=[
             pltpu.VMEM((L + 1, E, E, C), f32),
             pltpu.VMEM((L + 1, E, E, C), f32),
-            pltpu.VMEM((L + 1, 4, E, C), f32),
-            pltpu.VMEM((L, 5, FACE, SPAN), bf16),
-            pltpu.VMEM((16, C), f32),
-            pltpu.VMEM((L, 2, E, FACE, C), f32),
+            pltpu.VMEM((L + 1, 16, C), f32),
+            pltpu.VMEM((L, 5, 32, 6 * C), bf16),
         ],
-        compiler_params=params(24),
+        compiler_params=params(20),
         cost_estimate=cost(15e9, 18e6),
         name="first_conv",
     )(table, lines, clines, mask, *faces, *filters)
@@ -315,12 +347,7 @@
         sent[t] = whole[t, pl.ds(theirs, HALF), :].astype(bf16)
 
 
-def first_grad_kernel(cols, delta, kept, sent, turned, total, whole):
-    @pl.loop(0, L)
-    def _(leaf):
-        for half in range(2):
-            turned[half * C : half * C + C, pl.ds(pl.multiple_of(leaf * 256, 256), 256)] = half_planes(delta, leaf, half).T
-
+def first_grad_kernel(cols, turned, kept, sent, total, whole):
     total[...] = jnp.zeros_like(total)
     for tile in range(9):
         lanes = range(256 * tile, 256 * tile + 256, C)
@@ -345,35 +372,28 @@
     return jax.ShapeDtypeStruct((TAPS, HALF, C), f32), jax.ShapeDtypeStruct((TAPS, HALF, C), bf16)
 
 
-def first_grad(cols, delta):
+def first_grad(cols, turned):
     return pl.pallas_call(
         first_grad_kernel,
         out_shape=halves_shape(),
         in_specs=[vmem(), vmem()],
         out_specs=(vmem(), vmem()),
         scratch_shapes=[
-            pltpu.VMEM((2 * C, L * 256), bf16),
             pltpu.VMEM((3, C, SPAN), f32),
             pltpu.VMEM((TAPS, C, C), f32),
         ],
         compiler_params=params(16),
         cost_estimate=cost(6e9, 14e6),
         name="first_grad",
-    )(cols, delta)
+    )(cols, turned)
 
 
 def second_kernel(
-    table, hidden, one_in, two_in, cot, mask, sent_first,
-    cols, active_out, kept, sent,
-    lines, low, turned, total, whole, thin,
+    table, lines, one_in, two_in, turned, sent_first,
+    cols, kept, sent,
+    low, total, whole,
 ):
-    lines[L] = jnp.zeros((E, FACE, C), f32)
     low[L] = jnp.zeros((E, E, C), f32)
-    thin[...] = jnp.zeros_like(thin)
-
-    @pl.loop(0, L)
-    def _(leaf):
-        lines[leaf] = hidden[leaf].astype(f32)
 
     def receive(below, above):
         for leaf in range(L):
@@ -389,15 +409,6 @@
                     value = jnp.concatenate([parts[r][q + 2 * m] for m in range(4)], axis=0).astype(bf16)
                     at = (x % 2) * SPAN + (3 * q + r) * C
                     cols[leaf, x // 2, :, at : at + C] = value
-        active = []
-        for i in range(4):
-            plane = mask[leaf, 2 * i].astype(f32)
-            active += [plane[16 * j : 16 * j + E] for j in range(4)]
-        active = jnp.concatenate(active, axis=0)
-        active_out[leaf] = active.astype(bf16)
-        thin[leaf, pl.ds(0, FACE, stride=2), :] = cot[leaf].astype(f32)
-        upstream = (thin[leaf] * active).astype(bf16)
-        turned[:, 128 * leaf : 128 * leaf + 128] = upstream.T
 
     for tile in range(9):
         at = slice(256 * tile, 256 * tile + 256)
@@ -412,29 +423,25 @@
     split_halves(core_at(), whole, kept, sent.at[TAPS:])
 
 
-def second_grad(table, hidden, faces, cot, mask, sent_first):
+def second_grad(table, hidden, faces, upturned, sent_first):
     return pl.pallas_call(
         second_kernel,
         out_shape=(
             jax.ShapeDtypeStruct((L, 5, 32, 2 * SPAN), bf16),
-            jax.ShapeDtypeStruct((L, 2 * FACE, C), bf16),
             jax.ShapeDtypeStruct((TAPS, HALF, C), f32),
             jax.ShapeDtypeStruct((2 * TAPS, HALF, C), bf16),
         ),
-        in_specs=[smem()] + [vmem()] * 6,
-        out_specs=(vmem(),) * 4,
+        in_specs=[smem()] + [vmem()] * 5,
+        out_specs=(vmem(),) * 3,
         scratch_shapes=[
-            pltpu.VMEM((L + 1, E, FACE, C), f32),
             pltpu.VMEM((L + 1, E, E, C), f32),
-            pltpu.VMEM((C, L * 128), bf16),
             pltpu.VMEM((C, 3 * SPAN), f32),
             pltpu.VMEM((TAPS, C, C), f32),
-            pltpu.VMEM((L, 2 * FACE, C), f32),
         ],
-        compiler_params=params(20),
+        compiler_params=params(14),
         cost_estimate=cost(8e9, 6e6),
         name="second_grad",
-    )(table, hidden, *faces, cot, mask, sent_first)
+    )(table, hidden, *faces, upturned, sent_first)
 
 
 def coarse_kernel(cols, active, w2, coarse, thin):
@@ -459,14 +466,9 @@
     )(cols, active, w2)
 
 
-def adjoint_kernel(start, count, table, delta, mask, one_in, two_in, w, out, lines, low, high, cols, wa, wb):
-    lines[L] = jnp.zeros((E, FACE, C), f32)
+def adjoint_kernel(start, count, table, lines, mask, one_in, two_in, w, out, low, high, cols, wa, wb):
     low[L] = jnp.zeros((E, E, C), f32)
     high[L] = jnp.zeros((E, E, C), f32)
-
-    @pl.loop(0, L)
-    def _(leaf):
-        lines[leaf] = delta[leaf].astype(f32)
 
     def receive(below, above):
         for leaf in range(L):
@@ -477,19 +479,21 @@
 
     banded_turned(w, wa, wb)
 
-    for n in range(count):
-        leaf = start + n
-        for pair in range(5):
+    for base in range(0, count, TOGETHER):
+        for n in range(base, base + TOGETHER):
+            for pair in range(5):
+                for half in range(2):
+                    def store(at, value, n=n, pair=pair, half=half):
+                        cols[n, pair, :, half * SPAN + at : half * SPAN + at + C] = value
+                    fill_plane(store, table, lines, low, high, start + n, 2 * pair + half, E)
+        res_all = pairs_dot(dot_turned, cols, base, wa, wb)
+        for n in range(base, base + TOGETHER):
+            res = res_all[4 * FACE * (n - base) : 4 * FACE * (n - base) + 4 * FACE]
             for half in range(2):
-                def store(at, value, n=n, pair=pair, half=half):
-                    cols[n, pair, :, half * SPAN + at : half * SPAN + at + C] = value
-                fill_plane(store, table, lines, low, high, leaf, 2 * pair + half, E)
-        res = pairs_dot(dot_turned, cols, n, wa, wb)
-        for half in range(2):
-            m = half_planes(mask, leaf, half).astype(f32)
-            value = (res[:, half * C : half * C + C] * m).astype(bf16)
-            for pair in range(4):
-                out[n, 2 * pair + half] = value[FACE * pair : FACE * pair + FACE]
+                m = half_planes(mask, start + n, half).astype(f32)
+                value = (res[:, half * C : half * C + C] * m).astype(bf16)
+                for pair in range(4):
+                    out[n, 2 * pair + half] = value[FACE * pair : FACE * pair + FACE]
 
 
 def adjoint_conv(start, count, table, delta, mask, faces, w):
@@ -502,7 +506,6 @@
         in_specs=[smem()] + [vmem()] * 5,
         out_specs=vmem(),
         scratch_shapes=[
-            pltpu.VMEM((L + 1, E, FACE, C), f32),
             pltpu.VMEM((L + 1, E, E, C), f32),
             pltpu.VMEM((L + 1, E, E, C), f32),
             pltpu.VMEM((count, 5, FACE, 2 * SPAN), bf16),
@@ -525,7 +528,7 @@
             if d == 0:
                 own[t] = value
             else:
-                sends[d - 1][t] = value.astype(bf16)
+                sends[3 - d][t] = value.astype(bf16)
 
 
 def start_sum(kept1, kept2, got):
@@ -650,19 +653,19 @@
     with jax.named_scope("faces_in"):
         faces = exchanged(one, two)
     voxels, _ = lax.optimization_barrier((voxels, one))
-    mask, lines, clines, *filters = setup(voxels, feat, cot, weight_first, weight_second)
-    cols, hidden, delta, one, two = first_conv(table, lines, clines, mask, faces, filters)
+    mask, lines, clines, active, upturned, *filters = setup(voxels, feat, cot, weight_first, weight_second)
+    cols, hidden, delta, turned, one, two = first_conv(table, lines, clines, mask, faces, filters)
     with jax.named_scope("faces_mid"):
         faces = exchanged(one, two)
-    kept1, sent1 = first_grad(cols, delta)
-    cols2, active, kept2, sent = second_grad(table, hidden, faces, cot, mask, sent1)
+    kept1, sent1 = first_grad(cols, turned)
+    cols2, kept2, sent = second_grad(table, hidden, faces, upturned, sent1)
     with jax.named_scope("sum_core"):
         got = to_other_core(sent)
     own, *sends = start_sum(kept1, kept2, got)
     orders, groups = ring_orders(leaf_count), rest_groups(leaf_count)
     per = -(-2 * TAPS // leaf_count)
     with jax.named_scope("sum_ring"):
-        received = [lax.ppermute(s, both, o) for s, o in zip(sends, orders)]
+        received = [lax.ppermute(s, both, o) for s, o in zip(sends, orders[::-1])]
     input_grad = adjoint_conv(0, L, table, delta, mask, faces, weight_first)
     own, input_grad = lax.optimization_barrier((own, input_grad))
     parts = next_sum(own, received, per * leaf_count).reshape(leaf_count, per * PIECE, C)

time: 112 us -> 109 us (0.973)
  Pallas kernels: 33.1 us -> 31.2 us
    pallas_call x1, Pallas kernels: 9.89 us -> 8.63 us  [first_conv(): pl.pallas_call(first_kernel, out_shape=(jax.ShapeDtypeStruct((L, 5, FACE,...]
    unnamed x18 -> x16, local copies, waits for them, and re-layouts: 2.87 us -> 2.86 us
  transfers between devices with their start and end apart: 15 -> 15, of which waited for: 9 -> 8; matrix products, arithmetic and copies ran while one was open for 0% -> 0% of each run, Pallas kernels for 15% -> 15%
where the time goes in v5:
time: 109 us
  blocking collectives  42.1 us (39%)
  Pallas kernels  31.2 us (29%)
  starting transfers between devices  23 us (21%)
  waiting for transfers between devices  9.06 us (8%)
  local copies, waits for them, and re-layouts  2.87 us (3%)
    all_to_all x2, blocking collectives, shards(): lax.all_to_all(parts, both, 0, 0, axis_index_groups=groups, tiled=True)  42.1 us
    pallas_call x1, Pallas kernels, first_conv(): pl.pallas_call(first_kernel, out_shape=(jax.ShapeDtypeStruct((L, 5, FACE,...  8.63 us
    ppermute x3, starting transfers between devices, shards(): received = [lax.ppermute(s, both, o) for s, o in zip(sends, orders[::-1])]  8.33 us
    pallas_call x1, Pallas kernels, adjoint_conv(): pl.pallas_call(kernel, out_shape=jax.ShapeDtypeStruct((count, E, FACE, C)...  7.41 us
    ppermute x2, starting transfers between devices, exchanged(): lax.ppermute(first, 'leaf', pairs)  5.82 us
    pallas_call x1, Pallas kernels, first_grad(): pl.pallas_call(first_grad_kernel, out_shape=halves_shape(), in_specs=[vme...  4.48 us
    ppermute x5, starting transfers between devices, to_other_core(): lax.ppermute(block, 'scene', [(i, i ^ 1) for i in range(lax.axis_size('sc...  4.04 us
    ppermute x5, waiting for transfers between devices, to_other_core(): lax.ppermute(block, 'scene', [(i, i ^ 1) for i in range(lax.axis_size('sc...  3.65 us
  transfers between devices with their start and end apart: 15, of which 8 were waited for; matrix products, arithmetic and copies ran while one was open for 0% of the time, Pallas kernels for 15%

profile of v5, /device:TPU:1, one launch (start us, length us, event | category | flops | bytes accessed | tf_op | source)
XLA Modules:
  0.0 109.1 jit_solution(14435721517883658067)
XLA Ops:
  0.6 1.2 %copy-done.1 = bf16[1,8,8,8,8,128]{5,4,3,2,1,0:T(8,128)(2,1)S(1)} copy-done((bf16[1,8,8,8,8,128]{5,4,3,2,1,0:T(8,128)(2,1)S(1)}, bf16[1,8,8,8,8,128]{5,4,3,2,1,0:T(8,128)(2,1)}, u32[]{:S(2)}) %copy-start.1) | copy-done | bytes 1048600
  1.9 0.9 copy-done.4
  2.8 0.7 copy-done.5
  3.5 1.3 %first_faces.1 = (bf16[8,80,128]{2,1,0:T(8,128)(2,1)S(1)}, bf16[8,80,128]{2,1,0:T(8,128)(2,1)S(1)}) custom-call(s32[8,512]{1,0:T(8,128)S(1)} %bitcast.18, bf16[8,8,64,128]{3,2,1,0:T(8,128)(2,1)S(1)} %bitcast.14, bf16[8,64,128]{2,1,0:T(8,128)(2,1)S(1)} %bitcast.16), custom_call_target="tpu_custom_call" | custom-call | flops 6000000000 | bytes 8000000 | tf_op jit(solution)/shard_map/first_faces/pallas_call | solution.py:168
  4.8 0.7 collective-permute-start.1
  5.4 4.6 %collective-permute-start = (bf16[8,80,128]{2,1,0:T(8,128)(2,1)S(1)}, bf16[8,80,128]{2,1,0:T(8,128)(2,1)S(1)}, u32[]{:S(2)}, u32[]{:S(2)}) collective-permute-start(bf16[8,80,128]{2,1,0:T(8,128)(2,1)S(1)} %get-tuple-element.41), channel_id=1, source_target_pairs={{0,8},{8,0},{16,24},{24,16},{32,40},{40,32},{48,56},{56,48},{64,72... | collective-permute-start | bytes 491528 | tf_op jit(solution)/shard_map/faces_in/ppermute | solution.py:637
  10.0 1.4 %setup.1 = (bf16[8,8,64,128]{3,2,1,0:T(8,128)(2,1)S(1)}, f32[9,8,64,128]{3,2,1,0:T(8,128)S(1)}, f32[9,4,32,128]{3,2,1,0:T(8,128)S(1)}, bf16[8,128,128]{2,1,0:T(8...) custom-call(s32[8,512]{1,0:T(8,128)S(1)} %bitcast.19, ...), custom_call_target="tpu_custom_call" | custom-call | flops 1000000000 | bytes 8000000 | tf_op jit(solution)/shard_map/setup/pallas_call | solution.py:204
  11.5 2.2 %collective-permute-done.one_in = bf16[8,80,128]{2,1,0:T(8,128)(2,1)S(1)} collective-permute-done((bf16[8,80,128]{2,1,0:T(8,128)(2,1)S(1)}, bf16[8,80,128]{2,1,0:T(8,128)(2,1)S(1)}, u32[]{:S(2)}, u32[]{:S(2)}) %collective-permute-start) | collective-permute-done | bytes 163872 | tf_op jit(solution)/shard_map/faces_in/ppermute | solution.py:637
  13.6 8.6 %first_conv.1 = (bf16[8,5,64,2304]{3,2,1,0:T(8,128)(2,1)S(1)}, f32[9,8,64,128]{3,2,1,0:T(8,128)S(1)}, f32[9,8,64,128]{3,2,1,0:T(8,128)S(1)}, bf16[256,2048]{1,0:...) custom-call(s32[8,26]{1,0:T(8,128)S(1)} %bitcast.20, ...), custom_call_target="tpu_custom_call" | custom-call | flops 15000000512 | bytes 18000000 | tf_op jit(solution)/shard_map/first_conv/pallas_call | solution.py:318
  22.3 1.2 %collective-permute-start.2 = (bf16[2,8,64,128]{3,2,1,0:T(8,128)(2,1)S(1)}, bf16[2,8,64,128]{3,2,1,0:T(8,128)(2,1)S(1)}, u32[]{:S(2)}, u32[]{:S(2)}) collective-permute-start(bf16[2,8,64,128]{3,2,1,0:T(8,128)(2,1)S(1)} %get-tuple-element.51), channel_id=1, source_target_pairs={{0,8},{8,0},{16,24},{24,16},{32,40},{40,32},{48,56},{56,48},{64,72... | collective-permute-start | bytes 786440 | tf_op jit(solution)/shard_map/faces_mid/ppermute | solution.py:637
  23.5 0.8 collective-permute-start.3
  24.4 4.5 %first_grad.1 = (f32[27,64,128]{2,1,0:T(8,128)S(1)}, bf16[27,64,128]{2,1,0:T(8,128)(2,1)S(1)}) custom-call(bf16[8,5,64,2304]{3,2,1,0:T(8,128)(2,1)S(1)} %get-tuple-element.54.cols, bf16[256,2048]{1,0:T(8,128)(2,1)S(1)} %get-tuple-element.55.turned), custom_call_target="tpu_custom_call" | custom-call | flops 6000000000 | bytes 14000000 | tf_op jit(solution)/shard_map/first_grad/pallas_call | solution.py:376
  28.9 2.8 %second_grad.1 = (bf16[8,5,32,2304]{3,2,1,0:T(8,128)(2,1)S(1)}, f32[27,64,128]{2,1,0:T(8,128)S(1)}, bf16[54,64,128]{2,1,0:T(8,128)(2,1)S(1)}) custom-call(s32[8,26]{1,0:T(8,128)S(1)} %bitcast.21, f32[9,8,64,128]{3,2,1,0:T(8,128)S(1)} %get-tuple-element.50.lines, bf16[2,8,64,128]{3,2,1,0:T(8,128)(2,1)S(1)} %collective-permute-done.2.one_in.refs_3_, ...), custom_call_target="tpu_custom_call" | custom-call | flops 8000000000 | bytes 6000000 | tf_op jit(solution)/shard_map/second_grad/pallas_call | solution.py:427
  31.7 2.3 %collective-permute-start.4 = (bf16[54,64,128]{2,1,0:T(8,128)(2,1)S(1)}, bf16[54,64,128]{2,1,0:T(8,128)(2,1)S(1)}, u32[]{:S(2)}, u32[]{:S(2)}) collective-permute-start(bf16[54,64,128]{2,1,0:T(8,128)(2,1)S(1)} %get-tuple-element.60), channel_id=1, source_target_pairs={{0,1},{1,0},{2,3},{3,2},{4,5},{5,4},{6,7},{7,6},{8,9},{9,8},{10,11... | collective-permute-start | bytes 2654216 | tf_op jit(solution)/shard_map/sum_core/ppermute | solution.py:641
  34.0 2.1 %collective-permute-done.4.got = bf16[54,64,128]{2,1,0:T(8,128)(2,1)S(1)} collective-permute-done((bf16[54,64,128]{2,1,0:T(8,128)(2,1)S(1)}, bf16[54,64,128]{2,1,0:T(8,128)(2,1)S(1)}, u32[]{:S(2)}, u32[]{:S(2)}) %collective-permute-start.4) | collective-permute-done | bytes 884768 | tf_op jit(solution)/shard_map/sum_core/ppermute | solution.py:641
  36.0 0.2 start_sum.1
  36.3 7.6 %collective-permute-start.5 = (bf16[54,16,128]{2,1,0:T(8,128)(2,1)S(1)}, bf16[54,16,128]{2,1,0:T(8,128)(2,1)S(1)}, u32[]{:S(2)}, u32[]{:S(2)}) collective-permute-start(bf16[54,16,128]{2,1,0:T(8,128)(2,1)S(1)} %get-tuple-element.64), channel_id=1, source_target_pairs={{0,6},{1,25},{2,4},{3,27},{4,2},{5,29},{6,0},{7,31},{8,14},{9,17},... | collective-permute-start | bytes 663560 | tf_op jit(solution)/shard_map/sum_ring/ppermute | solution.py:668
  43.9 0.7 collective-permute-start.7
  44.6 7.4 %first_adjoint.1 = bf16[8,8,64,128]{3,2,1,0:T(8,128)(2,1)} custom-call(s32[8,26]{1,0:T(8,128)S(1)} %bitcast.22, f32[9,8,64,128]{3,2,1,0:T(8,128)S(1)} %get-tuple-element.62.refs_1_, bf16[8,8,64,128]{3,2,1,0:T(8,128)(2,1)S(1)} %get-tuple-element.45.mask.refs_2_, bf16[2,8,64,128]{3,2,1,0:T(8,128)(2,1)S(1)} %collective-permute-done.2.one_in.refs_3_, ...), custom_call_target="tpu_custom_call" | custom-call | flops 10000000000 | bytes 6000000 | tf_op jit(solution)/shard_map/first_adjoint/pallas_call | solution.py:503
  52.2 26.5 %all_to_all.10.refs_0_ = bf16[32,32,128]{2,1,0:T(8,128)(2,1)S(1)} all-to-all(bf16[32,32,128]{2,1,0:T(8,128)(2,1)S(1)} %bitcast.8), channel_id=1, replica_groups={{0,8,16,24,32,40,48,56,64,72,80,88,96,104,112,120,128,136,144,152,160,1..., dimensions={0} | all-to-all | bytes 524288 | tf_op jit(solution)/shard_map/sum_rest/all_to_all | solution.py:673
  78.7 15.6 %all_to_all.11 = bf16[32,32,128]{2,1,0:T(8,128)(2,1)S(1)} all-to-all(bf16[32,32,128]{2,1,0:T(8,128)(2,1)S(1)} %last_sum.1), channel_id=1, replica_groups={{0,8,16,24,32,40,48,56,64,72,80,88,96,104,112,120,128,136,144,152,160,1..., dimensions={0} | all-to-all | bytes 524288 | tf_op jit(solution)/shard_map/gather_rest/all_to_all | solution.py:676
  94.6 3.1 %collective-permute-start.8 = (bf16[54,16,128]{2,1,0:T(8,128)(2,1)S(1)}, bf16[54,16,128]{2,1,0:T(8,128)(2,1)S(1)}, u32[]{:S(2)}, u32[]{:S(2)}) collective-permute-start(bf16[54,16,128]{2,1,0:T(8,128)(2,1)S(1)} %bitcast.11), channel_id=1, source_target_pairs={{0,2},{1,9},{2,0},{3,11},{4,6},{5,13},{6,4},{7,15},{8,10},{9,1},{1... | collective-permute-start | bytes 663560 | tf_op jit(solution)/shard_map/gather_ring/ppermute | solution.py:679
  97.7 2.8 %coarse_conv.1 = bf16[8,64,128]{2,1,0:T(8,128)(2,1)} custom-call(bf16[8,5,32,2304]{3,2,1,0:T(8,128)(2,1)S(1)} %get-tuple-element.67.cols, bf16[8,128,128]{2,1,0:T(8,128)(2,1)S(1)} %get-tuple-element.68.active, bf16[27,128,128]{2,1,0:T(8,128)(2,1)S(1)} %copy-done), custom_call_target="tpu_custom_call" | custom-call | flops 1000000000 | bytes 2000000 | tf_op jit(solution)/shard_map/coarse_conv/pallas_call | solution.py:457
  100.5 2.6 %collective-permute-done.10.refs_3_ = bf16[54,16,128]{2,1,0:T(8,128)(2,1)S(1)} collective-permute-done((bf16[54,16,128]{2,1,0:T(8,128)(2,1)S(1)}, bf16[54,16,128]{2,1,0:T(8,128)(2,1)S(1)}, u32[]{:S(2)}, u32[]{:S(2)}) %collective-permute-start.10) | collective-permute-done | bytes 221216 | tf_op jit(solution)/shard_map/gather_ring/ppermute | solution.py:679
  103.1 0.6 collective-permute-done.8.refs_1_
  103.7 1.2 %collective-permute-start.11 = (bf16[54,16,128]{2,1,0:T(8,128)(2,1)S(1)}, bf16[54,16,128]{2,1,0:T(8,128)(2,1)S(1)}, u32[]{:S(2)}, u32[]{:S(2)}) collective-permute-start(bf16[54,16,128]{2,1,0:T(8,128)(2,1)S(1)} %bitcast.12), channel_id=1, source_target_pairs={{0,1},{1,0},{2,3},{3,2},{4,5},{5,4},{6,7},{7,6},{8,9},{9,8},{10,11... | collective-permute-start | bytes 663560 | tf_op jit(solution)/shard_map/gather_core/ppermute | solution.py:641
  104.9 0.5 collective-permute-start.13
  105.5 0.6 collective-permute-done.11.refs_4_
  106.0 0.4 collective-permute-done.12.refs_5_
  106.4 0.3 collective-permute-done.13.refs_6_
  106.7 0.3 collective-permute-done.14.refs_7_
  107.0 2.0 %finish.1 = (f32[27,128,128]{2,1,0:T(8,128)}, f32[27,128,128]{2,1,0:T(8,128)}) custom-call(bf16[54,16,128]{2,1,0:T(8,128)(2,1)S(1)} %bitcast.13, bf16[54,16,128]{2,1,0:T(8,128)(2,1)S(1)} %collective-permute-done.8.refs_1_, bf16[54,16,128]{2,1,0:T(8,128)(2,1)S(1)} %collective-permute-done.9.refs_2_, bf16[54,16,128]{2,1,0:T(8,128)(2,1)S(1)} %collective-permute-done.10.refs_3_, ...), custom_call_target="tpu_custom_call" | custom-call | flops 1000000 | bytes 6000000 | tf_op jit(solution)/shard_map/finish/pallas_call | solution.py:602
  (28 shorter events, 0.4 us)
Async XLA Ops:
  0.6 1.2 %copy-start.1 = (bf16[1,8,8,8,8,128]{5,4,3,2,1,0:T(8,128)(2,1)S(1)}, bf16[1,8,8,8,8,128]{5,4,3,2,1,0:T(8,128)(2,1)}, u32[]{:S(2)}) copy-start(bf16[1,8,8,8,8,128]{5,4,3,2,1,0:T(8,128)(2,1)} %param.6) | copy-start | bytes 3145732
  1.9 0.9 copy-start.4
  2.8 0.7 copy-start.5
  3.5 6.5 %copy-start = (bf16[27,128,128]{2,1,0:T(8,128)(2,1)S(1)}, bf16[27,128,128]{2,1,0:T(8,128)(2,1)}, u32[]{:S(2)}) copy-start(bf16[27,128,128]{2,1,0:T(8,128)(2,1)} %w2.3) | copy-start | bytes 2654212
  3.5 6.5 %copy-start.2 = (bf16[1,8,8,8,8,128]{5,4,3,2,1,0:T(8,128)(2,1)S(1)}, bf16[1,8,8,8,8,128]{5,4,3,2,1,0:T(8,128)(2,1)}, u32[]{:S(2)}) copy-start(bf16[1,8,8,8,8,128]{5,4,3,2,1,0:T(8,128)(2,1)} %param.6) | copy-start | bytes 3145732
  3.5 6.5 %copy-start.3 = (bf16[27,128,128]{2,1,0:T(8,128)(2,1)S(1)}, bf16[27,128,128]{2,1,0:T(8,128)(2,1)}, u32[]{:S(2)}) copy-start(bf16[27,128,128]{2,1,0:T(8,128)(2,1)} %refs_5_.1) | copy-start | bytes 2654212
  3.5 6.5 %copy-start.6 = (s32[1,8,512]{2,1,0:T(8,128)S(1)}, s32[1,8,512]{2,1,0:T(8,128)}, u32[]{:S(2)}) copy-start(s32[1,8,512]{2,1,0:T(8,128)} %param.11) | copy-start | bytes 49156
  4.8 8.9 %copy-start.7 = (s32[1,8,26]{2,1,0:T(8,128)S(1)}, s32[1,8,26]{2,1,0:T(8,128)}, u32[]{:S(2)}) copy-start(s32[1,8,26]{2,1,0:T(8,128)} %param.10) | copy-start | bytes 2500
  4.8 6.7 %collective-permute-start.1 = (bf16[8,80,128]{2,1,0:T(8,128)(2,1)S(1)}, bf16[8,80,128]{2,1,0:T(8,128)(2,1)S(1)}, u32[]{:S(2)}, u32[]{:S(2)}) collective-permute-start(bf16[8,80,128]{2,1,0:T(8,128)(2,1)S(1)} %get-tuple-element.46), channel_id=1, source_target_pairs={{8,16},{16,8},{24,32},{32,24},{40,48},{48,40},{56,64},{64,56},{72,... | collective-permute-start | bytes 491528 | tf_op jit(solution)/shard_map/faces_in/ppermute | solution.py:637
  5.4 8.2 %collective-permute-start = (bf16[8,80,128]{2,1,0:T(8,128)(2,1)S(1)}, bf16[8,80,128]{2,1,0:T(8,128)(2,1)S(1)}, u32[]{:S(2)}, u32[]{:S(2)}) collective-permute-start(bf16[8,80,128]{2,1,0:T(8,128)(2,1)S(1)} %get-tuple-element.41), channel_id=1, source_target_pairs={{0,8},{8,0},{16,24},{24,16},{32,40},{40,32},{48,56},{56,48},{64,72... | collective-permute-start | bytes 491528 | tf_op jit(solution)/shard_map/faces_in/ppermute | solution.py:637
  22.3 6.6 %collective-permute-start.2 = (bf16[2,8,64,128]{3,2,1,0:T(8,128)(2,1)S(1)}, bf16[2,8,64,128]{3,2,1,0:T(8,128)(2,1)S(1)}, u32[]{:S(2)}, u32[]{:S(2)}) collective-permute-start(bf16[2,8,64,128]{3,2,1,0:T(8,128)(2,1)S(1)} %get-tuple-element.51), channel_id=1, source_target_pairs={{0,8},{8,0},{16,24},{24,16},{32,40},{40,32},{48,56},{56,48},{64,72... | collective-permute-start | bytes 786440 | tf_op jit(solution)/shard_map/faces_mid/ppermute | solution.py:637
  23.5 5.4 %collective-permute-start.3 = (bf16[2,8,64,128]{3,2,1,0:T(8,128)(2,1)S(1)}, bf16[2,8,64,128]{3,2,1,0:T(8,128)(2,1)S(1)}, u32[]{:S(2)}, u32[]{:S(2)}) collective-permute-start(bf16[2,8,64,128]{3,2,1,0:T(8,128)(2,1)S(1)} %get-tuple-element.52), channel_id=1, source_target_pairs={{8,16},{16,8},{24,32},{32,24},{40,48},{48,40},{56,64},{64,56},{72,... | collective-permute-start | bytes 786440 | tf_op jit(solution)/shard_map/faces_mid/ppermute | solution.py:637
  31.7 4.3 %collective-permute-start.4 = (bf16[54,64,128]{2,1,0:T(8,128)(2,1)S(1)}, bf16[54,64,128]{2,1,0:T(8,128)(2,1)S(1)}, u32[]{:S(2)}, u32[]{:S(2)}) collective-permute-start(bf16[54,64,128]{2,1,0:T(8,128)(2,1)S(1)} %get-tuple-element.60), channel_id=1, source_target_pairs={{0,1},{1,0},{2,3},{3,2},{4,5},{5,4},{6,7},{7,6},{8,9},{9,8},{10,11... | collective-permute-start | bytes 2654216 | tf_op jit(solution)/shard_map/sum_core/ppermute | solution.py:641
  36.3 15.7 %collective-permute-start.5 = (bf16[54,16,128]{2,1,0:T(8,128)(2,1)S(1)}, bf16[54,16,128]{2,1,0:T(8,128)(2,1)S(1)}, u32[]{:S(2)}, u32[]{:S(2)}) collective-permute-start(bf16[54,16,128]{2,1,0:T(8,128)(2,1)S(1)} %get-tuple-element.64), channel_id=1, source_target_pairs={{0,6},{1,25},{2,4},{3,27},{4,2},{5,29},{6,0},{7,31},{8,14},{9,17},... | collective-permute-start | bytes 663560 | tf_op jit(solution)/shard_map/sum_ring/ppermute | solution.py:668
  43.9 8.1 %collective-permute-start.6 = (bf16[54,16,128]{2,1,0:T(8,128)(2,1)S(1)}, bf16[54,16,128]{2,1,0:T(8,128)(2,1)S(1)}, u32[]{:S(2)}, u32[]{:S(2)}) collective-permute-start(bf16[54,16,128]{2,1,0:T(8,128)(2,1)S(1)} %get-tuple-element.65), channel_id=1, source_target_pairs={{0,4},{1,17},{2,6},{3,19},{4,0},{5,21},{6,2},{7,23},{8,12},{9,25},... | collective-permute-start | bytes 663560 | tf_op jit(solution)/shard_map/sum_ring/ppermute | solution.py:668
  43.9 8.1 %collective-permute-start.7 = (bf16[54,16,128]{2,1,0:T(8,128)(2,1)S(1)}, bf16[54,16,128]{2,1,0:T(8,128)(2,1)S(1)}, u32[]{:S(2)}, u32[]{:S(2)}) collective-permute-start(bf16[54,16,128]{2,1,0:T(8,128)(2,1)S(1)} %get-tuple-element.66), channel_id=1, source_target_pairs={{0,2},{1,9},{2,0},{3,11},{4,6},{5,13},{6,4},{7,15},{8,10},{9,1},{1... | collective-permute-start | bytes 663560 | tf_op jit(solution)/shard_map/sum_ring/ppermute | solution.py:668
  94.4 8.7 %collective-permute-start.10 = (bf16[54,16,128]{2,1,0:T(8,128)(2,1)S(1)}, bf16[54,16,128]{2,1,0:T(8,128)(2,1)S(1)}, u32[]{:S(2)}, u32[]{:S(2)}) collective-permute-start(bf16[54,16,128]{2,1,0:T(8,128)(2,1)S(1)} %bitcast.9), channel_id=1, source_target_pairs={{0,6},{1,25},{2,4},{3,27},{4,2},{5,29},{6,0},{7,31},{8,14},{9,17},... | collective-permute-start | bytes 663560 | tf_op jit(solution)/shard_map/gather_ring/ppermute | solution.py:679
  94.5 8.6 %collective-permute-start.9 = (bf16[54,16,128]{2,1,0:T(8,128)(2,1)S(1)}, bf16[54,16,128]{2,1,0:T(8,128)(2,1)S(1)}, u32[]{:S(2)}, u32[]{:S(2)}) collective-permute-start(bf16[54,16,128]{2,1,0:T(8,128)(2,1)S(1)} %bitcast.10), channel_id=1, source_target_pairs={{0,4},{1,17},{2,6},{3,19},{4,0},{5,21},{6,2},{7,23},{8,12},{9,25},... | collective-permute-start | bytes 663560 | tf_op jit(solution)/shard_map/gather_ring/ppermute | solution.py:679
  94.6 9.1 %collective-permute-start.8 = (bf16[54,16,128]{2,1,0:T(8,128)(2,1)S(1)}, bf16[54,16,128]{2,1,0:T(8,128)(2,1)S(1)}, u32[]{:S(2)}, u32[]{:S(2)}) collective-permute-start(bf16[54,16,128]{2,1,0:T(8,128)(2,1)S(1)} %bitcast.11), channel_id=1, source_target_pairs={{0,2},{1,9},{2,0},{3,11},{4,6},{5,13},{6,4},{7,15},{8,10},{9,1},{1... | collective-permute-start | bytes 663560 | tf_op jit(solution)/shard_map/gather_ring/ppermute | solution.py:679
  103.7 2.4 %collective-permute-start.11 = (bf16[54,16,128]{2,1,0:T(8,128)(2,1)S(1)}, bf16[54,16,128]{2,1,0:T(8,128)(2,1)S(1)}, u32[]{:S(2)}, u32[]{:S(2)}) collective-permute-start(bf16[54,16,128]{2,1,0:T(8,128)(2,1)S(1)} %bitcast.12), channel_id=1, source_target_pairs={{0,1},{1,0},{2,3},{3,2},{4,5},{5,4},{6,7},{7,6},{8,9},{9,8},{10,11... | collective-permute-start | bytes 663560 | tf_op jit(solution)/shard_map/gather_core/ppermute | solution.py:641
  104.9 1.5 %collective-permute-start.12 = (bf16[54,16,128]{2,1,0:T(8,128)(2,1)S(1)}, bf16[54,16,128]{2,1,0:T(8,128)(2,1)S(1)}, u32[]{:S(2)}, u32[]{:S(2)}) collective-permute-start(bf16[54,16,128]{2,1,0:T(8,128)(2,1)S(1)} %collective-permute-done.8.refs_1_), channel_id=1, source_target_pairs={{0,1},{1,0},{2,3},{3,2},{4,5},{5,4},{6,7},{7,6},{8,9},{9,8},{10,11... | collective-permute-start | bytes 663560 | tf_op jit(solution)/shard_map/gather_core/ppermute | solution.py:641
  104.9 1.8 %collective-permute-start.13 = (bf16[54,16,128]{2,1,0:T(8,128)(2,1)S(1)}, bf16[54,16,128]{2,1,0:T(8,128)(2,1)S(1)}, u32[]{:S(2)}, u32[]{:S(2)}) collective-permute-start(bf16[54,16,128]{2,1,0:T(8,128)(2,1)S(1)} %collective-permute-done.9.refs_2_), channel_id=1, source_target_pairs={{0,1},{1,0},{2,3},{3,2},{4,5},{5,4},{6,7},{7,6},{8,9},{9,8},{10,11... | collective-permute-start | bytes 663560 | tf_op jit(solution)/shard_map/gather_core/ppermute | solution.py:641
  105.4 1.6 %collective-permute-start.14 = (bf16[54,16,128]{2,1,0:T(8,128)(2,1)S(1)}, bf16[54,16,128]{2,1,0:T(8,128)(2,1)S(1)}, u32[]{:S(2)}, u32[]{:S(2)}) collective-permute-start(bf16[54,16,128]{2,1,0:T(8,128)(2,1)S(1)} %collective-permute-done.10.refs_3_), channel_id=1, source_target_pairs={{0,1},{1,0},{2,3},{3,2},{4,5},{5,4},{6,7},{7,6},{8,9},{9,8},{10,11... | collective-permute-start | bytes 663560 | tf_op jit(solution)/shard_map/gather_core/ppermute | solution.py:641

commit v6 on v5

--- a/solution.py
+++ b/solution.py
@@ -679,7 +679,8 @@
         received = [lax.ppermute(own, both, o) for o in orders]
     cols2, own = lax.optimization_barrier((cols2, own))
     coarse = coarse_conv(cols2, active, weight_second)
-    coarse, mine = lax.optimization_barrier((coarse, [own, *received]))
+    coarse, late = lax.optimization_barrier((coarse, own))
+    mine = [late] + [lax.optimization_barrier((piece, late))[0] for piece in received]
     with jax.named_scope("gather_core"):
         theirs = [to_other_core(piece) for piece in mine]
     grad_first, grad_second = finish([*mine, *theirs])

time: 109 us -> 108 us (level)
  waiting for transfers between devices: 9.06 us -> 7.11 us
    ppermute x3, waiting for transfers between devices: 3.22 us -> 1.74 us  [shards(): received = [lax.ppermute(own, both, o) for o in orders]]
  transfers between devices with their start and end apart: 15 -> 15, of which waited for: 8 -> 5; matrix products, arithmetic and copies ran while one was open for 0% -> 0% of each run, Pallas kernels for 15% -> 15%
where the time goes in v6:
time: 108 us
  blocking collectives  42.1 us (39%)
  Pallas kernels  31.2 us (29%)
  starting transfers between devices  24 us (22%)
  waiting for transfers between devices  7.11 us (7%)
  local copies, waits for them, and re-layouts  2.87 us (3%)
    all_to_all x2, blocking collectives, shards(): lax.all_to_all(parts, both, 0, 0, axis_index_groups=groups, tiled=True)  42.1 us
    pallas_call x1, Pallas kernels, first_conv(): pl.pallas_call(first_kernel, out_shape=(jax.ShapeDtypeStruct((L, 5, FACE,...  8.63 us
    ppermute x3, starting transfers between devices, shards(): received = [lax.ppermute(s, both, o) for s, o in zip(sends, orders[::-1])]  8.33 us
    pallas_call x1, Pallas kernels, adjoint_conv(): pl.pallas_call(kernel, out_shape=jax.ShapeDtypeStruct((count, E, FACE, C)...  7.41 us
    ppermute x2, starting transfers between devices, exchanged(): lax.ppermute(first, 'leaf', pairs)  5.83 us
    ppermute x5, starting transfers between devices, to_other_core(): lax.ppermute(block, 'scene', [(i, i ^ 1) for i in range(lax.axis_size('sc...  5 us
    pallas_call x1, Pallas kernels, first_grad(): pl.pallas_call(first_grad_kernel, out_shape=halves_shape(), in_specs=[vme...  4.48 us
    ppermute x3, starting transfers between devices, shards(): received = [lax.ppermute(own, both, o) for o in orders]  3.33 us
  transfers between devices with their start and end apart: 15, of which 5 were waited for; matrix products, arithmetic and copies ran while one was open for 0% of the time, Pallas kernels for 15%

profile of v6, /device:TPU:1, one launch (start us, length us, event | category | flops | bytes accessed | tf_op | source)
XLA Modules:
  0.0 108.1 jit_solution(6452690753117347222)
XLA Ops:
  0.6 1.2 %copy-done.1 = bf16[1,8,8,8,8,128]{5,4,3,2,1,0:T(8,128)(2,1)S(1)} copy-done((bf16[1,8,8,8,8,128]{5,4,3,2,1,0:T(8,128)(2,1)S(1)}, bf16[1,8,8,8,8,128]{5,4,3,2,1,0:T(8,128)(2,1)}, u32[]{:S(2)}) %copy-start.1) | copy-done | bytes 1048600
  1.9 0.9 copy-done.4
  2.8 0.7 copy-done.5
  3.5 1.3 %first_faces.1 = (bf16[8,80,128]{2,1,0:T(8,128)(2,1)S(1)}, bf16[8,80,128]{2,1,0:T(8,128)(2,1)S(1)}) custom-call(s32[8,512]{1,0:T(8,128)S(1)} %bitcast.18, bf16[8,8,64,128]{3,2,1,0:T(8,128)(2,1)S(1)} %bitcast.14, bf16[8,64,128]{2,1,0:T(8,128)(2,1)S(1)} %bitcast.16), custom_call_target="tpu_custom_call" | custom-call | flops 6000000000 | bytes 8000000 | tf_op jit(solution)/shard_map/first_faces/pallas_call | solution.py:168
  4.8 0.7 collective-permute-start.1
  5.4 4.6 %collective-permute-start = (bf16[8,80,128]{2,1,0:T(8,128)(2,1)S(1)}, bf16[8,80,128]{2,1,0:T(8,128)(2,1)S(1)}, u32[]{:S(2)}, u32[]{:S(2)}) collective-permute-start(bf16[8,80,128]{2,1,0:T(8,128)(2,1)S(1)} %get-tuple-element.41), channel_id=1, source_target_pairs={{0,8},{8,0},{16,24},{24,16},{32,40},{40,32},{48,56},{56,48},{64,72... | collective-permute-start | bytes 491528 | tf_op jit(solution)/shard_map/faces_in/ppermute | solution.py:637
  10.0 1.4 %setup.1 = (bf16[8,8,64,128]{3,2,1,0:T(8,128)(2,1)S(1)}, f32[9,8,64,128]{3,2,1,0:T(8,128)S(1)}, f32[9,4,32,128]{3,2,1,0:T(8,128)S(1)}, bf16[8,128,128]{2,1,0:T(8...) custom-call(s32[8,512]{1,0:T(8,128)S(1)} %bitcast.19, ...), custom_call_target="tpu_custom_call" | custom-call | flops 1000000000 | bytes 8000000 | tf_op jit(solution)/shard_map/setup/pallas_call | solution.py:204
  11.5 2.2 %collective-permute-done.one_in = bf16[8,80,128]{2,1,0:T(8,128)(2,1)S(1)} collective-permute-done((bf16[8,80,128]{2,1,0:T(8,128)(2,1)S(1)}, bf16[8,80,128]{2,1,0:T(8,128)(2,1)S(1)}, u32[]{:S(2)}, u32[]{:S(2)}) %collective-permute-start) | collective-permute-done | bytes 163872 | tf_op jit(solution)/shard_map/faces_in/ppermute | solution.py:637
  13.6 8.6 %first_conv.1 = (bf16[8,5,64,2304]{3,2,1,0:T(8,128)(2,1)S(1)}, f32[9,8,64,128]{3,2,1,0:T(8,128)S(1)}, f32[9,8,64,128]{3,2,1,0:T(8,128)S(1)}, bf16[256,2048]{1,0:...) custom-call(s32[8,26]{1,0:T(8,128)S(1)} %bitcast.20, ...), custom_call_target="tpu_custom_call" | custom-call | flops 15000000512 | bytes 18000000 | tf_op jit(solution)/shard_map/first_conv/pallas_call | solution.py:318
  22.3 1.3 %collective-permute-start.2 = (bf16[2,8,64,128]{3,2,1,0:T(8,128)(2,1)S(1)}, bf16[2,8,64,128]{3,2,1,0:T(8,128)(2,1)S(1)}, u32[]{:S(2)}, u32[]{:S(2)}) collective-permute-start(bf16[2,8,64,128]{3,2,1,0:T(8,128)(2,1)S(1)} %get-tuple-element.51), channel_id=1, source_target_pairs={{0,8},{8,0},{16,24},{24,16},{32,40},{40,32},{48,56},{56,48},{64,72... | collective-permute-start | bytes 786440 | tf_op jit(solution)/shard_map/faces_mid/ppermute | solution.py:637
  23.5 0.8 collective-permute-start.3
  24.4 4.5 %first_grad.1 = (f32[27,64,128]{2,1,0:T(8,128)S(1)}, bf16[27,64,128]{2,1,0:T(8,128)(2,1)S(1)}) custom-call(bf16[8,5,64,2304]{3,2,1,0:T(8,128)(2,1)S(1)} %get-tuple-element.54.cols, bf16[256,2048]{1,0:T(8,128)(2,1)S(1)} %get-tuple-element.55.turned), custom_call_target="tpu_custom_call" | custom-call | flops 6000000000 | bytes 14000000 | tf_op jit(solution)/shard_map/first_grad/pallas_call | solution.py:376
  28.9 2.8 %second_grad.1 = (bf16[8,5,32,2304]{3,2,1,0:T(8,128)(2,1)S(1)}, f32[27,64,128]{2,1,0:T(8,128)S(1)}, bf16[54,64,128]{2,1,0:T(8,128)(2,1)S(1)}) custom-call(s32[8,26]{1,0:T(8,128)S(1)} %bitcast.21, f32[9,8,64,128]{3,2,1,0:T(8,128)S(1)} %get-tuple-element.50.lines, bf16[2,8,64,128]{3,2,1,0:T(8,128)(2,1)S(1)} %collective-permute-done.2.one_in.refs_3_, ...), custom_call_target="tpu_custom_call" | custom-call | flops 8000000000 | bytes 6000000 | tf_op jit(solution)/shard_map/second_grad/pallas_call | solution.py:427
  31.7 2.3 %collective-permute-start.4 = (bf16[54,64,128]{2,1,0:T(8,128)(2,1)S(1)}, bf16[54,64,128]{2,1,0:T(8,128)(2,1)S(1)}, u32[]{:S(2)}, u32[]{:S(2)}) collective-permute-start(bf16[54,64,128]{2,1,0:T(8,128)(2,1)S(1)} %get-tuple-element.60), channel_id=1, source_target_pairs={{0,1},{1,0},{2,3},{3,2},{4,5},{5,4},{6,7},{7,6},{8,9},{9,8},{10,11... | collective-permute-start | bytes 2654216 | tf_op jit(solution)/shard_map/sum_core/ppermute | solution.py:641
  34.0 2.1 %collective-permute-done.4.got = bf16[54,64,128]{2,1,0:T(8,128)(2,1)S(1)} collective-permute-done((bf16[54,64,128]{2,1,0:T(8,128)(2,1)S(1)}, bf16[54,64,128]{2,1,0:T(8,128)(2,1)S(1)}, u32[]{:S(2)}, u32[]{:S(2)}) %collective-permute-start.4) | collective-permute-done | bytes 884768 | tf_op jit(solution)/shard_map/sum_core/ppermute | solution.py:641
  36.0 0.2 start_sum.1
  36.3 7.6 %collective-permute-start.5 = (bf16[54,16,128]{2,1,0:T(8,128)(2,1)S(1)}, bf16[54,16,128]{2,1,0:T(8,128)(2,1)S(1)}, u32[]{:S(2)}, u32[]{:S(2)}) collective-permute-start(bf16[54,16,128]{2,1,0:T(8,128)(2,1)S(1)} %get-tuple-element.64), channel_id=1, source_target_pairs={{0,6},{1,25},{2,4},{3,27},{4,2},{5,29},{6,0},{7,31},{8,14},{9,17},... | collective-permute-start | bytes 663560 | tf_op jit(solution)/shard_map/sum_ring/ppermute | solution.py:668
  43.9 0.7 collective-permute-start.7
  44.6 7.4 %first_adjoint.1 = bf16[8,8,64,128]{3,2,1,0:T(8,128)(2,1)} custom-call(s32[8,26]{1,0:T(8,128)S(1)} %bitcast.22, f32[9,8,64,128]{3,2,1,0:T(8,128)S(1)} %get-tuple-element.62.refs_1_, bf16[8,8,64,128]{3,2,1,0:T(8,128)(2,1)S(1)} %get-tuple-element.45.mask.refs_2_, bf16[2,8,64,128]{3,2,1,0:T(8,128)(2,1)S(1)} %collective-permute-done.2.one_in.refs_3_, ...), custom_call_target="tpu_custom_call" | custom-call | flops 10000000000 | bytes 6000000 | tf_op jit(solution)/shard_map/first_adjoint/pallas_call | solution.py:503
  52.0 0.1 next_sum.1
  52.2 26.5 %all_to_all.10.refs_0_ = bf16[32,32,128]{2,1,0:T(8,128)(2,1)S(1)} all-to-all(bf16[32,32,128]{2,1,0:T(8,128)(2,1)S(1)} %bitcast.8), channel_id=1, replica_groups={{0,8,16,24,32,40,48,56,64,72,80,88,96,104,112,120,128,136,144,152,160,1..., dimensions={0} | all-to-all | bytes 524288 | tf_op jit(solution)/shard_map/sum_rest/all_to_all | solution.py:673
  78.7 15.6 %all_to_all.11 = bf16[32,32,128]{2,1,0:T(8,128)(2,1)S(1)} all-to-all(bf16[32,32,128]{2,1,0:T(8,128)(2,1)S(1)} %last_sum.1), channel_id=1, replica_groups={{0,8,16,24,32,40,48,56,64,72,80,88,96,104,112,120,128,136,144,152,160,1..., dimensions={0} | all-to-all | bytes 524288 | tf_op jit(solution)/shard_map/gather_rest/all_to_all | solution.py:676
  94.4 0.1 collective-permute-start.10
  94.6 3.1 %collective-permute-start.8 = (bf16[54,16,128]{2,1,0:T(8,128)(2,1)S(1)}, bf16[54,16,128]{2,1,0:T(8,128)(2,1)S(1)}, u32[]{:S(2)}, u32[]{:S(2)}) collective-permute-start(bf16[54,16,128]{2,1,0:T(8,128)(2,1)S(1)} %bitcast.11), channel_id=1, source_target_pairs={{0,2},{1,9},{2,0},{3,11},{4,6},{5,13},{6,4},{7,15},{8,10},{9,1},{1... | collective-permute-start | bytes 663560 | tf_op jit(solution)/shard_map/gather_ring/ppermute | solution.py:679
  97.7 2.8 %coarse_conv.1 = bf16[8,64,128]{2,1,0:T(8,128)(2,1)} custom-call(bf16[8,5,32,2304]{3,2,1,0:T(8,128)(2,1)S(1)} %get-tuple-element.67.cols, bf16[8,128,128]{2,1,0:T(8,128)(2,1)S(1)} %get-tuple-element.68.active, bf16[27,128,128]{2,1,0:T(8,128)(2,1)S(1)} %copy-done), custom_call_target="tpu_custom_call" | custom-call | flops 1000000000 | bytes 2000000 | tf_op jit(solution)/shard_map/coarse_conv/pallas_call | solution.py:457
  100.5 0.9 collective-permute-start.11
  101.4 1.7 %collective-permute-done.10.refs_3_ = bf16[54,16,128]{2,1,0:T(8,128)(2,1)S(1)} collective-permute-done((bf16[54,16,128]{2,1,0:T(8,128)(2,1)S(1)}, bf16[54,16,128]{2,1,0:T(8,128)(2,1)S(1)}, u32[]{:S(2)}, u32[]{:S(2)}) %collective-permute-start.10) | collective-permute-done | bytes 221216 | tf_op jit(solution)/shard_map/gather_ring/ppermute | solution.py:679
  103.1 1.5 %collective-permute-start.13 = (bf16[54,16,128]{2,1,0:T(8,128)(2,1)S(1)}, bf16[54,16,128]{2,1,0:T(8,128)(2,1)S(1)}, u32[]{:S(2)}, u32[]{:S(2)}) collective-permute-start(bf16[54,16,128]{2,1,0:T(8,128)(2,1)S(1)} %collective-permute-done.9.refs_2_), channel_id=1, source_target_pairs={{0,1},{1,0},{2,3},{3,2},{4,5},{5,4},{6,7},{7,6},{8,9},{9,8},{10,11... | collective-permute-start | bytes 663560 | tf_op jit(solution)/shard_map/gather_core/ppermute | solution.py:641
  104.6 0.4 collective-permute-start.12
  104.9 0.7 collective-permute-done.13.refs_6_
  105.7 0.4 collective-permute-done.12.refs_5_
  106.1 2.0 %finish.1 = (f32[27,128,128]{2,1,0:T(8,128)}, f32[27,128,128]{2,1,0:T(8,128)}) custom-call(bf16[54,16,128]{2,1,0:T(8,128)(2,1)S(1)} %bitcast.13, bf16[54,16,128]{2,1,0:T(8,128)(2,1)S(1)} %collective-permute-done.8.refs_1_, bf16[54,16,128]{2,1,0:T(8,128)(2,1)S(1)} %collective-permute-done.9.refs_2_, bf16[54,16,128]{2,1,0:T(8,128)(2,1)S(1)} %collective-permute-done.10.refs_3_, ...), custom_call_target="tpu_custom_call" | custom-call | flops 1000000 | bytes 6000000 | tf_op jit(solution)/shard_map/finish/pallas_call | solution.py:602
  (28 shorter events, 0.2 us)
Async XLA Ops:
  0.6 1.2 %copy-start.1 = (bf16[1,8,8,8,8,128]{5,4,3,2,1,0:T(8,128)(2,1)S(1)}, bf16[1,8,8,8,8,128]{5,4,3,2,1,0:T(8,128)(2,1)}, u32[]{:S(2)}) copy-start(bf16[1,8,8,8,8,128]{5,4,3,2,1,0:T(8,128)(2,1)} %param.6) | copy-start | bytes 3145732
  1.9 0.9 copy-start.4
  2.8 0.7 copy-start.5
  3.5 6.5 %copy-start = (bf16[27,128,128]{2,1,0:T(8,128)(2,1)S(1)}, bf16[27,128,128]{2,1,0:T(8,128)(2,1)}, u32[]{:S(2)}) copy-start(bf16[27,128,128]{2,1,0:T(8,128)(2,1)} %w2.3) | copy-start | bytes 2654212
  3.5 6.5 %copy-start.2 = (bf16[1,8,8,8,8,128]{5,4,3,2,1,0:T(8,128)(2,1)S(1)}, bf16[1,8,8,8,8,128]{5,4,3,2,1,0:T(8,128)(2,1)}, u32[]{:S(2)}) copy-start(bf16[1,8,8,8,8,128]{5,4,3,2,1,0:T(8,128)(2,1)} %param.6) | copy-start | bytes 3145732
  3.5 6.5 %copy-start.3 = (bf16[27,128,128]{2,1,0:T(8,128)(2,1)S(1)}, bf16[27,128,128]{2,1,0:T(8,128)(2,1)}, u32[]{:S(2)}) copy-start(bf16[27,128,128]{2,1,0:T(8,128)(2,1)} %refs_5_.1) | copy-start | bytes 2654212
  3.5 6.5 %copy-start.6 = (s32[1,8,512]{2,1,0:T(8,128)S(1)}, s32[1,8,512]{2,1,0:T(8,128)}, u32[]{:S(2)}) copy-start(s32[1,8,512]{2,1,0:T(8,128)} %param.11) | copy-start | bytes 49156
  4.8 8.9 %copy-start.7 = (s32[1,8,26]{2,1,0:T(8,128)S(1)}, s32[1,8,26]{2,1,0:T(8,128)}, u32[]{:S(2)}) copy-start(s32[1,8,26]{2,1,0:T(8,128)} %param.10) | copy-start | bytes 2500
  4.8 6.7 %collective-permute-start.1 = (bf16[8,80,128]{2,1,0:T(8,128)(2,1)S(1)}, bf16[8,80,128]{2,1,0:T(8,128)(2,1)S(1)}, u32[]{:S(2)}, u32[]{:S(2)}) collective-permute-start(bf16[8,80,128]{2,1,0:T(8,128)(2,1)S(1)} %get-tuple-element.46), channel_id=1, source_target_pairs={{8,16},{16,8},{24,32},{32,24},{40,48},{48,40},{56,64},{64,56},{72,... | collective-permute-start | bytes 491528 | tf_op jit(solution)/shard_map/faces_in/ppermute | solution.py:637
  5.4 8.2 %collective-permute-start = (bf16[8,80,128]{2,1,0:T(8,128)(2,1)S(1)}, bf16[8,80,128]{2,1,0:T(8,128)(2,1)S(1)}, u32[]{:S(2)}, u32[]{:S(2)}) collective-permute-start(bf16[8,80,128]{2,1,0:T(8,128)(2,1)S(1)} %get-tuple-element.41), channel_id=1, source_target_pairs={{0,8},{8,0},{16,24},{24,16},{32,40},{40,32},{48,56},{56,48},{64,72... | collective-permute-start | bytes 491528 | tf_op jit(solution)/shard_map/faces_in/ppermute | solution.py:637
  22.3 6.6 %collective-permute-start.2 = (bf16[2,8,64,128]{3,2,1,0:T(8,128)(2,1)S(1)}, bf16[2,8,64,128]{3,2,1,0:T(8,128)(2,1)S(1)}, u32[]{:S(2)}, u32[]{:S(2)}) collective-permute-start(bf16[2,8,64,128]{3,2,1,0:T(8,128)(2,1)S(1)} %get-tuple-element.51), channel_id=1, source_target_pairs={{0,8},{8,0},{16,24},{24,16},{32,40},{40,32},{48,56},{56,48},{64,72... | collective-permute-start | bytes 786440 | tf_op jit(solution)/shard_map/faces_mid/ppermute | solution.py:637
  23.5 5.4 %collective-permute-start.3 = (bf16[2,8,64,128]{3,2,1,0:T(8,128)(2,1)S(1)}, bf16[2,8,64,128]{3,2,1,0:T(8,128)(2,1)S(1)}, u32[]{:S(2)}, u32[]{:S(2)}) collective-permute-start(bf16[2,8,64,128]{3,2,1,0:T(8,128)(2,1)S(1)} %get-tuple-element.52), channel_id=1, source_target_pairs={{8,16},{16,8},{24,32},{32,24},{40,48},{48,40},{56,64},{64,56},{72,... | collective-permute-start | bytes 786440 | tf_op jit(solution)/shard_map/faces_mid/ppermute | solution.py:637
  31.7 4.3 %collective-permute-start.4 = (bf16[54,64,128]{2,1,0:T(8,128)(2,1)S(1)}, bf16[54,64,128]{2,1,0:T(8,128)(2,1)S(1)}, u32[]{:S(2)}, u32[]{:S(2)}) collective-permute-start(bf16[54,64,128]{2,1,0:T(8,128)(2,1)S(1)} %get-tuple-element.60), channel_id=1, source_target_pairs={{0,1},{1,0},{2,3},{3,2},{4,5},{5,4},{6,7},{7,6},{8,9},{9,8},{10,11... | collective-permute-start | bytes 2654216 | tf_op jit(solution)/shard_map/sum_core/ppermute | solution.py:641
  36.3 15.7 %collective-permute-start.5 = (bf16[54,16,128]{2,1,0:T(8,128)(2,1)S(1)}, bf16[54,16,128]{2,1,0:T(8,128)(2,1)S(1)}, u32[]{:S(2)}, u32[]{:S(2)}) collective-permute-start(bf16[54,16,128]{2,1,0:T(8,128)(2,1)S(1)} %get-tuple-element.64), channel_id=1, source_target_pairs={{0,6},{1,25},{2,4},{3,27},{4,2},{5,29},{6,0},{7,31},{8,14},{9,17},... | collective-permute-start | bytes 663560 | tf_op jit(solution)/shard_map/sum_ring/ppermute | solution.py:668
  43.9 8.1 %collective-permute-start.6 = (bf16[54,16,128]{2,1,0:T(8,128)(2,1)S(1)}, bf16[54,16,128]{2,1,0:T(8,128)(2,1)S(1)}, u32[]{:S(2)}, u32[]{:S(2)}) collective-permute-start(bf16[54,16,128]{2,1,0:T(8,128)(2,1)S(1)} %get-tuple-element.65), channel_id=1, source_target_pairs={{0,4},{1,17},{2,6},{3,19},{4,0},{5,21},{6,2},{7,23},{8,12},{9,25},... | collective-permute-start | bytes 663560 | tf_op jit(solution)/shard_map/sum_ring/ppermute | solution.py:668
  43.9 8.1 %collective-permute-start.7 = (bf16[54,16,128]{2,1,0:T(8,128)(2,1)S(1)}, bf16[54,16,128]{2,1,0:T(8,128)(2,1)S(1)}, u32[]{:S(2)}, u32[]{:S(2)}) collective-permute-start(bf16[54,16,128]{2,1,0:T(8,128)(2,1)S(1)} %get-tuple-element.66), channel_id=1, source_target_pairs={{0,2},{1,9},{2,0},{3,11},{4,6},{5,13},{6,4},{7,15},{8,10},{9,1},{1... | collective-permute-start | bytes 663560 | tf_op jit(solution)/shard_map/sum_ring/ppermute | solution.py:668
  94.4 8.7 %collective-permute-start.10 = (bf16[54,16,128]{2,1,0:T(8,128)(2,1)S(1)}, bf16[54,16,128]{2,1,0:T(8,128)(2,1)S(1)}, u32[]{:S(2)}, u32[]{:S(2)}) collective-permute-start(bf16[54,16,128]{2,1,0:T(8,128)(2,1)S(1)} %bitcast.9), channel_id=1, source_target_pairs={{0,6},{1,25},{2,4},{3,27},{4,2},{5,29},{6,0},{7,31},{8,14},{9,17},... | collective-permute-start | bytes 663560 | tf_op jit(solution)/shard_map/gather_ring/ppermute | solution.py:679
  94.5 8.7 %collective-permute-start.9 = (bf16[54,16,128]{2,1,0:T(8,128)(2,1)S(1)}, bf16[54,16,128]{2,1,0:T(8,128)(2,1)S(1)}, u32[]{:S(2)}, u32[]{:S(2)}) collective-permute-start(bf16[54,16,128]{2,1,0:T(8,128)(2,1)S(1)} %bitcast.10), channel_id=1, source_target_pairs={{0,4},{1,17},{2,6},{3,19},{4,0},{5,21},{6,2},{7,23},{8,12},{9,25},... | collective-permute-start | bytes 663560 | tf_op jit(solution)/shard_map/gather_ring/ppermute | solution.py:679
  94.6 10.0 %collective-permute-start.8 = (bf16[54,16,128]{2,1,0:T(8,128)(2,1)S(1)}, bf16[54,16,128]{2,1,0:T(8,128)(2,1)S(1)}, u32[]{:S(2)}, u32[]{:S(2)}) collective-permute-start(bf16[54,16,128]{2,1,0:T(8,128)(2,1)S(1)} %bitcast.11), channel_id=1, source_target_pairs={{0,2},{1,9},{2,0},{3,11},{4,6},{5,13},{6,4},{7,15},{8,10},{9,1},{1... | collective-permute-start | bytes 663560 | tf_op jit(solution)/shard_map/gather_ring/ppermute | solution.py:679
  100.5 4.5 %collective-permute-start.11 = (bf16[54,16,128]{2,1,0:T(8,128)(2,1)S(1)}, bf16[54,16,128]{2,1,0:T(8,128)(2,1)S(1)}, u32[]{:S(2)}, u32[]{:S(2)}) collective-permute-start(bf16[54,16,128]{2,1,0:T(8,128)(2,1)S(1)} %bitcast.12), channel_id=1, source_target_pairs={{0,1},{1,0},{2,3},{3,2},{4,5},{5,4},{6,7},{7,6},{8,9},{9,8},{10,11... | collective-permute-start | bytes 663560 | tf_op jit(solution)/shard_map/gather_core/ppermute | solution.py:641
  103.1 1.8 %collective-permute-start.14 = (bf16[54,16,128]{2,1,0:T(8,128)(2,1)S(1)}, bf16[54,16,128]{2,1,0:T(8,128)(2,1)S(1)}, u32[]{:S(2)}, u32[]{:S(2)}) collective-permute-start(bf16[54,16,128]{2,1,0:T(8,128)(2,1)S(1)} %collective-permute-done.10.refs_3_), channel_id=1, source_target_pairs={{0,1},{1,0},{2,3},{3,2},{4,5},{5,4},{6,7},{7,6},{8,9},{9,8},{10,11... | collective-permute-start | bytes 663560 | tf_op jit(solution)/shard_map/gather_core/ppermute | solution.py:641
  103.1 2.6 %collective-permute-start.13 = (bf16[54,16,128]{2,1,0:T(8,128)(2,1)S(1)}, bf16[54,16,128]{2,1,0:T(8,128)(2,1)S(1)}, u32[]{:S(2)}, u32[]{:S(2)}) collective-permute-start(bf16[54,16,128]{2,1,0:T(8,128)(2,1)S(1)} %collective-permute-done.9.refs_2_), channel_id=1, source_target_pairs={{0,1},{1,0},{2,3},{3,2},{4,5},{5,4},{6,7},{7,6},{8,9},{9,8},{10,11... | collective-permute-start | bytes 663560 | tf_op jit(solution)/shard_map/gather_core/ppermute | solution.py:641
  104.6 1.5 %collective-permute-start.12 = (bf16[54,16,128]{2,1,0:T(8,128)(2,1)S(1)}, bf16[54,16,128]{2,1,0:T(8,128)(2,1)S(1)}, u32[]{:S(2)}, u32[]{:S(2)}) collective-permute-start(bf16[54,16,128]{2,1,0:T(8,128)(2,1)S(1)} %collective-permute-done.8.refs_1_), channel_id=1, source_target_pairs={{0,1},{1,0},{2,3},{3,2},{4,5},{5,4},{6,7},{7,6},{8,9},{9,8},{10,11... | collective-permute-start | bytes 663560 | tf_op jit(solution)/shard_map/gather_core/ppermute | solution.py:641
